TPU v7x, 32 devices: a whole 2x2x4 slice. The times are simulated.
32 devices in a mesh: dp: 2 (over x), fsdp: 4 (over y, core), tensor: 4 (over z).
Axes of the slice: x: 2, y: 2, z: 4, core: 2. Of those that a mesh axis runs over, the one named last changes fastest.
Arguments:
- tokens: bfloat16 [4096, 576], P(('dp', 'fsdp', 'tensor')), may hold values from -6 to 6
- gate_weight: bfloat16 [576, 1536], P('fsdp', 'tensor'), may hold values from -0.25 to 0.25
- up_weight: bfloat16 [576, 1536], P('fsdp', 'tensor'), may hold values from -0.25 to 0.25
- down_weight: bfloat16 [1536, 576], P('tensor', 'fsdp'), may hold values from -0.15625 to 0.15625
- cotangent: bfloat16 [4096, 576], P(('dp', 'fsdp', 'tensor')), may hold values from -0.119628906 to 0.119628906
Outputs:
- mixed: bfloat16 [4096, 576], P(('dp', 'fsdp', 'tensor'))
- grad_tokens: bfloat16 [4096, 576], P(('dp', 'fsdp', 'tensor'))
- grad_gate_weight: bfloat16 [576, 1536], P('fsdp', 'tensor')
- grad_up_weight: bfloat16 [576, 1536], P('fsdp', 'tensor')
- grad_down_weight: bfloat16 [1536, 576], P('tensor', 'fsdp')
All inputs are finite; a program needn't handle non-finite values.
Results may differ from a plain program's by a relative error of at most 0.025.
Values may be sent and summed in bfloat16 or wider, within the bound.
No kernel may reach another device: no remote copies, remote signals or barrier semaphores. Data moves between devices by JAX's collectives and lax.ppermute only.
A program may use at most 64 MiB of HBM per device.

v0:
```python
import jax
import jax.numpy as jnp
from jax import lax
from jax.sharding import PartitionSpec as P


def activate(gate_sum, up_sum):
    sig = jax.nn.sigmoid(gate_sum)
    swished = gate_sum * sig
    slopes = up_sum * sig * (1.0 + gate_sum * (1.0 - sig))
    hidden = (swished * up_sum).astype(jnp.bfloat16)
    return (hidden, swished, slopes)


def inner_rows(left, right):
    return lax.dot_general(
        left, right, (((0,), (0,)), ((), ())), preferred_element_type=jnp.float32
    )


def inner_cols(left, right):
    return lax.dot_general(
        left, right, (((1,), (1,)), ((), ())), preferred_element_type=jnp.float32
    )


def reduce_rows(term_fn, own_rows):
    return lax.psum_scatter(
        term_fn(jnp.int32(0), lax.axis_size("tensor") * own_rows).astype(jnp.bfloat16),
        "tensor",
        scatter_dimension=0,
        tiled=True,
    ).astype(jnp.float32)


def per_device(tokens, gate_weight, up_weight, down_weight, cotangent):
    own_rows = tokens.shape[0]
    all_tokens, all_cotangent = (
        lax.all_gather(tokens, "tensor", axis=0, tiled=True),
        lax.all_gather(cotangent, "tensor", axis=0, tiled=True),
    )
    gate_full, up_full = (
        lax.all_gather(gate_weight, "fsdp", axis=0, tiled=True),
        lax.all_gather(up_weight, "fsdp", axis=0, tiled=True),
    )
    down_full = lax.all_gather(down_weight, "fsdp", axis=1, tiled=True)
    gate_sum = jnp.dot(all_tokens, gate_full, preferred_element_type=jnp.float32)
    up_sum = jnp.dot(all_tokens, up_full, preferred_element_type=jnp.float32)
    hidden, swished, slopes = activate(gate_sum, up_sum)

    def output_term(first_row, row_count):
        return jnp.dot(hidden, down_full, preferred_element_type=jnp.float32)

    mixed = reduce_rows(output_term, own_rows).astype(jnp.bfloat16)
    grad_hidden = inner_cols(all_cotangent, down_full)
    grad_gate = (grad_hidden * slopes).astype(jnp.bfloat16)
    grad_up = (grad_hidden * swished).astype(jnp.bfloat16)

    def input_term(first_row, row_count):
        return inner_cols(grad_gate, gate_full) + inner_cols(grad_up, up_full)

    grad_tokens = reduce_rows(input_term, own_rows).astype(jnp.bfloat16)
    stacked = jnp.stack(
        [
            inner_rows(all_tokens, grad_gate),
            inner_rows(all_tokens, grad_up),
            inner_rows(all_cotangent, hidden),
        ],
        axis=0,
    )
    share = lax.psum_scatter(stacked.astype(jnp.bfloat16), "fsdp", scatter_dimension=1, tiled=True)
    summed = lax.psum(share, "dp")
    return (mixed, grad_tokens, summed[0], summed[1], summed[2].T)


def solution(mesh):
    return jax.shard_map(
        per_device,
        mesh=mesh,
        in_specs=(
            P(("dp", "fsdp", "tensor"), None),
            P("fsdp", "tensor"),
            P("fsdp", "tensor"),
            P("tensor", "fsdp"),
            P(("dp", "fsdp", "tensor"), None),
        ),
        out_specs=(
            P(("dp", "fsdp", "tensor"), None),
            P(("dp", "fsdp", "tensor"), None),
            P("fsdp", "tensor"),
            P("fsdp", "tensor"),
            P("tensor", "fsdp"),
        ),
        check_vma=False,
    )
```

profile of v0, /device:TPU:0, one launch (start us, length us, event | category | flops | bytes accessed | tf_op | source)
XLA Modules:
  0.0 173.4 jit_solution(4400689107027741352)
XLA Ops:
  7.2 8.5 %all_gather.16 = bf16[576,384]{1,0:T(8,128)(2,1)S(1)} all-gather(bf16[144,384]{1,0:T(8,128)(2,1)} %param.6), channel_id=1, replica_groups=mesh['dp'=2,'fsdp'=4,'tensor'=4] {'fsdp'}, dimensions={0}, use_global_device_ids=true | all-gather | bytes 552960 | tf_op jit(solution)/shard_map/all_gather | solution.py:43
  15.8 7.0 %all_gather.17 = bf16[576,384]{1,0:T(8,128)(2,1)S(1)} all-gather(bf16[144,384]{1,0:T(8,128)(2,1)} %param.7), channel_id=1, replica_groups=mesh['dp'=2,'fsdp'=4,'tensor'=4] {'fsdp'}, dimensions={0}, use_global_device_ids=true | all-gather | bytes 552960 | tf_op jit(solution)/shard_map/all_gather | solution.py:44
  22.8 7.0 %all_gather.18 = bf16[384,576]{0,1:T(8,128)(2,1)S(1)} all-gather(bf16[384,144]{0,1:T(8,128)(2,1)} %param.8), channel_id=1, replica_groups=mesh['dp'=2,'fsdp'=4,'tensor'=4] {'fsdp'}, dimensions={1}, use_global_device_ids=true | all-gather | bytes 552960 | tf_op jit(solution)/shard_map/all_gather | solution.py:46
  29.9 16.6 %all_gather.15 = bf16[512,576]{0,1:T(8,128)(2,1)S(1)} all-gather(bf16[128,576]{0,1:T(8,128)(2,1)S(1)} %copy-done), channel_id=1, replica_groups=mesh['dp'=2,'fsdp'=4,'tensor'=4] {'tensor'}, dimensions={0}, use_global_device_ids=true | all-gather | bytes 737280 | tf_op jit(solution)/shard_map/all_gather | solution.py:39
  46.5 15.2 %all_gather.19 = bf16[512,576]{0,1:T(8,128)(2,1)S(1)} all-gather(bf16[128,576]{0,1:T(8,128)(2,1)S(1)} %copy-done.1), channel_id=1, replica_groups=mesh['dp'=2,'fsdp'=4,'tensor'=4] {'tensor'}, dimensions={0}, use_global_device_ids=true | all-gather | bytes 737280 | tf_op jit(solution)/shard_map/all_gather | solution.py:40
  61.8 0.6 fusion.6
  62.4 0.6 fusion.5
  62.9 0.8 multiply_convert_fusion
  63.8 0.5 fusion.3
  64.3 0.5 fusion.2
  64.7 0.5 fusion.1
  65.2 1.3 pad_maximum_fusion
  66.5 0.5 convolution_convert_fusion
  67.0 1.1 copy.10
  68.2 0.5 fusion.7
  68.7 0.5 fusion
  69.2 1.1 copy.12
  70.4 21.2 %reduce-scatter.8.cloned.1.call-done = bf16[3,144,384]{2,1,0:T(8,128)(2,1)} async-done(((bf16[3,576,384]{2,1,0:T(8,128)(2,1)}), bf16[3,144,384]{2,1,0:T(8,128)(2,1)}) %reduce-scatter.8.cloned.1.call-update) | async-done | bytes 331792 | tf_op jit(solution)/shard_map/reduce_scatter | solution.py:71
  91.6 24.5 %reduce-scatter.10.cloned.1.call-done = bf16[128,576]{1,0:T(8,128)(2,1)} async-done(((bf16[512,576]{1,0:T(8,128)(2,1)}), bf16[128,576]{1,0:T(8,128)(2,1)}) %reduce-scatter.10.cloned.1.call-update) | async-done | bytes 147472
  116.1 1.7 copy.11
  117.8 21.8 %reduce-scatter.12.cloned.1.call-done = bf16[128,576]{1,0:T(8,128)(2,1)} async-done(((bf16[512,576]{1,0:T(8,128)(2,1)}), bf16[128,576]{1,0:T(8,128)(2,1)}) %reduce-scatter.12.cloned.1.call-update) | async-done | bytes 147472
  139.6 1.7 copy.13
  141.3 23.9 %all-reduce.2.cloned.1.call-done = bf16[3,144,384]{2,1,0:T(8,128)(2,1)} async-done(((bf16[3,144,384]{2,1,0:T(8,128)(2,1)}), bf16[3,144,384]{2,1,0:T(8,128)(2,1)}) %all-reduce.2.cloned.1.call-update) | async-done | bytes 331792 | tf_op jit(solution)/shard_map/psum | solution.py:72
  165.2 1.7 slice_bitcast_fusion
  (12 shorter events, 0.2 us)
Async XLA Ops:
  7.2 22.7 %copy-start = (bf16[128,576]{0,1:T(8,128)(2,1)S(1)}, bf16[128,576]{0,1:T(8,128)(2,1)}, u32[]{:S(2)}) copy-start(bf16[128,576]{0,1:T(8,128)(2,1)} %param.5) | copy-start | bytes 442372
  7.2 39.3 %copy-start.1 = (bf16[128,576]{0,1:T(8,128)(2,1)S(1)}, bf16[128,576]{0,1:T(8,128)(2,1)}, u32[]{:S(2)}) copy-start(bf16[128,576]{0,1:T(8,128)(2,1)} %param.9) | copy-start | bytes 442372
  7.2 84.4 %reduce-scatter.8.cloned.1.call-start = ((), (), s32[]{:S(2)}) async-start(), calls=%async_computation.3 | async-start | bytes 1658880 | tf_op jit(solution)/shard_map/reduce_scatter | solution.py:71
  66.5 49.6 %reduce-scatter.10.cloned.1.call-start = ((), (), s32[]{:S(2)}) async-start(), calls=%async_computation.5 | async-start | bytes 819200
  68.2 71.4 %reduce-scatter.12.cloned.1.call-start = ((), (), s32[]{:S(2)}) async-start(), calls=%async_computation.6 | async-start | bytes 819200
  70.3 94.8 %all-reduce.2.cloned.1.call-start = ((), (), s32[]{:S(2)}) async-start(), calls=%async_computation.4 | async-start | bytes 663552 | tf_op jit(solution)/shard_map/psum | solution.py:72
Sparse Core Ops, SparseCore 0:
  66.6 24.9 reduce-scatter.7
  93.9 22.1 reduce-scatter.9
  118.5 21.0 reduce-scatter.11
  141.9 23.2 all-reduce.1
where the time goes:
time: 174 us; the launch traced here: 173 us
  waiting for transfers between devices  91.4 us (53%)
  blocking collectives  54.5 us (31%)
  between operations  13.8 us (8%)
  local copies, waits for them, and re-layouts  7.32 us (4%)
  matrix products  4.91 us (3%)
    unnamed x6, waiting for transfers between devices  46.4 us
    psum x1, waiting for transfers between devices, per_device(): summed = lax.psum(share, 'dp')  23.9 us
    reduce_scatter x1, waiting for transfers between devices, per_device(): lax.psum_scatter(stacked.astype(jnp.bfloat16), 'fsdp', scatter_dimension=...  21.2 us
    all_gather x1, blocking collectives, per_device(): lax.all_gather(tokens, 'tensor', axis=0, tiled=True)  16.6 us
    all_gather x1, blocking collectives, per_device(): lax.all_gather(cotangent, 'tensor', axis=0, tiled=True)  15.2 us
    all_gather x1, blocking collectives, per_device(): lax.all_gather(gate_weight, 'fsdp', axis=0, tiled=True)  8.55 us
    all_gather x1, blocking collectives, per_device(): lax.all_gather(up_weight, 'fsdp', axis=0, tiled=True)  7.04 us
    all_gather x1, blocking collectives, per_device(): down_full = lax.all_gather(down_weight, 'fsdp', axis=1, tiled=True)  7.04 us
  transfers between devices with their start and end apart: 4, of which 4 were waited for; matrix products, arithmetic and copies ran while one was open for 4% of the time, Pallas kernels for 0%

commit v1 on v0

v1 whole, which is shorter than its diff:
```python
import functools

import jax
import jax.numpy as jnp
from jax import lax
from jax.experimental import pallas as pl
from jax.experimental.pallas import tpu as pltpu
from jax.sharding import PartitionSpec as P

BF16, F32 = jnp.bfloat16, jnp.float32
SCOPED_BYTES = 16 * 1024 * 1024


def contract(left, right, left_dim, right_dim):
    return lax.dot_general(left, right, (((left_dim,), (right_dim,)), ((), ())), preferred_element_type=F32)


def exchange(array, axis, mask):
    return lax.ppermute(array, axis, [(i, i ^ mask) for i in range(lax.axis_size(axis))])


def call(body, outs, operands, inside=pltpu.VMEM, outside=False, scratch=()):
    whole = pl.BlockSpec(memory_space=pltpu.VMEM)
    kind = jax.ShapeDtypeStruct if outside else pltpu.VMEM
    return pl.pallas_call(
        body,
        out_shape=[kind(shape, dtype) for shape, dtype in outs],
        in_specs=[pl.BlockSpec(memory_space=inside)] * len(operands),
        out_specs=[whole] * len(outs),
        scratch_shapes=list(scratch),
        cost_estimate=pl.CostEstimate(flops=1, bytes_accessed=1, transcendentals=0),
        compiler_params=pltpu.CompilerParams(vmem_limit_bytes=SCOPED_BYTES),
    )(*[pltpu.with_memory_space_constraint(operand, inside) for operand in operands])


def stack_kernel(counts, *refs):
    arrays, stacks, sems = refs[: sum(counts)], refs[sum(counts):-1], refs[-1]
    places = [stack.at[i] for stack, count in zip(stacks, counts) for i in range(count)]
    copies = [pltpu.make_async_copy(array, place, sems.at[i]) for i, (array, place) in enumerate(zip(arrays, places))]
    for copy in copies:
        copy.start()
    for copy in copies:
        copy.wait()


def stack(*groups):
    arrays = [array for group in groups for array in group]
    return call(
        functools.partial(stack_kernel, [len(group) for group in groups]),
        [((len(group), *group[0].shape), group[0].dtype) for group in groups],
        arrays,
        inside=pltpu.HBM,
        scratch=[pltpu.SemaphoreType.DMA((len(arrays),))],
    )


def join_kernel(*refs):
    runs, joined = refs[:-1], refs[-1]
    first = 0
    for run in runs:
        joined[first:first + run.shape[0]] = run[...]
        first += run.shape[0]


def assemble_kernel(masks, *refs):
    blocks, (whole, turned) = refs[: len(masks)], refs[len(masks):]
    index = lax.axis_index("fsdp")
    rows = blocks[0].shape[1]
    for mask, block in zip(masks, blocks):
        start = pl.multiple_of((index ^ mask) * rows, 16)
        whole[:, pl.ds(start, rows), :] = block[...]
    for i in range(whole.shape[0]):
        turned[i] = whole[i].T


def forward(turned, rows):
    gate_sum = contract(turned[0], rows, 1, 0)
    up_sum = contract(turned[1], rows, 1, 0)
    sig = 1.0 / (1.0 + jnp.exp(-gate_sum))
    swished = gate_sum * sig
    slopes = up_sum * sig * (1.0 + gate_sum * (1.0 - sig))
    return (swished * up_sum).astype(BF16), swished, slopes


def block_grads(turned, blocks):
    rows = jnp.concatenate([block[0] for block in blocks], axis=1)
    columns = jnp.concatenate([block[1] for block in blocks], axis=1)
    hidden, swished, slopes = forward(turned, rows)
    grad_hidden = contract(turned[2], columns, 1, 0)
    grad_gate = (grad_hidden * slopes).astype(BF16)
    grad_up = (grad_hidden * swished).astype(BF16)
    return rows, columns, hidden, grad_gate, grad_up


def token_parts(whole, hidden, grad_gate, grad_up, parts):
    out = contract(whole[2], hidden, 1, 0)
    back = contract(whole[0], grad_gate, 1, 0) + contract(whole[1], grad_up, 1, 0)
    width = out.shape[1] // len(parts)
    rows = out.shape[0]
    for i, part in enumerate(parts):
        part[0, :rows] = out[:, i * width:(i + 1) * width].astype(part.dtype)
        part[1, :rows] = back[:, i * width:(i + 1) * width].astype(part.dtype)
        if part.shape[1] > rows:
            part[:, rows:] = jnp.zeros((2, part.shape[1] - rows, width), part.dtype)


def weight_terms(rows, columns, hidden, grad_gate, grad_up):
    return ((rows, grad_gate), (rows, grad_up), (columns, hidden))


def group_kernel(count, first, whole, turned, *refs):
    blocks, refs = refs[:count], refs[count:]
    before, (after, *parts) = (None, refs) if first else (refs[0], refs[1:])
    rows, columns, hidden, grad_gate, grad_up = block_grads(turned, blocks)
    for i, (left, right) in enumerate(weight_terms(rows, columns, hidden, grad_gate, grad_up)):
        term = contract(left, right, 1, 1)
        after[i] = term if first else before[i] + term
    token_parts(whole, hidden, grad_gate, grad_up, parts)


def last_kernel(whole, turned, block, _, hidden_out, gate_out, up_out, part):
    _, _, hidden, grad_gate, grad_up = block_grads(turned, [block])
    hidden_out[...], gate_out[...], up_out[...] = hidden, grad_gate, grad_up
    token_parts(whole, hidden, grad_gate, grad_up, [part])


def share_kernel(other, block, hidden, grad_gate, grad_up, before, *outs):
    own = lax.axis_index("fsdp") % 2
    pick = 1 - own if other else own
    pairs, size = outs[0].shape[:2]
    for i, (side, right) in enumerate(((0, grad_gate), (0, grad_up), (1, hidden))):
        for pair in range(pairs):
            start = pl.multiple_of((2 * pair + pick) * size, 16)
            term = contract(block[side, pl.ds(start, size), :], right[...], 1, 1)
            outs[i][pair] = (before[i, pl.ds(start, size), :] + term).astype(outs[i].dtype)


def pair_sums(count, refs):
    kept, received = refs[:count], refs[count:2 * count]
    return lambda i, pair: (kept[i][pair] + received[i][pair].astype(F32)).astype(BF16)


def whole_parts_kernel(count, *refs):
    sums, parts = pair_sums(count, refs), refs[2 * count:]
    index = lax.axis_index("fsdp") // 2
    for mask, part in enumerate(parts):
        for i in range(count):
            part[i] = sums(i, index ^ mask)


def split_parts_kernel(count, *refs):
    sums, parts, rows = pair_sums(count, refs), refs[2 * count:-1], refs[-1]
    index, own = lax.axis_index("fsdp") // 2, lax.axis_index("dp")
    size, length = rows.shape[0] // count, parts[0].shape[0]
    for mask in range(len(parts) // 2):
        for i in range(count):
            rows[i * size:(i + 1) * size] = sums(i, index ^ mask)
        for flip in range(2):
            start = pl.multiple_of((own ^ flip) * (rows.shape[0] - length), 16)
            parts[2 * mask + flip][...] = rows[pl.ds(start, length), :]


def add_kernel(*refs):
    total = refs[0][...].astype(F32)
    for ref in refs[1:-1]:
        total = total + ref[...].astype(F32)
    refs[-1][...] = total.astype(BF16)


def merge_kernel(count, mine, other, *refs):
    outs, rows = refs[:count], refs[count]
    first = lax.axis_index("dp") == 0
    length = mine.shape[0]
    rows[:length] = jnp.where(first, mine[...], other[...])
    rows[rows.shape[0] - length:] = jnp.where(first, other[...], mine[...])
    size = rows.shape[0] // count
    for i, out in enumerate(outs):
        out[...] = rows[i * size:(i + 1) * size]


def middle_kernel(part, received, *refs):
    total = refs[-1]
    total[...] = (part[...] + received[...].astype(F32)).astype(BF16)


def rows_sum_kernel(count, own, *refs):
    received, outs = refs[:count], refs[count:]
    for i, out in enumerate(outs):
        total = own[i]
        for ref in received:
            total = total + ref[i, :out.shape[0]].astype(F32)
        out[...] = total.astype(BF16)


def per_device(tokens, gate_weight, up_weight, down_weight, cotangent):
    tensor, fsdp, dp = (lax.axis_size(axis) for axis in ("tensor", "fsdp", "dp"))
    own_count, width = tokens.shape
    rows, hidden_width = gate_weight.shape

    block, weight = {}, {}
    own_weights = [gate_weight, up_weight, down_weight.T]
    block[0], = stack([tokens.T, cotangent.T])
    weight[0], *runs = stack(own_weights, own_weights[:2], own_weights[2:])
    even, odd = list(range(2, tensor, 2)), list(range(3, tensor, 2))
    for mask in even + [1]:
        block[mask] = exchange(block[0], "tensor", mask)
    for mask in odd:
        block[mask - 1], block[1] = lax.optimization_barrier((block[mask - 1], block[1]))
        block[mask] = exchange(block[mask - 1], "tensor", 1)
    masks = list(range(fsdp))
    weight[1] = exchange(weight[0], "fsdp", 1)
    for mask in masks[2::2]:
        weight[mask], = call(
            join_kernel, [(weight[0].shape, BF16)], [exchange(run, "fsdp", mask) for run in runs]
        )
        weight[mask + 1] = exchange(weight[mask], "fsdp", 1)
    whole, turned = call(
        functools.partial(assemble_kernel, masks),
        [((3, width, hidden_width), BF16), ((3, hidden_width, width), BF16)],
        [weight[mask] for mask in masks],
    )

    part_shape = (2, width, own_count)
    sums_shape = ((3, width, hidden_width), F32)
    sums, part = [], {}
    for group in [[0, 1]] + [[mask] for mask in even + odd[:-1]]:
        kinds = {mask: (part_shape, BF16 if mask % 2 else F32) for mask in group}
        if 1 in group:
            kinds[1] = ((2, width + 16, own_count), BF16)
        sums, *parts = call(
            functools.partial(group_kernel, len(group), 0 in group),
            [sums_shape] + [kinds[mask] for mask in group],
            [whole, turned] + [block[mask] for mask in group] + ([] if 0 in group else [sums]),
        )
        part.update(zip(group, parts))
    last = odd[-1]
    *state, part[last] = call(
        last_kernel,
        [((hidden_width, own_count), BF16)] * 3 + [(part_shape, BF16)],
        [whole, turned, block[last], sums],
    )
    half_shape = (fsdp // 2, rows, hidden_width)
    sent = call(functools.partial(share_kernel, True), [(half_shape, BF16)] * 3, [block[last], *state, sums])
    kept = call(functools.partial(share_kernel, False), [(half_shape, F32)] * 3, [block[last], *state, sums])

    received = [exchange(array, "fsdp", 1) for array in sent]
    if dp == 2:
        total = 3 * rows
        length = (total // 2 + 15) // 16 * 16
        half = ((length, hidden_width), BF16)
        shares = call(
            functools.partial(split_parts_kernel, 3),
            [half] * fsdp,
            [*kept, *received],
            scratch=[pltpu.VMEM((total, hidden_width), BF16)],
        )
        ready = shares[0]
        landed = [ready]
        for i, share in list(enumerate(shares))[1:]:
            mask, flip = 2 * (i // 2), i % 2
            perm = [(d * fsdp + f, (d ^ flip) * fsdp + (f ^ mask)) for d in range(dp) for f in range(fsdp)]
            landed.append(lax.ppermute(share, ("dp", "fsdp"), perm))
        mine, = call(add_kernel, [half], landed)
        grads = call(
            functools.partial(merge_kernel, 3),
            [((rows, hidden_width), BF16)] * 3,
            [mine, exchange(mine, "dp", 1)],
            outside=True,
            scratch=[pltpu.VMEM((total, hidden_width), BF16)],
        )
    else:
        blocks = call(
            functools.partial(whole_parts_kernel, 3),
            [((3, rows, hidden_width), BF16)] * (fsdp // 2),
            [*kept, *received],
        )
        ready = blocks[0]
        landed = [exchange(blocks[mask], "fsdp", 2 * mask) for mask in range(1, fsdp // 2)]
        mine, = call(add_kernel, [(ready.shape, BF16)], [ready, *landed])
        grads = lax.psum(mine, "dp")

    back = [exchange(part[1], "tensor", 1)]
    for mask in even:
        arrived = exchange(part[mask + 1], "tensor", 1)
        total, = call(middle_kernel, [(part_shape, BF16)], [part[mask], arrived, ready])
        back.append(exchange(total, "tensor", mask))
    part[0], grads = lax.optimization_barrier((part[0], grads))
    mixed, grad_tokens = call(
        functools.partial(rows_sum_kernel, len(back)),
        [((width, own_count), BF16)] * 2,
        [part[0], *back],
        outside=True,
    )
    return mixed.T, grad_tokens.T, grads[0], grads[1], grads[2].T


def solution(mesh):
    token_spec = P(("dp", "fsdp", "tensor"), None)
    return jax.shard_map(
        per_device,
        mesh=mesh,
        in_specs=(token_spec, P("fsdp", "tensor"), P("fsdp", "tensor"), P("tensor", "fsdp"), token_spec),
        out_specs=(token_spec, token_spec, P("fsdp", "tensor"), P("fsdp", "tensor"), P("tensor", "fsdp")),
        check_vma=False,
    )
```

time: 174 us -> 52.2 us (0.30)
  waiting for transfers between devices: 91.4 us -> 20.9 us
  blocking collectives: 54.5 us -> 0 us
  starting transfers between devices: 0.16 us -> 20 us
  between operations: 13.8 us -> 0.74 us
  Pallas kernels: 0 us -> 9.92 us
  local copies, waits for them, and re-layouts: 7.32 us -> 0 us
  matrix products: 4.91 us -> 0 us
    all_gather x5 -> x0, blocking collectives: 54.5 us -> none  [the longest x1 16.6 us: per_device(): lax.all_gather(tokens, 'tensor', axis=0, tiled=True)]
    unnamed x6 -> x0, waiting for transfers between devices: 46.4 us -> none
    psum x1 -> x0, waiting for transfers between devices: 23.9 us -> none  [per_device(): summed = lax.psum(share, 'dp')]
    reduce_scatter x1 -> x0, waiting for transfers between devices: 21.2 us -> none  [per_device(): lax.psum_scatter(stacked.astype(jnp.bfloat16), 'fsdp', scatter_dimension=...]
    ppermute x0 -> x17, waiting for transfers between devices: none -> 20.9 us  [the longest x14 16.9 us: exchange(): lax.ppermute(array, axis, [(i, i ^ mask) for i in range(lax.axis_size(axi...]
    ppermute x0 -> x17, starting transfers between devices: none -> 20 us  [the longest x14 16.5 us: exchange(): lax.ppermute(array, axis, [(i, i ^ mask) for i in range(lax.axis_size(axi...]
    pallas_call x0 -> x14, Pallas kernels: none -> 9.92 us  [call(): pl.pallas_call(body, out_shape=[kind(shape, dtype) for shape, dtype in ou...]
    unnamed x8 -> x0, local copies, waits for them, and re-layouts: 5.59 us -> none
  transfers between devices with their start and end apart: 4 -> 17, of which waited for: 4 -> 10; matrix products, arithmetic and copies ran while one was open for 4% -> 0% of each run, Pallas kernels for 0% -> 14%
where the time goes in v1:
time: 52.2 us; the launch traced here: 51.6 us
  waiting for transfers between devices  20.9 us (40%)
  starting transfers between devices  20 us (38%)
  Pallas kernels  9.92 us (19%)
  between operations  0.74 us (1%)
    ppermute x14, waiting for transfers between devices, exchange(): lax.ppermute(array, axis, [(i, i ^ mask) for i in range(lax.axis_size(axi...  16.9 us
    ppermute x14, starting transfers between devices, exchange(): lax.ppermute(array, axis, [(i, i ^ mask) for i in range(lax.axis_size(axi...  16.5 us
    pallas_call x14, Pallas kernels, call(): pl.pallas_call(body, out_shape=[kind(shape, dtype) for shape, dtype in ou...  9.92 us
    ppermute x3, waiting for transfers between devices, per_device(): landed.append(lax.ppermute(share, ('dp', 'fsdp'), perm))  4.06 us
    ppermute x3, starting transfers between devices, per_device(): landed.append(lax.ppermute(share, ('dp', 'fsdp'), perm))  3.55 us
  transfers between devices with their start and end apart: 17, of which 10 were waited for; matrix products, arithmetic and copies ran while one was open for 0% of the time, Pallas kernels for 14%

profile of v1, /device:TPU:0, one launch (start us, length us, event | category | flops | bytes accessed | tf_op | source)
XLA Modules:
  0.0 51.6 jit_solution(35653901028393080)
XLA Ops:
  0.6 1.0 %shard_map.95.refs_0_ = bf16[2,576,128]{2,1,0:T(8,128)(2,1)S(1)} custom-call(bf16[576,128]{1,0:T(8,128)(2,1)} %bitcast.8, bf16[576,128]{1,0:T(8,128)(2,1)} %bitcast.9), custom_call_target="tpu_custom_call" | custom-call | flops 1 | bytes 1 | tf_op jit(solution)/shard_map/pallas_call | solution.py:25
  1.6 4.1 %collective-permute-start.4 = (bf16[2,576,128]{2,1,0:T(8,128)(2,1)S(1)}, bf16[2,576,128]{2,1,0:T(8,128)(2,1)S(1)}, u32[]{:S(2)}, u32[]{:S(2)}) collective-permute-start(bf16[2,576,128]{2,1,0:T(8,128)(2,1)S(1)} %shard_map.95.refs_0_), channel_id=1, source_target_pairs={{0,2},{1,3},{2,0},{3,1},{4,6},{5,7},{6,4},{7,5},{8,10},{9,11},{10,... | collective-permute-start | bytes 884744 | tf_op jit(solution)/shard_map/ppermute | solution.py:19
  5.7 1.6 %collective-permute-start.5 = (bf16[2,576,128]{2,1,0:T(8,128)(2,1)S(1)}, bf16[2,576,128]{2,1,0:T(8,128)(2,1)S(1)}, u32[]{:S(2)}, u32[]{:S(2)}) collective-permute-start(bf16[2,576,128]{2,1,0:T(8,128)(2,1)S(1)} %shard_map.95.refs_0_), channel_id=1, source_target_pairs={{0,1},{1,0},{2,3},{3,2},{4,5},{5,4},{6,7},{7,6},{8,9},{9,8},{10,11... | collective-permute-start | bytes 884744 | tf_op jit(solution)/shard_map/ppermute | solution.py:19
  7.3 1.2 %shard_map.92 = (bf16[3,144,384]{2,1,0:T(8,128)(2,1)S(1)}, bf16[2,144,384]{2,1,0:T(8,128)(2,1)S(1)}, bf16[1,144,384]{2,1,0:T(8,128)(2,1)S(1)}) custom-call(bf16[144,384]{1,0:T(8,128)(2,1)} %refs_3_.1, bf16[144,384]{1,0:T(8,128)(2,1)} %refs_4_.1, bf16[144,384]{1,0:T(8,128)(2,1)} %bitcast.6, bf16[144,384]{1,0:T(8,128)(2,1)} %refs_3_.1, ...), custom_call_target="tpu_custom_call" | custom-call | flops 1 | bytes 1 | tf_op jit(solution)/shard_map/pallas_call | solution.py:25
  8.5 1.6 %collective-permute-start.1 = (bf16[2,144,384]{2,1,0:T(8,128)(2,1)S(1)}, bf16[2,144,384]{2,1,0:T(8,128)(2,1)S(1)}, u32[]{:S(2)}, u32[]{:S(2)}) collective-permute-start(bf16[2,144,384]{2,1,0:T(8,128)(2,1)S(1)} %get-tuple-element.41), channel_id=1, source_target_pairs={{0,8},{4,12},{8,0},{12,4},{1,9},{5,13},{9,1},{13,5},{2,10},{6,14},... | collective-permute-start | bytes 663560 | tf_op jit(solution)/shard_map/ppermute | solution.py:19
  10.6 6.9 %collective-permute-done.2.refs_1_ = bf16[1,144,384]{2,1,0:T(8,128)(2,1)S(1)} collective-permute-done((bf16[1,144,384]{2,1,0:T(8,128)(2,1)S(1)}, bf16[1,144,384]{2,1,0:T(8,128)(2,1)S(1)}, u32[]{:S(2)}, u32[]{:S(2)}) %collective-permute-start.2) | collective-permute-done | bytes 110624 | tf_op jit(solution)/shard_map/ppermute | solution.py:19
  17.7 1.5 %collective-permute-done.4.refs_0_ = bf16[2,576,128]{2,1,0:T(8,128)(2,1)S(1)} collective-permute-done((bf16[2,576,128]{2,1,0:T(8,128)(2,1)S(1)}, bf16[2,576,128]{2,1,0:T(8,128)(2,1)S(1)}, u32[]{:S(2)}, u32[]{:S(2)}) %collective-permute-start.4) | collective-permute-done | bytes 294944 | tf_op jit(solution)/shard_map/ppermute | solution.py:19
  19.4 1.5 %collective-permute-start.6 = (bf16[2,576,128]{2,1,0:T(8,128)(2,1)S(1)}, bf16[2,576,128]{2,1,0:T(8,128)(2,1)S(1)}, u32[]{:S(2)}, u32[]{:S(2)}) collective-permute-start(bf16[2,576,128]{2,1,0:T(8,128)(2,1)S(1)} %collective-permute-done.4.refs_0_), channel_id=1, source_target_pairs={{0,1},{1,0},{2,3},{3,2},{4,5},{5,4},{6,7},{7,6},{8,9},{9,8},{10,11... | collective-permute-start | bytes 884744 | tf_op jit(solution)/shard_map/ppermute | solution.py:19
  20.9 0.6 %shard_map.94 = (bf16[3,576,384]{2,1,0:T(8,128)(2,1)S(1)}, bf16[3,384,576]{2,1,0:T(8,128)(2,1)S(1)}) custom-call(bf16[3,144,384]{2,1,0:T(8,128)(2,1)S(1)} %get-tuple-element.40.refs_0_, bf16[3,144,384]{2,1,0:T(8,128)(2,1)S(1)} %collective-permute-done.refs_1_, bf16[3,144,384]{2,1,0:T(8,128)(2,1)S(1)} %shard_map.93.refs_2_, ...), custom_call_target="tpu_custom_call" | custom-call | flops 1 | bytes 1 | tf_op jit(solution)/shard_map/pallas_call | solution.py:25
  21.4 2.0 %shard_map.96 = (f32[3,576,384]{2,1,0:T(8,128)S(1)}, f32[2,576,128]{2,1,0:T(8,128)S(1)}, bf16[2,592,128]{2,1,0:T(8,128)(2,1)S(1)}) custom-call(bf16[3,576,384]{2,1,0:T(8,128)(2,1)S(1)} %get-tuple-element.43.whole, bf16[3,384,576]{2,1,0:T(8,128)(2,1)S(1)} %get-tuple-element.44.turned, bf16[2,576,128]{2,1,0:T(8,128)(2,1)S(1)} %shard_map.95.refs_0_, ...), custom_call_target="tpu_custom_call" | custom-call | flops 1 | bytes 1 | tf_op jit(solution)/shard_map/pallas_call | solution.py:25
  23.5 1.5 %shard_map.97 = (f32[3,576,384]{2,1,0:T(8,128)S(1)}, f32[2,576,128]{2,1,0:T(8,128)S(1)}) custom-call(bf16[3,576,384]{2,1,0:T(8,128)(2,1)S(1)} %get-tuple-element.43.whole, bf16[3,384,576]{2,1,0:T(8,128)(2,1)S(1)} %get-tuple-element.44.turned, bf16[2,576,128]{2,1,0:T(8,128)(2,1)S(1)} %collective-permute-done.4.refs_0_, ...), custom_call_target="tpu_custom_call" | custom-call | flops 1 | bytes 1 | tf_op jit(solution)/shard_map/pallas_call | solution.py:25
  24.9 2.4 %collective-permute-done.6.block = bf16[2,576,128]{2,1,0:T(8,128)(2,1)S(1)} collective-permute-done((bf16[2,576,128]{2,1,0:T(8,128)(2,1)S(1)}, bf16[2,576,128]{2,1,0:T(8,128)(2,1)S(1)}, u32[]{:S(2)}, u32[]{:S(2)}) %collective-permute-start.6) | collective-permute-done | bytes 294944 | tf_op jit(solution)/shard_map/ppermute | solution.py:19
  27.3 0.9 %shard_map.98 = (bf16[384,128]{1,0:T(8,128)(2,1)S(1)}, bf16[384,128]{1,0:T(8,128)(2,1)S(1)}, bf16[384,128]{1,0:T(8,128)(2,1)S(1)}, bf16[2,576,128]{2,1,0:T(8,128)(2,1)S(1)}) custom-call(bf16[3,576,384]{2,1,0:T(8,128)(2,1)S(1)} %get-tuple-element.43.whole, bf16[3,384,576]{2,1,0:T(8,128)(2,1)S(1)} %get-tuple-element.44.turned, ...), custom_call_target="tpu_custom_call" | custom-call | flops 1 | bytes 1 | tf_op jit(solution)/shard_map/pallas_call | solution.py:25
  28.3 1.5 %collective-permute-start.15 = (bf16[2,576,128]{2,1,0:T(8,128)(2,1)S(1)}, bf16[2,576,128]{2,1,0:T(8,128)(2,1)S(1)}, u32[]{:S(2)}, u32[]{:S(2)}) collective-permute-start(bf16[2,576,128]{2,1,0:T(8,128)(2,1)S(1)} %get-tuple-element.69), channel_id=1, source_target_pairs={{0,1},{1,0},{2,3},{3,2},{4,5},{5,4},{6,7},{7,6},{8,9},{9,8},{10,11... | collective-permute-start | bytes 884744 | tf_op jit(solution)/shard_map/ppermute | solution.py:19
  32.5 1.6 %collective-permute-start.10 = (bf16[224,384]{1,0:T(8,128)(2,1)S(1)}, bf16[224,384]{1,0:T(8,128)(2,1)S(1)}, u32[]{:S(2)}, u32[]{:S(2)}) collective-permute-start(bf16[224,384]{1,0:T(8,128)(2,1)S(1)} %get-tuple-element.60), channel_id=1, source_target_pairs={{0,16},{4,20},{8,24},{12,28},{16,0},{20,4},{24,8},{28,12},{1,17},{... | collective-permute-start | bytes 516104 | tf_op jit(solution)/shard_map/ppermute | solution.py:262
  34.1 1.5 %collective-permute-start.11 = (bf16[224,384]{1,0:T(8,128)(2,1)S(1)}, bf16[224,384]{1,0:T(8,128)(2,1)S(1)}, u32[]{:S(2)}, u32[]{:S(2)}) collective-permute-start(bf16[224,384]{1,0:T(8,128)(2,1)S(1)} %get-tuple-element.61), channel_id=1, source_target_pairs={{0,8},{4,12},{8,0},{12,4},{16,24},{20,28},{24,16},{28,20},{1,9},{5... | collective-permute-start | bytes 516104 | tf_op jit(solution)/shard_map/ppermute | solution.py:262
  36.1 0.6 %collective-permute-start.14 = (bf16[2,592,128]{2,1,0:T(8,128)(2,1)S(1)}, bf16[2,592,128]{2,1,0:T(8,128)(2,1)S(1)}, u32[]{:S(2)}, u32[]{:S(2)}) collective-permute-start(bf16[2,592,128]{2,1,0:T(8,128)(2,1)S(1)} %get-tuple-element.67), channel_id=1, source_target_pairs={{0,1},{1,0},{2,3},{3,2},{4,5},{5,4},{6,7},{7,6},{8,9},{9,8},{10,11... | collective-permute-start | bytes 909320 | tf_op jit(solution)/shard_map/ppermute | solution.py:19
  36.8 3.1 %collective-permute-start.16 = (bf16[2,576,128]{2,1,0:T(8,128)(2,1)S(1)}, bf16[2,576,128]{2,1,0:T(8,128)(2,1)S(1)}, u32[]{:S(2)}, u32[]{:S(2)}) collective-permute-start(bf16[2,576,128]{2,1,0:T(8,128)(2,1)S(1)} %shard_map.104), channel_id=1, source_target_pairs={{0,2},{1,3},{2,0},{3,1},{4,6},{5,7},{6,4},{7,5},{8,10},{9,11},{10,... | collective-permute-start | bytes 884744 | tf_op jit(solution)/shard_map/ppermute | solution.py:19
  39.9 4.1 %collective-permute-done.11.refs_2_ = bf16[224,384]{1,0:T(8,128)(2,1)S(1)} collective-permute-done((bf16[224,384]{1,0:T(8,128)(2,1)S(1)}, bf16[224,384]{1,0:T(8,128)(2,1)S(1)}, u32[]{:S(2)}, u32[]{:S(2)}) %collective-permute-start.11) | collective-permute-done | bytes 172064 | tf_op jit(solution)/shard_map/ppermute | solution.py:262
  44.1 1.3 %collective-permute-start.13 = (bf16[224,384]{1,0:T(8,128)(2,1)S(1)}, bf16[224,384]{1,0:T(8,128)(2,1)S(1)}, u32[]{:S(2)}, u32[]{:S(2)}) collective-permute-start(bf16[224,384]{1,0:T(8,128)(2,1)S(1)} %shard_map.102.mine), channel_id=1, source_target_pairs={{0,16},{16,0},{1,17},{17,1},{2,18},{18,2},{3,19},{19,3},{4,20},{20... | collective-permute-start | bytes 516104 | tf_op jit(solution)/shard_map/ppermute | solution.py:19
  45.4 4.2 %collective-permute-done.13.other = bf16[224,384]{1,0:T(8,128)(2,1)S(1)} collective-permute-done((bf16[224,384]{1,0:T(8,128)(2,1)S(1)}, bf16[224,384]{1,0:T(8,128)(2,1)S(1)}, u32[]{:S(2)}, u32[]{:S(2)}) %collective-permute-start.13) | collective-permute-done | bytes 172064 | tf_op jit(solution)/shard_map/ppermute | solution.py:19
  49.6 0.8 %shard_map.103 = (bf16[144,384]{1,0:T(8,128)(2,1)}, bf16[144,384]{1,0:T(8,128)(2,1)}, bf16[144,384]{1,0:T(8,128)(2,1)}) custom-call(bf16[224,384]{1,0:T(8,128)(2,1)S(1)} %shard_map.102.mine, bf16[224,384]{1,0:T(8,128)(2,1)S(1)} %collective-permute-done.13.other), custom_call_target="tpu_custom_call" | custom-call | flops 1 | bytes 1 | tf_op jit(solution)/shard_map/pallas_call | solution.py:25
  50.3 0.5 %collective-permute-done.14.refs_0_ = bf16[2,592,128]{2,1,0:T(8,128)(2,1)S(1)} collective-permute-done((bf16[2,592,128]{2,1,0:T(8,128)(2,1)S(1)}, bf16[2,592,128]{2,1,0:T(8,128)(2,1)S(1)}, u32[]{:S(2)}, u32[]{:S(2)}) %collective-permute-start.14) | collective-permute-done | bytes 303136 | tf_op jit(solution)/shard_map/ppermute | solution.py:19
  50.9 0.8 %shard_map.105 = (bf16[576,128]{1,0:T(8,128)(2,1)}, bf16[576,128]{1,0:T(8,128)(2,1)}) custom-call(f32[2,576,128]{2,1,0:T(8,128)S(1)} %get-tuple-element.66.own, bf16[2,592,128]{2,1,0:T(8,128)(2,1)S(1)} %collective-permute-done.14.refs_0_, bf16[2,576,128]{2,1,0:T(8,128)(2,1)S(1)} %collective-permute-done.16.refs_1_), custom_call_target="tpu_custom_call" | custom-call | flops 1 | bytes 1 | tf_op jit(solution)/shard_map/pallas_call | solution.py:25
  (24 shorter events, 4.2 us)
Async XLA Ops:
  1.6 17.5 %collective-permute-start.4 = (bf16[2,576,128]{2,1,0:T(8,128)(2,1)S(1)}, bf16[2,576,128]{2,1,0:T(8,128)(2,1)S(1)}, u32[]{:S(2)}, u32[]{:S(2)}) collective-permute-start(bf16[2,576,128]{2,1,0:T(8,128)(2,1)S(1)} %shard_map.95.refs_0_), channel_id=1, source_target_pairs={{0,2},{1,3},{2,0},{3,1},{4,6},{5,7},{6,4},{7,5},{8,10},{9,11},{10,... | collective-permute-start | bytes 884744 | tf_op jit(solution)/shard_map/ppermute | solution.py:19
  5.7 13.6 %collective-permute-start.5 = (bf16[2,576,128]{2,1,0:T(8,128)(2,1)S(1)}, bf16[2,576,128]{2,1,0:T(8,128)(2,1)S(1)}, u32[]{:S(2)}, u32[]{:S(2)}) collective-permute-start(bf16[2,576,128]{2,1,0:T(8,128)(2,1)S(1)} %shard_map.95.refs_0_), channel_id=1, source_target_pairs={{0,1},{1,0},{2,3},{3,2},{4,5},{5,4},{6,7},{7,6},{8,9},{9,8},{10,11... | collective-permute-start | bytes 884744 | tf_op jit(solution)/shard_map/ppermute | solution.py:19
  8.5 9.0 %collective-permute-start.1 = (bf16[2,144,384]{2,1,0:T(8,128)(2,1)S(1)}, bf16[2,144,384]{2,1,0:T(8,128)(2,1)S(1)}, u32[]{:S(2)}, u32[]{:S(2)}) collective-permute-start(bf16[2,144,384]{2,1,0:T(8,128)(2,1)S(1)} %get-tuple-element.41), channel_id=1, source_target_pairs={{0,8},{4,12},{8,0},{12,4},{1,9},{5,13},{9,1},{13,5},{2,10},{6,14},... | collective-permute-start | bytes 663560 | tf_op jit(solution)/shard_map/ppermute | solution.py:19
  10.1 7.5 %collective-permute-start.2 = (bf16[1,144,384]{2,1,0:T(8,128)(2,1)S(1)}, bf16[1,144,384]{2,1,0:T(8,128)(2,1)S(1)}, u32[]{:S(2)}, u32[]{:S(2)}) collective-permute-start(bf16[1,144,384]{2,1,0:T(8,128)(2,1)S(1)} %get-tuple-element.42), channel_id=1, source_target_pairs={{0,8},{4,12},{8,0},{12,4},{1,9},{5,13},{9,1},{13,5},{2,10},{6,14},... | collective-permute-start | bytes 331784 | tf_op jit(solution)/shard_map/ppermute | solution.py:19
  10.6 10.2 %collective-permute-start = (bf16[3,144,384]{2,1,0:T(8,128)(2,1)S(1)}, bf16[3,144,384]{2,1,0:T(8,128)(2,1)S(1)}, u32[]{:S(2)}, u32[]{:S(2)}) collective-permute-start(bf16[3,144,384]{2,1,0:T(8,128)(2,1)S(1)} %get-tuple-element.40.refs_0_), channel_id=1, source_target_pairs={{0,4},{4,0},{8,12},{12,8},{1,5},{5,1},{9,13},{13,9},{2,6},{6,2},{1... | collective-permute-start | bytes 995336 | tf_op jit(solution)/shard_map/ppermute | solution.py:19
  17.6 3.2 %collective-permute-start.3 = (bf16[3,144,384]{2,1,0:T(8,128)(2,1)S(1)}, bf16[3,144,384]{2,1,0:T(8,128)(2,1)S(1)}, u32[]{:S(2)}, u32[]{:S(2)}) collective-permute-start(bf16[3,144,384]{2,1,0:T(8,128)(2,1)S(1)} %shard_map.93.refs_2_), channel_id=1, source_target_pairs={{0,4},{4,0},{8,12},{12,8},{1,5},{5,1},{9,13},{13,9},{2,6},{6,2},{1... | collective-permute-start | bytes 995336 | tf_op jit(solution)/shard_map/ppermute | solution.py:19
  19.4 7.9 %collective-permute-start.6 = (bf16[2,576,128]{2,1,0:T(8,128)(2,1)S(1)}, bf16[2,576,128]{2,1,0:T(8,128)(2,1)S(1)}, u32[]{:S(2)}, u32[]{:S(2)}) collective-permute-start(bf16[2,576,128]{2,1,0:T(8,128)(2,1)S(1)} %collective-permute-done.4.refs_0_), channel_id=1, source_target_pairs={{0,1},{1,0},{2,3},{3,2},{4,5},{5,4},{6,7},{7,6},{8,9},{9,8},{10,11... | collective-permute-start | bytes 884744 | tf_op jit(solution)/shard_map/ppermute | solution.py:19
  28.3 8.4 %collective-permute-start.15 = (bf16[2,576,128]{2,1,0:T(8,128)(2,1)S(1)}, bf16[2,576,128]{2,1,0:T(8,128)(2,1)S(1)}, u32[]{:S(2)}, u32[]{:S(2)}) collective-permute-start(bf16[2,576,128]{2,1,0:T(8,128)(2,1)S(1)} %get-tuple-element.69), channel_id=1, source_target_pairs={{0,1},{1,0},{2,3},{3,2},{4,5},{5,4},{6,7},{7,6},{8,9},{9,8},{10,11... | collective-permute-start | bytes 884744 | tf_op jit(solution)/shard_map/ppermute | solution.py:19
  30.1 1.5 %collective-permute-start.7 = (bf16[2,144,384]{2,1,0:T(8,128)(2,1)S(1)}, bf16[2,144,384]{2,1,0:T(8,128)(2,1)S(1)}, u32[]{:S(2)}, u32[]{:S(2)}) collective-permute-start(bf16[2,144,384]{2,1,0:T(8,128)(2,1)S(1)} %get-tuple-element.56), channel_id=1, source_target_pairs={{0,4},{4,0},{8,12},{12,8},{1,5},{5,1},{9,13},{13,9},{2,6},{6,2},{1... | collective-permute-start | bytes 663560 | tf_op jit(solution)/shard_map/ppermute | solution.py:19
  30.2 1.8 %collective-permute-start.8 = (bf16[2,144,384]{2,1,0:T(8,128)(2,1)S(1)}, bf16[2,144,384]{2,1,0:T(8,128)(2,1)S(1)}, u32[]{:S(2)}, u32[]{:S(2)}) collective-permute-start(bf16[2,144,384]{2,1,0:T(8,128)(2,1)S(1)} %get-tuple-element.57), channel_id=1, source_target_pairs={{0,4},{4,0},{8,12},{12,8},{1,5},{5,1},{9,13},{13,9},{2,6},{6,2},{1... | collective-permute-start | bytes 663560 | tf_op jit(solution)/shard_map/ppermute | solution.py:19
  30.7 1.6 %collective-permute-start.9 = (bf16[2,144,384]{2,1,0:T(8,128)(2,1)S(1)}, bf16[2,144,384]{2,1,0:T(8,128)(2,1)S(1)}, u32[]{:S(2)}, u32[]{:S(2)}) collective-permute-start(bf16[2,144,384]{2,1,0:T(8,128)(2,1)S(1)} %get-tuple-element.58), channel_id=1, source_target_pairs={{0,4},{4,0},{8,12},{12,8},{1,5},{5,1},{9,13},{13,9},{2,6},{6,2},{1... | collective-permute-start | bytes 663560 | tf_op jit(solution)/shard_map/ppermute | solution.py:19
  32.5 7.4 %collective-permute-start.10 = (bf16[224,384]{1,0:T(8,128)(2,1)S(1)}, bf16[224,384]{1,0:T(8,128)(2,1)S(1)}, u32[]{:S(2)}, u32[]{:S(2)}) collective-permute-start(bf16[224,384]{1,0:T(8,128)(2,1)S(1)} %get-tuple-element.60), channel_id=1, source_target_pairs={{0,16},{4,20},{8,24},{12,28},{16,0},{20,4},{24,8},{28,12},{1,17},{... | collective-permute-start | bytes 516104 | tf_op jit(solution)/shard_map/ppermute | solution.py:262
  34.1 9.9 %collective-permute-start.11 = (bf16[224,384]{1,0:T(8,128)(2,1)S(1)}, bf16[224,384]{1,0:T(8,128)(2,1)S(1)}, u32[]{:S(2)}, u32[]{:S(2)}) collective-permute-start(bf16[224,384]{1,0:T(8,128)(2,1)S(1)} %get-tuple-element.61), channel_id=1, source_target_pairs={{0,8},{4,12},{8,0},{12,4},{16,24},{20,28},{24,16},{28,20},{1,9},{5... | collective-permute-start | bytes 516104 | tf_op jit(solution)/shard_map/ppermute | solution.py:262
  35.6 8.4 %collective-permute-start.12 = (bf16[224,384]{1,0:T(8,128)(2,1)S(1)}, bf16[224,384]{1,0:T(8,128)(2,1)S(1)}, u32[]{:S(2)}, u32[]{:S(2)}) collective-permute-start(bf16[224,384]{1,0:T(8,128)(2,1)S(1)} %get-tuple-element.62), channel_id=1, source_target_pairs={{0,24},{4,28},{8,16},{12,20},{16,8},{20,12},{24,0},{28,4},{1,25},{... | collective-permute-start | bytes 516104 | tf_op jit(solution)/shard_map/ppermute | solution.py:262
  36.1 14.8 %collective-permute-start.14 = (bf16[2,592,128]{2,1,0:T(8,128)(2,1)S(1)}, bf16[2,592,128]{2,1,0:T(8,128)(2,1)S(1)}, u32[]{:S(2)}, u32[]{:S(2)}) collective-permute-start(bf16[2,592,128]{2,1,0:T(8,128)(2,1)S(1)} %get-tuple-element.67), channel_id=1, source_target_pairs={{0,1},{1,0},{2,3},{3,2},{4,5},{5,4},{6,7},{7,6},{8,9},{9,8},{10,11... | collective-permute-start | bytes 909320 | tf_op jit(solution)/shard_map/ppermute | solution.py:19
  36.8 14.1 %collective-permute-start.16 = (bf16[2,576,128]{2,1,0:T(8,128)(2,1)S(1)}, bf16[2,576,128]{2,1,0:T(8,128)(2,1)S(1)}, u32[]{:S(2)}, u32[]{:S(2)}) collective-permute-start(bf16[2,576,128]{2,1,0:T(8,128)(2,1)S(1)} %shard_map.104), channel_id=1, source_target_pairs={{0,2},{1,3},{2,0},{3,1},{4,6},{5,7},{6,4},{7,5},{8,10},{9,11},{10,... | collective-permute-start | bytes 884744 | tf_op jit(solution)/shard_map/ppermute | solution.py:19
  44.1 5.5 %collective-permute-start.13 = (bf16[224,384]{1,0:T(8,128)(2,1)S(1)}, bf16[224,384]{1,0:T(8,128)(2,1)S(1)}, u32[]{:S(2)}, u32[]{:S(2)}) collective-permute-start(bf16[224,384]{1,0:T(8,128)(2,1)S(1)} %shard_map.102.mine), channel_id=1, source_target_pairs={{0,16},{16,0},{1,17},{17,1},{2,18},{18,2},{3,19},{19,3},{4,20},{20... | collective-permute-start | bytes 516104 | tf_op jit(solution)/shard_map/ppermute | solution.py:19

commit v2 on v1

--- a/solution.py
+++ b/solution.py
@@ -201,12 +201,12 @@
     own_weights = [gate_weight, up_weight, down_weight.T]
     block[0], = stack([tokens.T, cotangent.T])
     weight[0], *runs = stack(own_weights, own_weights[:2], own_weights[2:])
-    even, odd = list(range(2, tensor, 2)), list(range(3, tensor, 2))
-    for mask in even + [1]:
+    straight = list(range(3, tensor, 2))
+    for mask in straight + [1]:
         block[mask] = exchange(block[0], "tensor", mask)
-    for mask in odd:
-        block[mask - 1], block[1] = lax.optimization_barrier((block[mask - 1], block[1]))
-        block[mask] = exchange(block[mask - 1], "tensor", 1)
+    for mask in straight:
+        block[mask], block[1] = lax.optimization_barrier((block[mask], block[1]))
+        block[mask ^ 1] = exchange(block[mask], "tensor", 1)
     masks = list(range(fsdp))
     weight[1] = exchange(weight[0], "fsdp", 1)
     for mask in masks[2::2]:
@@ -223,8 +223,10 @@
     part_shape = (2, width, own_count)
     sums_shape = ((3, width, hidden_width), F32)
     sums, part = [], {}
-    for group in [[0, 1]] + [[mask] for mask in even + odd[:-1]]:
-        kinds = {mask: (part_shape, BF16 if mask % 2 else F32) for mask in group}
+    forwarded = [mask ^ 1 for mask in straight]
+    last = forwarded[-1]
+    for group in [[0, 1]] + [[mask] for mask in straight + forwarded[:-1]]:
+        kinds = {mask: (part_shape, BF16 if mask in forwarded else F32) for mask in group}
         if 1 in group:
             kinds[1] = ((2, width + 16, own_count), BF16)
         sums, *parts = call(
@@ -233,7 +235,6 @@
             [whole, turned] + [block[mask] for mask in group] + ([] if 0 in group else [sums]),
         )
         part.update(zip(group, parts))
-    last = odd[-1]
     *state, part[last] = call(
         last_kernel,
         [((hidden_width, own_count), BF16)] * 3 + [(part_shape, BF16)],
@@ -280,8 +281,8 @@
         grads = lax.psum(mine, "dp")
 
     back = [exchange(part[1], "tensor", 1)]
-    for mask in even:
-        arrived = exchange(part[mask + 1], "tensor", 1)
+    for mask in straight:
+        arrived = exchange(part[mask ^ 1], "tensor", 1)
         total, = call(middle_kernel, [(part_shape, BF16)], [part[mask], arrived, ready])
         back.append(exchange(total, "tensor", mask))
     part[0], grads = lax.optimization_barrier((part[0], grads))

time: 52.2 us -> 52.9 us (1.013)
  waiting for transfers between devices: 20.9 us -> 24.8 us
  starting transfers between devices: 20 us -> 17.3 us
    ppermute x14, starting transfers between devices: 16.5 us -> 13.7 us  [exchange(): lax.ppermute(array, axis, [(i, i ^ mask) for i in range(lax.axis_size(axi...]
    ppermute x14, waiting for transfers between devices: 16.9 us -> 19.1 us  [exchange(): lax.ppermute(array, axis, [(i, i ^ mask) for i in range(lax.axis_size(axi...]
    ppermute x3, waiting for transfers between devices: 4.06 us -> 5.73 us  [per_device(): landed.append(lax.ppermute(share, ('dp', 'fsdp'), perm))]
where the time goes in v2:
time: 52.9 us; the launch traced here: 52.8 us
  waiting for transfers between devices  24.8 us (47%)
  starting transfers between devices  17.3 us (33%)
  Pallas kernels  9.93 us (19%)
  between operations  0.75 us (1%)
    ppermute x14, waiting for transfers between devices, exchange(): lax.ppermute(array, axis, [(i, i ^ mask) for i in range(lax.axis_size(axi...  19.1 us
    ppermute x14, starting transfers between devices, exchange(): lax.ppermute(array, axis, [(i, i ^ mask) for i in range(lax.axis_size(axi...  13.7 us
    pallas_call x14, Pallas kernels, call(): pl.pallas_call(body, out_shape=[kind(shape, dtype) for shape, dtype in ou...  9.93 us
    ppermute x3, waiting for transfers between devices, per_device(): landed.append(lax.ppermute(share, ('dp', 'fsdp'), perm))  5.73 us
    ppermute x3, starting transfers between devices, per_device(): landed.append(lax.ppermute(share, ('dp', 'fsdp'), perm))  3.55 us
  transfers between devices with their start and end apart: 17, of which 10 were waited for; matrix products, arithmetic and copies ran while one was open for 0% of the time, Pallas kernels for 14%

profile of v2, /device:TPU:0, one launch (start us, length us, event | category | flops | bytes accessed | tf_op | source)
XLA Modules:
  0.0 52.8 jit_solution(14496155425280155972)
XLA Ops:
  0.6 1.0 %shard_map.95.refs_0_ = bf16[2,576,128]{2,1,0:T(8,128)(2,1)S(1)} custom-call(bf16[576,128]{1,0:T(8,128)(2,1)} %bitcast.8, bf16[576,128]{1,0:T(8,128)(2,1)} %bitcast.9), custom_call_target="tpu_custom_call" | custom-call | flops 1 | bytes 1 | tf_op jit(solution)/shard_map/pallas_call | solution.py:25
  1.6 5.1 %collective-permute-start.4 = (bf16[2,576,128]{2,1,0:T(8,128)(2,1)S(1)}, bf16[2,576,128]{2,1,0:T(8,128)(2,1)S(1)}, u32[]{:S(2)}, u32[]{:S(2)}) collective-permute-start(bf16[2,576,128]{2,1,0:T(8,128)(2,1)S(1)} %shard_map.95.refs_0_), channel_id=1, source_target_pairs={{0,3},{1,2},{2,1},{3,0},{4,7},{5,6},{6,5},{7,4},{8,11},{9,10},{10,... | collective-permute-start | bytes 884744 | tf_op jit(solution)/shard_map/ppermute | solution.py:19
  6.8 1.2 %shard_map.92 = (bf16[3,144,384]{2,1,0:T(8,128)(2,1)S(1)}, bf16[2,144,384]{2,1,0:T(8,128)(2,1)S(1)}, bf16[1,144,384]{2,1,0:T(8,128)(2,1)S(1)}) custom-call(bf16[144,384]{1,0:T(8,128)(2,1)} %refs_3_.1, bf16[144,384]{1,0:T(8,128)(2,1)} %refs_4_.1, bf16[144,384]{1,0:T(8,128)(2,1)} %bitcast.6, bf16[144,384]{1,0:T(8,128)(2,1)} %refs_3_.1, ...), custom_call_target="tpu_custom_call" | custom-call | flops 1 | bytes 1 | tf_op jit(solution)/shard_map/pallas_call | solution.py:25
  8.0 1.6 %collective-permute-start.1 = (bf16[2,144,384]{2,1,0:T(8,128)(2,1)S(1)}, bf16[2,144,384]{2,1,0:T(8,128)(2,1)S(1)}, u32[]{:S(2)}, u32[]{:S(2)}) collective-permute-start(bf16[2,144,384]{2,1,0:T(8,128)(2,1)S(1)} %get-tuple-element.41), channel_id=1, source_target_pairs={{0,8},{4,12},{8,0},{12,4},{1,9},{5,13},{9,1},{13,5},{2,10},{6,14},... | collective-permute-start | bytes 663560 | tf_op jit(solution)/shard_map/ppermute | solution.py:19
  10.1 7.2 %collective-permute-done.2.refs_1_ = bf16[1,144,384]{2,1,0:T(8,128)(2,1)S(1)} collective-permute-done((bf16[1,144,384]{2,1,0:T(8,128)(2,1)S(1)}, bf16[1,144,384]{2,1,0:T(8,128)(2,1)S(1)}, u32[]{:S(2)}, u32[]{:S(2)}) %collective-permute-start.2) | collective-permute-done | bytes 110624 | tf_op jit(solution)/shard_map/ppermute | solution.py:19
  17.4 2.7 %collective-permute-done.5.refs_1_ = bf16[2,576,128]{2,1,0:T(8,128)(2,1)S(1)} collective-permute-done((bf16[2,576,128]{2,1,0:T(8,128)(2,1)S(1)}, bf16[2,576,128]{2,1,0:T(8,128)(2,1)S(1)}, u32[]{:S(2)}, u32[]{:S(2)}) %collective-permute-start.5) | collective-permute-done | bytes 294944 | tf_op jit(solution)/shard_map/ppermute | solution.py:19
  20.2 1.7 %collective-permute-start.6 = (bf16[2,576,128]{2,1,0:T(8,128)(2,1)S(1)}, bf16[2,576,128]{2,1,0:T(8,128)(2,1)S(1)}, u32[]{:S(2)}, u32[]{:S(2)}) collective-permute-start(bf16[2,576,128]{2,1,0:T(8,128)(2,1)S(1)} %collective-permute-done.4.refs_0_), channel_id=1, source_target_pairs={{0,1},{1,0},{2,3},{3,2},{4,5},{5,4},{6,7},{7,6},{8,9},{9,8},{10,11... | collective-permute-start | bytes 884744 | tf_op jit(solution)/shard_map/ppermute | solution.py:19
  21.9 0.6 %shard_map.94 = (bf16[3,576,384]{2,1,0:T(8,128)(2,1)S(1)}, bf16[3,384,576]{2,1,0:T(8,128)(2,1)S(1)}) custom-call(bf16[3,144,384]{2,1,0:T(8,128)(2,1)S(1)} %get-tuple-element.40.refs_0_, bf16[3,144,384]{2,1,0:T(8,128)(2,1)S(1)} %collective-permute-done.refs_1_, bf16[3,144,384]{2,1,0:T(8,128)(2,1)S(1)} %shard_map.93.refs_2_, ...), custom_call_target="tpu_custom_call" | custom-call | flops 1 | bytes 1 | tf_op jit(solution)/shard_map/pallas_call | solution.py:25
  22.5 2.0 %shard_map.96 = (f32[3,576,384]{2,1,0:T(8,128)S(1)}, f32[2,576,128]{2,1,0:T(8,128)S(1)}, bf16[2,592,128]{2,1,0:T(8,128)(2,1)S(1)}) custom-call(bf16[3,576,384]{2,1,0:T(8,128)(2,1)S(1)} %get-tuple-element.43.whole, bf16[3,384,576]{2,1,0:T(8,128)(2,1)S(1)} %get-tuple-element.44.turned, bf16[2,576,128]{2,1,0:T(8,128)(2,1)S(1)} %shard_map.95.refs_0_, ...), custom_call_target="tpu_custom_call" | custom-call | flops 1 | bytes 1 | tf_op jit(solution)/shard_map/pallas_call | solution.py:25
  24.5 1.5 %shard_map.97 = (f32[3,576,384]{2,1,0:T(8,128)S(1)}, f32[2,576,128]{2,1,0:T(8,128)S(1)}) custom-call(bf16[3,576,384]{2,1,0:T(8,128)(2,1)S(1)} %get-tuple-element.43.whole, bf16[3,384,576]{2,1,0:T(8,128)(2,1)S(1)} %get-tuple-element.44.turned, bf16[2,576,128]{2,1,0:T(8,128)(2,1)S(1)} %collective-permute-done.4.refs_0_, ...), custom_call_target="tpu_custom_call" | custom-call | flops 1 | bytes 1 | tf_op jit(solution)/shard_map/pallas_call | solution.py:25
  26.0 3.2 %collective-permute-done.6.block = bf16[2,576,128]{2,1,0:T(8,128)(2,1)S(1)} collective-permute-done((bf16[2,576,128]{2,1,0:T(8,128)(2,1)S(1)}, bf16[2,576,128]{2,1,0:T(8,128)(2,1)S(1)}, u32[]{:S(2)}, u32[]{:S(2)}) %collective-permute-start.6) | collective-permute-done | bytes 294944 | tf_op jit(solution)/shard_map/ppermute | solution.py:19
  29.1 0.9 %shard_map.98 = (bf16[384,128]{1,0:T(8,128)(2,1)S(1)}, bf16[384,128]{1,0:T(8,128)(2,1)S(1)}, bf16[384,128]{1,0:T(8,128)(2,1)S(1)}, bf16[2,576,128]{2,1,0:T(8,128)(2,1)S(1)}) custom-call(bf16[3,576,384]{2,1,0:T(8,128)(2,1)S(1)} %get-tuple-element.43.whole, bf16[3,384,576]{2,1,0:T(8,128)(2,1)S(1)} %get-tuple-element.44.turned, ...), custom_call_target="tpu_custom_call" | custom-call | flops 1 | bytes 1 | tf_op jit(solution)/shard_map/pallas_call | solution.py:25
  30.1 0.7 %collective-permute-start.15 = (bf16[2,576,128]{2,1,0:T(8,128)(2,1)S(1)}, bf16[2,576,128]{2,1,0:T(8,128)(2,1)S(1)}, u32[]{:S(2)}, u32[]{:S(2)}) collective-permute-start(bf16[2,576,128]{2,1,0:T(8,128)(2,1)S(1)} %get-tuple-element.69), channel_id=1, source_target_pairs={{0,1},{1,0},{2,3},{3,2},{4,5},{5,4},{6,7},{7,6},{8,9},{9,8},{10,11... | collective-permute-start | bytes 884744 | tf_op jit(solution)/shard_map/ppermute | solution.py:19
  33.6 1.6 %collective-permute-start.10 = (bf16[224,384]{1,0:T(8,128)(2,1)S(1)}, bf16[224,384]{1,0:T(8,128)(2,1)S(1)}, u32[]{:S(2)}, u32[]{:S(2)}) collective-permute-start(bf16[224,384]{1,0:T(8,128)(2,1)S(1)} %get-tuple-element.60), channel_id=1, source_target_pairs={{0,16},{4,20},{8,24},{12,28},{16,0},{20,4},{24,8},{28,12},{1,17},{... | collective-permute-start | bytes 516104 | tf_op jit(solution)/shard_map/ppermute | solution.py:263
  35.1 1.5 %collective-permute-start.11 = (bf16[224,384]{1,0:T(8,128)(2,1)S(1)}, bf16[224,384]{1,0:T(8,128)(2,1)S(1)}, u32[]{:S(2)}, u32[]{:S(2)}) collective-permute-start(bf16[224,384]{1,0:T(8,128)(2,1)S(1)} %get-tuple-element.61), channel_id=1, source_target_pairs={{0,8},{4,12},{8,0},{12,4},{16,24},{20,28},{24,16},{28,20},{1,9},{5... | collective-permute-start | bytes 516104 | tf_op jit(solution)/shard_map/ppermute | solution.py:263
  37.1 1.3 %collective-permute-start.14 = (bf16[2,592,128]{2,1,0:T(8,128)(2,1)S(1)}, bf16[2,592,128]{2,1,0:T(8,128)(2,1)S(1)}, u32[]{:S(2)}, u32[]{:S(2)}) collective-permute-start(bf16[2,592,128]{2,1,0:T(8,128)(2,1)S(1)} %get-tuple-element.67), channel_id=1, source_target_pairs={{0,1},{1,0},{2,3},{3,2},{4,5},{5,4},{6,7},{7,6},{8,9},{9,8},{10,11... | collective-permute-start | bytes 909320 | tf_op jit(solution)/shard_map/ppermute | solution.py:19
  38.6 0.7 %collective-permute-start.16 = (bf16[2,576,128]{2,1,0:T(8,128)(2,1)S(1)}, bf16[2,576,128]{2,1,0:T(8,128)(2,1)S(1)}, u32[]{:S(2)}, u32[]{:S(2)}) collective-permute-start(bf16[2,576,128]{2,1,0:T(8,128)(2,1)S(1)} %shard_map.104), channel_id=1, source_target_pairs={{0,3},{1,2},{2,1},{3,0},{4,7},{5,6},{6,5},{7,4},{8,11},{9,10},{10,... | collective-permute-start | bytes 884744 | tf_op jit(solution)/shard_map/ppermute | solution.py:19
  39.3 1.6 %collective-permute-done.10.refs_1_ = bf16[224,384]{1,0:T(8,128)(2,1)S(1)} collective-permute-done((bf16[224,384]{1,0:T(8,128)(2,1)S(1)}, bf16[224,384]{1,0:T(8,128)(2,1)S(1)}, u32[]{:S(2)}, u32[]{:S(2)}) %collective-permute-start.10) | collective-permute-done | bytes 172064 | tf_op jit(solution)/shard_map/ppermute | solution.py:263
  40.9 4.2 %collective-permute-done.11.refs_2_ = bf16[224,384]{1,0:T(8,128)(2,1)S(1)} collective-permute-done((bf16[224,384]{1,0:T(8,128)(2,1)S(1)}, bf16[224,384]{1,0:T(8,128)(2,1)S(1)}, u32[]{:S(2)}, u32[]{:S(2)}) %collective-permute-start.11) | collective-permute-done | bytes 172064 | tf_op jit(solution)/shard_map/ppermute | solution.py:263
  45.1 1.3 %collective-permute-start.13 = (bf16[224,384]{1,0:T(8,128)(2,1)S(1)}, bf16[224,384]{1,0:T(8,128)(2,1)S(1)}, u32[]{:S(2)}, u32[]{:S(2)}) collective-permute-start(bf16[224,384]{1,0:T(8,128)(2,1)S(1)} %shard_map.102.mine), channel_id=1, source_target_pairs={{0,16},{16,0},{1,17},{17,1},{2,18},{18,2},{3,19},{19,3},{4,20},{20... | collective-permute-start | bytes 516104 | tf_op jit(solution)/shard_map/ppermute | solution.py:19
  46.4 4.2 %collective-permute-done.13.other = bf16[224,384]{1,0:T(8,128)(2,1)S(1)} collective-permute-done((bf16[224,384]{1,0:T(8,128)(2,1)S(1)}, bf16[224,384]{1,0:T(8,128)(2,1)S(1)}, u32[]{:S(2)}, u32[]{:S(2)}) %collective-permute-start.13) | collective-permute-done | bytes 172064 | tf_op jit(solution)/shard_map/ppermute | solution.py:19
  50.6 0.8 %shard_map.103 = (bf16[144,384]{1,0:T(8,128)(2,1)}, bf16[144,384]{1,0:T(8,128)(2,1)}, bf16[144,384]{1,0:T(8,128)(2,1)}) custom-call(bf16[224,384]{1,0:T(8,128)(2,1)S(1)} %shard_map.102.mine, bf16[224,384]{1,0:T(8,128)(2,1)S(1)} %collective-permute-done.13.other), custom_call_target="tpu_custom_call" | custom-call | flops 1 | bytes 1 | tf_op jit(solution)/shard_map/pallas_call | solution.py:25
  51.4 0.6 %collective-permute-done.16.refs_1_ = bf16[2,576,128]{2,1,0:T(8,128)(2,1)S(1)} collective-permute-done((bf16[2,576,128]{2,1,0:T(8,128)(2,1)S(1)}, bf16[2,576,128]{2,1,0:T(8,128)(2,1)S(1)}, u32[]{:S(2)}, u32[]{:S(2)}) %collective-permute-start.16) | collective-permute-done | bytes 294944 | tf_op jit(solution)/shard_map/ppermute | solution.py:19
  52.0 0.8 %shard_map.105 = (bf16[576,128]{1,0:T(8,128)(2,1)}, bf16[576,128]{1,0:T(8,128)(2,1)}) custom-call(f32[2,576,128]{2,1,0:T(8,128)S(1)} %get-tuple-element.66.own, bf16[2,592,128]{2,1,0:T(8,128)(2,1)S(1)} %collective-permute-done.14.refs_0_, bf16[2,576,128]{2,1,0:T(8,128)(2,1)S(1)} %collective-permute-done.16.refs_1_), custom_call_target="tpu_custom_call" | custom-call | flops 1 | bytes 1 | tf_op jit(solution)/shard_map/pallas_call | solution.py:25
  (24 shorter events, 4.0 us)
Async XLA Ops:
  1.6 15.8 %collective-permute-start.4 = (bf16[2,576,128]{2,1,0:T(8,128)(2,1)S(1)}, bf16[2,576,128]{2,1,0:T(8,128)(2,1)S(1)}, u32[]{:S(2)}, u32[]{:S(2)}) collective-permute-start(bf16[2,576,128]{2,1,0:T(8,128)(2,1)S(1)} %shard_map.95.refs_0_), channel_id=1, source_target_pairs={{0,3},{1,2},{2,1},{3,0},{4,7},{5,6},{6,5},{7,4},{8,11},{9,10},{10,... | collective-permute-start | bytes 884744 | tf_op jit(solution)/shard_map/ppermute | solution.py:19
  6.8 13.4 %collective-permute-start.5 = (bf16[2,576,128]{2,1,0:T(8,128)(2,1)S(1)}, bf16[2,576,128]{2,1,0:T(8,128)(2,1)S(1)}, u32[]{:S(2)}, u32[]{:S(2)}) collective-permute-start(bf16[2,576,128]{2,1,0:T(8,128)(2,1)S(1)} %shard_map.95.refs_0_), channel_id=1, source_target_pairs={{0,1},{1,0},{2,3},{3,2},{4,5},{5,4},{6,7},{7,6},{8,9},{9,8},{10,11... | collective-permute-start | bytes 884744 | tf_op jit(solution)/shard_map/ppermute | solution.py:19
  8.0 9.3 %collective-permute-start.1 = (bf16[2,144,384]{2,1,0:T(8,128)(2,1)S(1)}, bf16[2,144,384]{2,1,0:T(8,128)(2,1)S(1)}, u32[]{:S(2)}, u32[]{:S(2)}) collective-permute-start(bf16[2,144,384]{2,1,0:T(8,128)(2,1)S(1)} %get-tuple-element.41), channel_id=1, source_target_pairs={{0,8},{4,12},{8,0},{12,4},{1,9},{5,13},{9,1},{13,5},{2,10},{6,14},... | collective-permute-start | bytes 663560 | tf_op jit(solution)/shard_map/ppermute | solution.py:19
  9.6 7.7 %collective-permute-start.2 = (bf16[1,144,384]{2,1,0:T(8,128)(2,1)S(1)}, bf16[1,144,384]{2,1,0:T(8,128)(2,1)S(1)}, u32[]{:S(2)}, u32[]{:S(2)}) collective-permute-start(bf16[1,144,384]{2,1,0:T(8,128)(2,1)S(1)} %get-tuple-element.42), channel_id=1, source_target_pairs={{0,8},{4,12},{8,0},{12,4},{1,9},{5,13},{9,1},{13,5},{2,10},{6,14},... | collective-permute-start | bytes 331784 | tf_op jit(solution)/shard_map/ppermute | solution.py:19
  10.1 11.8 %collective-permute-start = (bf16[3,144,384]{2,1,0:T(8,128)(2,1)S(1)}, bf16[3,144,384]{2,1,0:T(8,128)(2,1)S(1)}, u32[]{:S(2)}, u32[]{:S(2)}) collective-permute-start(bf16[3,144,384]{2,1,0:T(8,128)(2,1)S(1)} %get-tuple-element.40.refs_0_), channel_id=1, source_target_pairs={{0,4},{4,0},{8,12},{12,8},{1,5},{5,1},{9,13},{13,9},{2,6},{6,2},{1... | collective-permute-start | bytes 995336 | tf_op jit(solution)/shard_map/ppermute | solution.py:19
  17.3 4.5 %collective-permute-start.3 = (bf16[3,144,384]{2,1,0:T(8,128)(2,1)S(1)}, bf16[3,144,384]{2,1,0:T(8,128)(2,1)S(1)}, u32[]{:S(2)}, u32[]{:S(2)}) collective-permute-start(bf16[3,144,384]{2,1,0:T(8,128)(2,1)S(1)} %shard_map.93.refs_2_), channel_id=1, source_target_pairs={{0,4},{4,0},{8,12},{12,8},{1,5},{5,1},{9,13},{13,9},{2,6},{6,2},{1... | collective-permute-start | bytes 995336 | tf_op jit(solution)/shard_map/ppermute | solution.py:19
  20.2 8.9 %collective-permute-start.6 = (bf16[2,576,128]{2,1,0:T(8,128)(2,1)S(1)}, bf16[2,576,128]{2,1,0:T(8,128)(2,1)S(1)}, u32[]{:S(2)}, u32[]{:S(2)}) collective-permute-start(bf16[2,576,128]{2,1,0:T(8,128)(2,1)S(1)} %collective-permute-done.4.refs_0_), channel_id=1, source_target_pairs={{0,1},{1,0},{2,3},{3,2},{4,5},{5,4},{6,7},{7,6},{8,9},{9,8},{10,11... | collective-permute-start | bytes 884744 | tf_op jit(solution)/shard_map/ppermute | solution.py:19
  30.1 8.4 %collective-permute-start.15 = (bf16[2,576,128]{2,1,0:T(8,128)(2,1)S(1)}, bf16[2,576,128]{2,1,0:T(8,128)(2,1)S(1)}, u32[]{:S(2)}, u32[]{:S(2)}) collective-permute-start(bf16[2,576,128]{2,1,0:T(8,128)(2,1)S(1)} %get-tuple-element.69), channel_id=1, source_target_pairs={{0,1},{1,0},{2,3},{3,2},{4,5},{5,4},{6,7},{7,6},{8,9},{9,8},{10,11... | collective-permute-start | bytes 884744 | tf_op jit(solution)/shard_map/ppermute | solution.py:19
  31.2 1.5 %collective-permute-start.7 = (bf16[2,144,384]{2,1,0:T(8,128)(2,1)S(1)}, bf16[2,144,384]{2,1,0:T(8,128)(2,1)S(1)}, u32[]{:S(2)}, u32[]{:S(2)}) collective-permute-start(bf16[2,144,384]{2,1,0:T(8,128)(2,1)S(1)} %get-tuple-element.56), channel_id=1, source_target_pairs={{0,4},{4,0},{8,12},{12,8},{1,5},{5,1},{9,13},{13,9},{2,6},{6,2},{1... | collective-permute-start | bytes 663560 | tf_op jit(solution)/shard_map/ppermute | solution.py:19
  31.3 1.8 %collective-permute-start.8 = (bf16[2,144,384]{2,1,0:T(8,128)(2,1)S(1)}, bf16[2,144,384]{2,1,0:T(8,128)(2,1)S(1)}, u32[]{:S(2)}, u32[]{:S(2)}) collective-permute-start(bf16[2,144,384]{2,1,0:T(8,128)(2,1)S(1)} %get-tuple-element.57), channel_id=1, source_target_pairs={{0,4},{4,0},{8,12},{12,8},{1,5},{5,1},{9,13},{13,9},{2,6},{6,2},{1... | collective-permute-start | bytes 663560 | tf_op jit(solution)/shard_map/ppermute | solution.py:19
  31.8 1.6 %collective-permute-start.9 = (bf16[2,144,384]{2,1,0:T(8,128)(2,1)S(1)}, bf16[2,144,384]{2,1,0:T(8,128)(2,1)S(1)}, u32[]{:S(2)}, u32[]{:S(2)}) collective-permute-start(bf16[2,144,384]{2,1,0:T(8,128)(2,1)S(1)} %get-tuple-element.58), channel_id=1, source_target_pairs={{0,4},{4,0},{8,12},{12,8},{1,5},{5,1},{9,13},{13,9},{2,6},{6,2},{1... | collective-permute-start | bytes 663560 | tf_op jit(solution)/shard_map/ppermute | solution.py:19
  33.6 7.3 %collective-permute-start.10 = (bf16[224,384]{1,0:T(8,128)(2,1)S(1)}, bf16[224,384]{1,0:T(8,128)(2,1)S(1)}, u32[]{:S(2)}, u32[]{:S(2)}) collective-permute-start(bf16[224,384]{1,0:T(8,128)(2,1)S(1)} %get-tuple-element.60), channel_id=1, source_target_pairs={{0,16},{4,20},{8,24},{12,28},{16,0},{20,4},{24,8},{28,12},{1,17},{... | collective-permute-start | bytes 516104 | tf_op jit(solution)/shard_map/ppermute | solution.py:263
  35.1 9.9 %collective-permute-start.11 = (bf16[224,384]{1,0:T(8,128)(2,1)S(1)}, bf16[224,384]{1,0:T(8,128)(2,1)S(1)}, u32[]{:S(2)}, u32[]{:S(2)}) collective-permute-start(bf16[224,384]{1,0:T(8,128)(2,1)S(1)} %get-tuple-element.61), channel_id=1, source_target_pairs={{0,8},{4,12},{8,0},{12,4},{16,24},{20,28},{24,16},{28,20},{1,9},{5... | collective-permute-start | bytes 516104 | tf_op jit(solution)/shard_map/ppermute | solution.py:263
  36.7 8.4 %collective-permute-start.12 = (bf16[224,384]{1,0:T(8,128)(2,1)S(1)}, bf16[224,384]{1,0:T(8,128)(2,1)S(1)}, u32[]{:S(2)}, u32[]{:S(2)}) collective-permute-start(bf16[224,384]{1,0:T(8,128)(2,1)S(1)} %get-tuple-element.62), channel_id=1, source_target_pairs={{0,24},{4,28},{8,16},{12,20},{16,8},{20,12},{24,0},{28,4},{1,25},{... | collective-permute-start | bytes 516104 | tf_op jit(solution)/shard_map/ppermute | solution.py:263
  37.1 14.2 %collective-permute-start.14 = (bf16[2,592,128]{2,1,0:T(8,128)(2,1)S(1)}, bf16[2,592,128]{2,1,0:T(8,128)(2,1)S(1)}, u32[]{:S(2)}, u32[]{:S(2)}) collective-permute-start(bf16[2,592,128]{2,1,0:T(8,128)(2,1)S(1)} %get-tuple-element.67), channel_id=1, source_target_pairs={{0,1},{1,0},{2,3},{3,2},{4,5},{5,4},{6,7},{7,6},{8,9},{9,8},{10,11... | collective-permute-start | bytes 909320 | tf_op jit(solution)/shard_map/ppermute | solution.py:19
  38.6 13.4 %collective-permute-start.16 = (bf16[2,576,128]{2,1,0:T(8,128)(2,1)S(1)}, bf16[2,576,128]{2,1,0:T(8,128)(2,1)S(1)}, u32[]{:S(2)}, u32[]{:S(2)}) collective-permute-start(bf16[2,576,128]{2,1,0:T(8,128)(2,1)S(1)} %shard_map.104), channel_id=1, source_target_pairs={{0,3},{1,2},{2,1},{3,0},{4,7},{5,6},{6,5},{7,4},{8,11},{9,10},{10,... | collective-permute-start | bytes 884744 | tf_op jit(solution)/shard_map/ppermute | solution.py:19
  45.1 5.5 %collective-permute-start.13 = (bf16[224,384]{1,0:T(8,128)(2,1)S(1)}, bf16[224,384]{1,0:T(8,128)(2,1)S(1)}, u32[]{:S(2)}, u32[]{:S(2)}) collective-permute-start(bf16[224,384]{1,0:T(8,128)(2,1)S(1)} %shard_map.102.mine), channel_id=1, source_target_pairs={{0,16},{16,0},{1,17},{17,1},{2,18},{18,2},{3,19},{19,3},{4,20},{20... | collective-permute-start | bytes 516104 | tf_op jit(solution)/shard_map/ppermute | solution.py:19

commit v3 on v2

--- a/solution.py
+++ b/solution.py
@@ -9,6 +9,7 @@
 
 BF16, F32 = jnp.bfloat16, jnp.float32
 SCOPED_BYTES = 16 * 1024 * 1024
+SPARE = 16
 
 
 def contract(left, right, left_dim, right_dim):
@@ -35,19 +36,26 @@
 
 def stack_kernel(counts, *refs):
     arrays, stacks, sems = refs[: sum(counts)], refs[sum(counts):-1], refs[-1]
-    places = [stack.at[i] for stack, count in zip(stacks, counts) for i in range(count)]
-    copies = [pltpu.make_async_copy(array, place, sems.at[i]) for i, (array, place) in enumerate(zip(arrays, places))]
+    places = [(stack, i) for stack, count in zip(stacks, counts) for i in range(count)]
+    copies = [
+        pltpu.make_async_copy(array, stack.at[i, pl.ds(0, array.shape[0]), :], sems.at[number])
+        for number, (array, (stack, i)) in enumerate(zip(arrays, places))
+    ]
     for copy in copies:
         copy.start()
     for copy in copies:
         copy.wait()
 
 
-def stack(*groups):
+def stack(*groups, spare=()):
     arrays = [array for group in groups for array in group]
+    spares = list(spare) + [0] * (len(groups) - len(spare))
     return call(
         functools.partial(stack_kernel, [len(group) for group in groups]),
-        [((len(group), *group[0].shape), group[0].dtype) for group in groups],
+        [
+            ((len(group), group[0].shape[0] + rows, *group[0].shape[1:]), group[0].dtype)
+            for group, rows in zip(groups, spares)
+        ],
         arrays,
         inside=pltpu.HBM,
         scratch=[pltpu.SemaphoreType.DMA((len(arrays),))],
@@ -83,8 +91,8 @@
 
 
 def block_grads(turned, blocks):
-    rows = jnp.concatenate([block[0] for block in blocks], axis=1)
-    columns = jnp.concatenate([block[1] for block in blocks], axis=1)
+    width = turned.shape[2]
+    rows, columns = (jnp.concatenate([block[side, :width] for block in blocks], axis=1) for side in range(2))
     hidden, swished, slopes = forward(turned, rows)
     grad_hidden = contract(turned[2], columns, 1, 0)
     grad_gate = (grad_hidden * slopes).astype(BF16)
@@ -118,21 +126,27 @@
     token_parts(whole, hidden, grad_gate, grad_up, parts)
 
 
-def last_kernel(whole, turned, block, _, hidden_out, gate_out, up_out, part):
+def last_kernel(turned, block, _, hidden_out, gate_out, up_out):
     _, _, hidden, grad_gate, grad_up = block_grads(turned, [block])
     hidden_out[...], gate_out[...], up_out[...] = hidden, grad_gate, grad_up
-    token_parts(whole, hidden, grad_gate, grad_up, [part])
-
-
-def share_kernel(other, block, hidden, grad_gate, grad_up, before, *outs):
-    own = lax.axis_index("fsdp") % 2
-    pick = 1 - own if other else own
+
+
+def share_terms(pick, block, hidden, grad_gate, grad_up, before, outs):
     pairs, size = outs[0].shape[:2]
     for i, (side, right) in enumerate(((0, grad_gate), (0, grad_up), (1, hidden))):
         for pair in range(pairs):
             start = pl.multiple_of((2 * pair + pick) * size, 16)
             term = contract(block[side, pl.ds(start, size), :], right[...], 1, 1)
             outs[i][pair] = (before[i, pl.ds(start, size), :] + term).astype(outs[i].dtype)
+
+
+def sent_kernel(block, hidden, grad_gate, grad_up, before, *outs):
+    share_terms(1 - lax.axis_index("fsdp") % 2, block, hidden, grad_gate, grad_up, before, outs)
+
+
+def kept_kernel(whole, block, hidden, grad_gate, grad_up, before, *outs):
+    share_terms(lax.axis_index("fsdp") % 2, block, hidden, grad_gate, grad_up, before, outs[:-1])
+    token_parts(whole, hidden[...], grad_gate[...], grad_up[...], outs[-1:])
 
 
 def pair_sums(count, refs):
@@ -199,11 +213,12 @@
 
     block, weight = {}, {}
     own_weights = [gate_weight, up_weight, down_weight.T]
-    block[0], = stack([tokens.T, cotangent.T])
+    own = [tokens.T, cotangent.T]
+    near, block[0] = stack(own, own, spare=[SPARE])
     weight[0], *runs = stack(own_weights, own_weights[:2], own_weights[2:])
     straight = list(range(3, tensor, 2))
     for mask in straight + [1]:
-        block[mask] = exchange(block[0], "tensor", mask)
+        block[mask] = exchange(near if mask == 1 else block[0], "tensor", mask)
     for mask in straight:
         block[mask], block[1] = lax.optimization_barrier((block[mask], block[1]))
         block[mask ^ 1] = exchange(block[mask], "tensor", 1)
@@ -226,23 +241,23 @@
     forwarded = [mask ^ 1 for mask in straight]
     last = forwarded[-1]
     for group in [[0, 1]] + [[mask] for mask in straight + forwarded[:-1]]:
-        kinds = {mask: (part_shape, BF16 if mask in forwarded else F32) for mask in group}
-        if 1 in group:
-            kinds[1] = ((2, width + 16, own_count), BF16)
+        kinds = {mask: (part_shape, BF16 if mask % 2 else F32) for mask in group}
         sums, *parts = call(
             functools.partial(group_kernel, len(group), 0 in group),
             [sums_shape] + [kinds[mask] for mask in group],
             [whole, turned] + [block[mask] for mask in group] + ([] if 0 in group else [sums]),
         )
         part.update(zip(group, parts))
-    *state, part[last] = call(
-        last_kernel,
-        [((hidden_width, own_count), BF16)] * 3 + [(part_shape, BF16)],
-        [whole, turned, block[last], sums],
-    )
+    arrived = {}
+    for mask in straight:
+        part[mask], block[last] = lax.optimization_barrier((part[mask], block[last]))
+        arrived[mask] = exchange(part[mask], "tensor", 1)
+    state = call(last_kernel, [((hidden_width, own_count), BF16)] * 3, [turned, block[last], sums])
     half_shape = (fsdp // 2, rows, hidden_width)
-    sent = call(functools.partial(share_kernel, True), [(half_shape, BF16)] * 3, [block[last], *state, sums])
-    kept = call(functools.partial(share_kernel, False), [(half_shape, F32)] * 3, [block[last], *state, sums])
+    sent = call(sent_kernel, [(half_shape, BF16)] * 3, [block[last], *state, sums])
+    *kept, part[last] = call(
+        kept_kernel, [(half_shape, F32)] * 3 + [(part_shape, F32)], [whole, block[last], *state, sums]
+    )
 
     received = [exchange(array, "fsdp", 1) for array in sent]
     if dp == 2:
@@ -280,11 +295,12 @@
         mine, = call(add_kernel, [(ready.shape, BF16)], [ready, *landed])
         grads = lax.psum(mine, "dp")
 
-    back = [exchange(part[1], "tensor", 1)]
+    back = []
     for mask in straight:
-        arrived = exchange(part[mask ^ 1], "tensor", 1)
-        total, = call(middle_kernel, [(part_shape, BF16)], [part[mask], arrived, ready])
-        back.append(exchange(total, "tensor", mask))
+        total, = call(middle_kernel, [(part_shape, BF16)], [part[mask ^ 1], arrived[mask], ready])
+        part[1], total = lax.optimization_barrier((part[1], total))
+        back.append(exchange(total, "tensor", mask ^ 1))
+    back.append(exchange(part[1], "tensor", 1))
     part[0], grads = lax.optimization_barrier((part[0], grads))
     mixed, grad_tokens = call(
         functools.partial(rows_sum_kernel, len(back)),

time: 52.9 us -> 52.2 us (0.987)
  starting transfers between devices: 17.3 us -> 15.8 us
  waiting for transfers between devices: 24.8 us -> 25.4 us
    ppermute x14, starting transfers between devices: 13.7 us -> 12.3 us  [exchange(): lax.ppermute(array, axis, [(i, i ^ mask) for i in range(lax.axis_size(axi...]
    ppermute x14, waiting for transfers between devices: 19.1 us -> 19.9 us  [exchange(): lax.ppermute(array, axis, [(i, i ^ mask) for i in range(lax.axis_size(axi...]
  transfers between devices with their start and end apart: 17 -> 17, of which waited for: 10 -> 10; matrix products, arithmetic and copies ran while one was open for 0% -> 0% of each run, Pallas kernels for 14% -> 16%
where the time goes in v3:
time: 52.2 us; the launch traced here: 52 us
  waiting for transfers between devices  25.4 us (49%)
  starting transfers between devices  15.8 us (30%)
  Pallas kernels  10 us (19%)
  between operations  0.75 us (1%)
    ppermute x14, waiting for transfers between devices, exchange(): lax.ppermute(array, axis, [(i, i ^ mask) for i in range(lax.axis_size(axi...  19.9 us
    ppermute x14, starting transfers between devices, exchange(): lax.ppermute(array, axis, [(i, i ^ mask) for i in range(lax.axis_size(axi...  12.3 us
    pallas_call x14, Pallas kernels, call(): pl.pallas_call(body, out_shape=[kind(shape, dtype) for shape, dtype in ou...  10 us
    ppermute x3, waiting for transfers between devices, per_device(): landed.append(lax.ppermute(share, ('dp', 'fsdp'), perm))  5.49 us
    ppermute x3, starting transfers between devices, per_device(): landed.append(lax.ppermute(share, ('dp', 'fsdp'), perm))  3.55 us
  transfers between devices with their start and end apart: 17, of which 10 were waited for; matrix products, arithmetic and copies ran while one was open for 0% of the time, Pallas kernels for 16%

profile of v3, /device:TPU:0, one launch (start us, length us, event | category | flops | bytes accessed | tf_op | source)
XLA Modules:
  0.0 52.0 jit_solution(4080884333853605377)
XLA Ops:
  0.6 1.2 %shard_map.95 = (bf16[2,592,128]{2,1,0:T(8,128)(2,1)S(1)}, bf16[2,576,128]{2,1,0:T(8,128)(2,1)S(1)}) custom-call(bf16[576,128]{1,0:T(8,128)(2,1)} %bitcast.6, bf16[576,128]{1,0:T(8,128)(2,1)} %bitcast.8, bf16[576,128]{1,0:T(8,128)(2,1)} %bitcast.7, bf16[576,128]{1,0:T(8,128)(2,1)} %bitcast.9), custom_call_target="tpu_custom_call" | custom-call | flops 1 | bytes 1 | tf_op jit(solution)/shard_map/pallas_call | solution.py:26
  1.8 3.1 %collective-permute-start.5 = (bf16[2,592,128]{2,1,0:T(8,128)(2,1)S(1)}, bf16[2,592,128]{2,1,0:T(8,128)(2,1)S(1)}, u32[]{:S(2)}, u32[]{:S(2)}) collective-permute-start(bf16[2,592,128]{2,1,0:T(8,128)(2,1)S(1)} %get-tuple-element.52), channel_id=1, source_target_pairs={{0,1},{1,0},{2,3},{3,2},{4,5},{5,4},{6,7},{7,6},{8,9},{9,8},{10,11... | collective-permute-start | bytes 909320 | tf_op jit(solution)/shard_map/ppermute | solution.py:20
  4.9 2.5 %collective-permute-start.4 = (bf16[2,576,128]{2,1,0:T(8,128)(2,1)S(1)}, bf16[2,576,128]{2,1,0:T(8,128)(2,1)S(1)}, u32[]{:S(2)}, u32[]{:S(2)}) collective-permute-start(bf16[2,576,128]{2,1,0:T(8,128)(2,1)S(1)} %get-tuple-element.51.refs_0_), channel_id=1, source_target_pairs={{0,3},{1,2},{2,1},{3,0},{4,7},{5,6},{6,5},{7,4},{8,11},{9,10},{10,... | collective-permute-start | bytes 884744 | tf_op jit(solution)/shard_map/ppermute | solution.py:20
  7.4 1.2 %shard_map.92 = (bf16[3,144,384]{2,1,0:T(8,128)(2,1)S(1)}, bf16[2,144,384]{2,1,0:T(8,128)(2,1)S(1)}, bf16[1,144,384]{2,1,0:T(8,128)(2,1)S(1)}) custom-call(bf16[144,384]{1,0:T(8,128)(2,1)} %refs_3_.1, bf16[144,384]{1,0:T(8,128)(2,1)} %refs_4_.1, bf16[144,384]{1,0:T(8,128)(2,1)} %bitcast.10, bf16[144,384]{1,0:T(8,128)(2,1)} %refs_3_.1, ...), custom_call_target="tpu_custom_call" | custom-call | flops 1 | bytes 1 | tf_op jit(solution)/shard_map/pallas_call | solution.py:26
  8.6 1.6 %collective-permute-start.1 = (bf16[2,144,384]{2,1,0:T(8,128)(2,1)S(1)}, bf16[2,144,384]{2,1,0:T(8,128)(2,1)S(1)}, u32[]{:S(2)}, u32[]{:S(2)}) collective-permute-start(bf16[2,144,384]{2,1,0:T(8,128)(2,1)S(1)} %get-tuple-element.47), channel_id=1, source_target_pairs={{0,8},{4,12},{8,0},{12,4},{1,9},{5,13},{9,1},{13,5},{2,10},{6,14},... | collective-permute-start | bytes 663560 | tf_op jit(solution)/shard_map/ppermute | solution.py:20
  10.7 6.9 %collective-permute-done.2.refs_1_ = bf16[1,144,384]{2,1,0:T(8,128)(2,1)S(1)} collective-permute-done((bf16[1,144,384]{2,1,0:T(8,128)(2,1)S(1)}, bf16[1,144,384]{2,1,0:T(8,128)(2,1)S(1)}, u32[]{:S(2)}, u32[]{:S(2)}) %collective-permute-start.2) | collective-permute-done | bytes 110624 | tf_op jit(solution)/shard_map/ppermute | solution.py:20
  17.7 2.8 %collective-permute-done.4.refs_0_ = bf16[2,576,128]{2,1,0:T(8,128)(2,1)S(1)} collective-permute-done((bf16[2,576,128]{2,1,0:T(8,128)(2,1)S(1)}, bf16[2,576,128]{2,1,0:T(8,128)(2,1)S(1)}, u32[]{:S(2)}, u32[]{:S(2)}) %collective-permute-start.4) | collective-permute-done | bytes 294944 | tf_op jit(solution)/shard_map/ppermute | solution.py:20
  20.6 0.6 %shard_map.94 = (bf16[3,576,384]{2,1,0:T(8,128)(2,1)S(1)}, bf16[3,384,576]{2,1,0:T(8,128)(2,1)S(1)}) custom-call(bf16[3,144,384]{2,1,0:T(8,128)(2,1)S(1)} %get-tuple-element.46.refs_0_, bf16[3,144,384]{2,1,0:T(8,128)(2,1)S(1)} %collective-permute-done.refs_1_, bf16[3,144,384]{2,1,0:T(8,128)(2,1)S(1)} %shard_map.93.refs_2_, ...), custom_call_target="tpu_custom_call" | custom-call | flops 1 | bytes 1 | tf_op jit(solution)/shard_map/pallas_call | solution.py:26
  21.2 2.0 %shard_map.96 = (f32[3,576,384]{2,1,0:T(8,128)S(1)}, f32[2,576,128]{2,1,0:T(8,128)S(1)}, bf16[2,576,128]{2,1,0:T(8,128)(2,1)S(1)}) custom-call(bf16[3,576,384]{2,1,0:T(8,128)(2,1)S(1)} %get-tuple-element.49.whole, bf16[3,384,576]{2,1,0:T(8,128)(2,1)S(1)} %get-tuple-element.50.turned, bf16[2,576,128]{2,1,0:T(8,128)(2,1)S(1)} %get-tuple-element.51.refs_0_, ...), custom_call_target="tpu_custom_call" | custom-call | flops 1 | bytes 1 | tf_op jit(solution)/shard_map/pallas_call | solution.py:26
  23.2 1.5 %shard_map.97 = (f32[3,576,384]{2,1,0:T(8,128)S(1)}, bf16[2,576,128]{2,1,0:T(8,128)(2,1)S(1)}) custom-call(bf16[3,576,384]{2,1,0:T(8,128)(2,1)S(1)} %get-tuple-element.49.whole, bf16[3,384,576]{2,1,0:T(8,128)(2,1)S(1)} %get-tuple-element.50.turned, bf16[2,576,128]{2,1,0:T(8,128)(2,1)S(1)} %collective-permute-done.4.refs_0_, ...), custom_call_target="tpu_custom_call" | custom-call | flops 1 | bytes 1 | tf_op jit(solution)/shard_map/pallas_call | solution.py:26
  24.7 3.8 %collective-permute-done.6.block = bf16[2,576,128]{2,1,0:T(8,128)(2,1)S(1)} collective-permute-done((bf16[2,576,128]{2,1,0:T(8,128)(2,1)S(1)}, bf16[2,576,128]{2,1,0:T(8,128)(2,1)S(1)}, u32[]{:S(2)}, u32[]{:S(2)}) %collective-permute-start.6) | collective-permute-done | bytes 294944 | tf_op jit(solution)/shard_map/ppermute | solution.py:20
  28.7 0.5 %shard_map.98 = (bf16[384,128]{1,0:T(8,128)(2,1)S(1)}, bf16[384,128]{1,0:T(8,128)(2,1)S(1)}, bf16[384,128]{1,0:T(8,128)(2,1)S(1)}) custom-call(bf16[3,384,576]{2,1,0:T(8,128)(2,1)S(1)} %get-tuple-element.50.turned, bf16[2,576,128]{2,1,0:T(8,128)(2,1)S(1)} %collective-permute-done.6.block, f32[3,576,384]{2,1,0:T(8,128)S(1)} %get-tuple-element.59._.before), custom_call_target="tpu_custom_call" | custom-call | flops 1 | bytes 1 | tf_op jit(solution)/shard_map/pallas_call | solution.py:26
  30.3 0.8 %shard_map.99 = (f32[2,144,384]{2,1,0:T(8,128)S(1)}, f32[2,144,384]{2,1,0:T(8,128)S(1)}, f32[2,144,384]{2,1,0:T(8,128)S(1)}, f32[2,576,128]{2,1,0:T(8,128)S(1)}) custom-call(bf16[3,576,384]{2,1,0:T(8,128)(2,1)S(1)} %get-tuple-element.49.whole, bf16[2,576,128]{2,1,0:T(8,128)(2,1)S(1)} %collective-permute-done.6.block, ...), custom_call_target="tpu_custom_call" | custom-call | flops 1 | bytes 1 | tf_op jit(solution)/shard_map/pallas_call | solution.py:26
  32.1 1.6 %collective-permute-start.10 = (bf16[224,384]{1,0:T(8,128)(2,1)S(1)}, bf16[224,384]{1,0:T(8,128)(2,1)S(1)}, u32[]{:S(2)}, u32[]{:S(2)}) collective-permute-start(bf16[224,384]{1,0:T(8,128)(2,1)S(1)} %get-tuple-element.70), channel_id=1, source_target_pairs={{0,16},{4,20},{8,24},{12,28},{16,0},{20,4},{24,8},{28,12},{1,17},{... | collective-permute-start | bytes 516104 | tf_op jit(solution)/shard_map/ppermute | solution.py:278
  33.6 1.5 %collective-permute-start.11 = (bf16[224,384]{1,0:T(8,128)(2,1)S(1)}, bf16[224,384]{1,0:T(8,128)(2,1)S(1)}, u32[]{:S(2)}, u32[]{:S(2)}) collective-permute-start(bf16[224,384]{1,0:T(8,128)(2,1)S(1)} %get-tuple-element.71), channel_id=1, source_target_pairs={{0,8},{4,12},{8,0},{12,4},{16,24},{20,28},{24,16},{28,20},{1,9},{5... | collective-permute-start | bytes 516104 | tf_op jit(solution)/shard_map/ppermute | solution.py:278
  35.7 1.7 %collective-permute-start.15 = (bf16[2,576,128]{2,1,0:T(8,128)(2,1)S(1)}, bf16[2,576,128]{2,1,0:T(8,128)(2,1)S(1)}, u32[]{:S(2)}, u32[]{:S(2)}) collective-permute-start(bf16[2,576,128]{2,1,0:T(8,128)(2,1)S(1)} %shard_map.104), channel_id=1, source_target_pairs={{0,2},{1,3},{2,0},{3,1},{4,6},{5,7},{6,4},{7,5},{8,10},{9,11},{10,... | collective-permute-start | bytes 884744 | tf_op jit(solution)/shard_map/ppermute | solution.py:20
  37.4 0.6 %collective-permute-start.16 = (bf16[2,576,128]{2,1,0:T(8,128)(2,1)S(1)}, bf16[2,576,128]{2,1,0:T(8,128)(2,1)S(1)}, u32[]{:S(2)}, u32[]{:S(2)}) collective-permute-start(bf16[2,576,128]{2,1,0:T(8,128)(2,1)S(1)} %get-tuple-element.81), channel_id=1, source_target_pairs={{0,1},{1,0},{2,3},{3,2},{4,5},{5,4},{6,7},{7,6},{8,9},{9,8},{10,11... | collective-permute-start | bytes 884744 | tf_op jit(solution)/shard_map/ppermute | solution.py:20
  38.0 1.3 %collective-permute-done.10.refs_1_ = bf16[224,384]{1,0:T(8,128)(2,1)S(1)} collective-permute-done((bf16[224,384]{1,0:T(8,128)(2,1)S(1)}, bf16[224,384]{1,0:T(8,128)(2,1)S(1)}, u32[]{:S(2)}, u32[]{:S(2)}) %collective-permute-start.10) | collective-permute-done | bytes 172064 | tf_op jit(solution)/shard_map/ppermute | solution.py:278
  39.4 4.2 %collective-permute-done.11.refs_2_ = bf16[224,384]{1,0:T(8,128)(2,1)S(1)} collective-permute-done((bf16[224,384]{1,0:T(8,128)(2,1)S(1)}, bf16[224,384]{1,0:T(8,128)(2,1)S(1)}, u32[]{:S(2)}, u32[]{:S(2)}) %collective-permute-start.11) | collective-permute-done | bytes 172064 | tf_op jit(solution)/shard_map/ppermute | solution.py:278
  43.6 1.3 %collective-permute-start.13 = (bf16[224,384]{1,0:T(8,128)(2,1)S(1)}, bf16[224,384]{1,0:T(8,128)(2,1)S(1)}, u32[]{:S(2)}, u32[]{:S(2)}) collective-permute-start(bf16[224,384]{1,0:T(8,128)(2,1)S(1)} %shard_map.102.mine), channel_id=1, source_target_pairs={{0,16},{16,0},{1,17},{17,1},{2,18},{18,2},{3,19},{19,3},{4,20},{20... | collective-permute-start | bytes 516104 | tf_op jit(solution)/shard_map/ppermute | solution.py:20
  44.9 4.2 %collective-permute-done.13.other = bf16[224,384]{1,0:T(8,128)(2,1)S(1)} collective-permute-done((bf16[224,384]{1,0:T(8,128)(2,1)S(1)}, bf16[224,384]{1,0:T(8,128)(2,1)S(1)}, u32[]{:S(2)}, u32[]{:S(2)}) %collective-permute-start.13) | collective-permute-done | bytes 172064 | tf_op jit(solution)/shard_map/ppermute | solution.py:20
  49.1 0.8 %shard_map.103 = (bf16[144,384]{1,0:T(8,128)(2,1)}, bf16[144,384]{1,0:T(8,128)(2,1)}, bf16[144,384]{1,0:T(8,128)(2,1)}) custom-call(bf16[224,384]{1,0:T(8,128)(2,1)S(1)} %shard_map.102.mine, bf16[224,384]{1,0:T(8,128)(2,1)S(1)} %collective-permute-done.13.other), custom_call_target="tpu_custom_call" | custom-call | flops 1 | bytes 1 | tf_op jit(solution)/shard_map/pallas_call | solution.py:26
  49.9 1.4 %collective-permute-done.15.refs_0_ = bf16[2,576,128]{2,1,0:T(8,128)(2,1)S(1)} collective-permute-done((bf16[2,576,128]{2,1,0:T(8,128)(2,1)S(1)}, bf16[2,576,128]{2,1,0:T(8,128)(2,1)S(1)}, u32[]{:S(2)}, u32[]{:S(2)}) %collective-permute-start.15) | collective-permute-done | bytes 294944 | tf_op jit(solution)/shard_map/ppermute | solution.py:20
  51.2 0.8 %shard_map.105 = (bf16[576,128]{1,0:T(8,128)(2,1)}, bf16[576,128]{1,0:T(8,128)(2,1)}) custom-call(f32[2,576,128]{2,1,0:T(8,128)S(1)} %get-tuple-element.76.own, bf16[2,576,128]{2,1,0:T(8,128)(2,1)S(1)} %collective-permute-done.15.refs_0_, bf16[2,576,128]{2,1,0:T(8,128)(2,1)S(1)} %collective-permute-done.16.refs_1_), custom_call_target="tpu_custom_call" | custom-call | flops 1 | bytes 1 | tf_op jit(solution)/shard_map/pallas_call | solution.py:26
  (24 shorter events, 3.6 us)
Async XLA Ops:
  1.8 18.8 %collective-permute-start.5 = (bf16[2,592,128]{2,1,0:T(8,128)(2,1)S(1)}, bf16[2,592,128]{2,1,0:T(8,128)(2,1)S(1)}, u32[]{:S(2)}, u32[]{:S(2)}) collective-permute-start(bf16[2,592,128]{2,1,0:T(8,128)(2,1)S(1)} %get-tuple-element.52), channel_id=1, source_target_pairs={{0,1},{1,0},{2,3},{3,2},{4,5},{5,4},{6,7},{7,6},{8,9},{9,8},{10,11... | collective-permute-start | bytes 909320 | tf_op jit(solution)/shard_map/ppermute | solution.py:20
  4.9 15.7 %collective-permute-start.4 = (bf16[2,576,128]{2,1,0:T(8,128)(2,1)S(1)}, bf16[2,576,128]{2,1,0:T(8,128)(2,1)S(1)}, u32[]{:S(2)}, u32[]{:S(2)}) collective-permute-start(bf16[2,576,128]{2,1,0:T(8,128)(2,1)S(1)} %get-tuple-element.51.refs_0_), channel_id=1, source_target_pairs={{0,3},{1,2},{2,1},{3,0},{4,7},{5,6},{6,5},{7,4},{8,11},{9,10},{10,... | collective-permute-start | bytes 884744 | tf_op jit(solution)/shard_map/ppermute | solution.py:20
  8.6 9.0 %collective-permute-start.1 = (bf16[2,144,384]{2,1,0:T(8,128)(2,1)S(1)}, bf16[2,144,384]{2,1,0:T(8,128)(2,1)S(1)}, u32[]{:S(2)}, u32[]{:S(2)}) collective-permute-start(bf16[2,144,384]{2,1,0:T(8,128)(2,1)S(1)} %get-tuple-element.47), channel_id=1, source_target_pairs={{0,8},{4,12},{8,0},{12,4},{1,9},{5,13},{9,1},{13,5},{2,10},{6,14},... | collective-permute-start | bytes 663560 | tf_op jit(solution)/shard_map/ppermute | solution.py:20
  10.2 7.5 %collective-permute-start.2 = (bf16[1,144,384]{2,1,0:T(8,128)(2,1)S(1)}, bf16[1,144,384]{2,1,0:T(8,128)(2,1)S(1)}, u32[]{:S(2)}, u32[]{:S(2)}) collective-permute-start(bf16[1,144,384]{2,1,0:T(8,128)(2,1)S(1)} %get-tuple-element.48), channel_id=1, source_target_pairs={{0,8},{4,12},{8,0},{12,4},{1,9},{5,13},{9,1},{13,5},{2,10},{6,14},... | collective-permute-start | bytes 331784 | tf_op jit(solution)/shard_map/ppermute | solution.py:20
  10.7 9.9 %collective-permute-start = (bf16[3,144,384]{2,1,0:T(8,128)(2,1)S(1)}, bf16[3,144,384]{2,1,0:T(8,128)(2,1)S(1)}, u32[]{:S(2)}, u32[]{:S(2)}) collective-permute-start(bf16[3,144,384]{2,1,0:T(8,128)(2,1)S(1)} %get-tuple-element.46.refs_0_), channel_id=1, source_target_pairs={{0,4},{4,0},{8,12},{12,8},{1,5},{5,1},{9,13},{13,9},{2,6},{6,2},{1... | collective-permute-start | bytes 995336 | tf_op jit(solution)/shard_map/ppermute | solution.py:20
  17.7 2.9 %collective-permute-start.3 = (bf16[3,144,384]{2,1,0:T(8,128)(2,1)S(1)}, bf16[3,144,384]{2,1,0:T(8,128)(2,1)S(1)}, u32[]{:S(2)}, u32[]{:S(2)}) collective-permute-start(bf16[3,144,384]{2,1,0:T(8,128)(2,1)S(1)} %shard_map.93.refs_2_), channel_id=1, source_target_pairs={{0,4},{4,0},{8,12},{12,8},{1,5},{5,1},{9,13},{13,9},{2,6},{6,2},{1... | collective-permute-start | bytes 995336 | tf_op jit(solution)/shard_map/ppermute | solution.py:20
  20.6 7.9 %collective-permute-start.6 = (bf16[2,576,128]{2,1,0:T(8,128)(2,1)S(1)}, bf16[2,576,128]{2,1,0:T(8,128)(2,1)S(1)}, u32[]{:S(2)}, u32[]{:S(2)}) collective-permute-start(bf16[2,576,128]{2,1,0:T(8,128)(2,1)S(1)} %collective-permute-done.4.refs_0_), channel_id=1, source_target_pairs={{0,1},{1,0},{2,3},{3,2},{4,5},{5,4},{6,7},{7,6},{8,9},{9,8},{10,11... | collective-permute-start | bytes 884744 | tf_op jit(solution)/shard_map/ppermute | solution.py:20
  28.5 7.2 %collective-permute-start.14 = (bf16[2,576,128]{2,1,0:T(8,128)(2,1)S(1)}, bf16[2,576,128]{2,1,0:T(8,128)(2,1)S(1)}, u32[]{:S(2)}, u32[]{:S(2)}) collective-permute-start(bf16[2,576,128]{2,1,0:T(8,128)(2,1)S(1)} %get-tuple-element.79), channel_id=1, source_target_pairs={{0,1},{1,0},{2,3},{3,2},{4,5},{5,4},{6,7},{7,6},{8,9},{9,8},{10,11... | collective-permute-start | bytes 884744 | tf_op jit(solution)/shard_map/ppermute | solution.py:20
  29.7 1.5 %collective-permute-start.7 = (bf16[2,144,384]{2,1,0:T(8,128)(2,1)S(1)}, bf16[2,144,384]{2,1,0:T(8,128)(2,1)S(1)}, u32[]{:S(2)}, u32[]{:S(2)}) collective-permute-start(bf16[2,144,384]{2,1,0:T(8,128)(2,1)S(1)} %get-tuple-element.66), channel_id=1, source_target_pairs={{0,4},{4,0},{8,12},{12,8},{1,5},{5,1},{9,13},{13,9},{2,6},{6,2},{1... | collective-permute-start | bytes 663560 | tf_op jit(solution)/shard_map/ppermute | solution.py:20
  29.8 1.8 %collective-permute-start.8 = (bf16[2,144,384]{2,1,0:T(8,128)(2,1)S(1)}, bf16[2,144,384]{2,1,0:T(8,128)(2,1)S(1)}, u32[]{:S(2)}, u32[]{:S(2)}) collective-permute-start(bf16[2,144,384]{2,1,0:T(8,128)(2,1)S(1)} %get-tuple-element.67), channel_id=1, source_target_pairs={{0,4},{4,0},{8,12},{12,8},{1,5},{5,1},{9,13},{13,9},{2,6},{6,2},{1... | collective-permute-start | bytes 663560 | tf_op jit(solution)/shard_map/ppermute | solution.py:20
  30.3 1.6 %collective-permute-start.9 = (bf16[2,144,384]{2,1,0:T(8,128)(2,1)S(1)}, bf16[2,144,384]{2,1,0:T(8,128)(2,1)S(1)}, u32[]{:S(2)}, u32[]{:S(2)}) collective-permute-start(bf16[2,144,384]{2,1,0:T(8,128)(2,1)S(1)} %get-tuple-element.68), channel_id=1, source_target_pairs={{0,4},{4,0},{8,12},{12,8},{1,5},{5,1},{9,13},{13,9},{2,6},{6,2},{1... | collective-permute-start | bytes 663560 | tf_op jit(solution)/shard_map/ppermute | solution.py:20
  32.1 7.3 %collective-permute-start.10 = (bf16[224,384]{1,0:T(8,128)(2,1)S(1)}, bf16[224,384]{1,0:T(8,128)(2,1)S(1)}, u32[]{:S(2)}, u32[]{:S(2)}) collective-permute-start(bf16[224,384]{1,0:T(8,128)(2,1)S(1)} %get-tuple-element.70), channel_id=1, source_target_pairs={{0,16},{4,20},{8,24},{12,28},{16,0},{20,4},{24,8},{28,12},{1,17},{... | collective-permute-start | bytes 516104 | tf_op jit(solution)/shard_map/ppermute | solution.py:278
  33.6 9.9 %collective-permute-start.11 = (bf16[224,384]{1,0:T(8,128)(2,1)S(1)}, bf16[224,384]{1,0:T(8,128)(2,1)S(1)}, u32[]{:S(2)}, u32[]{:S(2)}) collective-permute-start(bf16[224,384]{1,0:T(8,128)(2,1)S(1)} %get-tuple-element.71), channel_id=1, source_target_pairs={{0,8},{4,12},{8,0},{12,4},{16,24},{20,28},{24,16},{28,20},{1,9},{5... | collective-permute-start | bytes 516104 | tf_op jit(solution)/shard_map/ppermute | solution.py:278
  35.2 8.4 %collective-permute-start.12 = (bf16[224,384]{1,0:T(8,128)(2,1)S(1)}, bf16[224,384]{1,0:T(8,128)(2,1)S(1)}, u32[]{:S(2)}, u32[]{:S(2)}) collective-permute-start(bf16[224,384]{1,0:T(8,128)(2,1)S(1)} %get-tuple-element.72), channel_id=1, source_target_pairs={{0,24},{4,28},{8,16},{12,20},{16,8},{20,12},{24,0},{28,4},{1,25},{... | collective-permute-start | bytes 516104 | tf_op jit(solution)/shard_map/ppermute | solution.py:278
  35.7 15.6 %collective-permute-start.15 = (bf16[2,576,128]{2,1,0:T(8,128)(2,1)S(1)}, bf16[2,576,128]{2,1,0:T(8,128)(2,1)S(1)}, u32[]{:S(2)}, u32[]{:S(2)}) collective-permute-start(bf16[2,576,128]{2,1,0:T(8,128)(2,1)S(1)} %shard_map.104), channel_id=1, source_target_pairs={{0,2},{1,3},{2,0},{3,1},{4,6},{5,7},{6,4},{7,5},{8,10},{9,11},{10,... | collective-permute-start | bytes 884744 | tf_op jit(solution)/shard_map/ppermute | solution.py:20
  37.4 13.8 %collective-permute-start.16 = (bf16[2,576,128]{2,1,0:T(8,128)(2,1)S(1)}, bf16[2,576,128]{2,1,0:T(8,128)(2,1)S(1)}, u32[]{:S(2)}, u32[]{:S(2)}) collective-permute-start(bf16[2,576,128]{2,1,0:T(8,128)(2,1)S(1)} %get-tuple-element.81), channel_id=1, source_target_pairs={{0,1},{1,0},{2,3},{3,2},{4,5},{5,4},{6,7},{7,6},{8,9},{9,8},{10,11... | collective-permute-start | bytes 884744 | tf_op jit(solution)/shard_map/ppermute | solution.py:20
  43.6 5.5 %collective-permute-start.13 = (bf16[224,384]{1,0:T(8,128)(2,1)S(1)}, bf16[224,384]{1,0:T(8,128)(2,1)S(1)}, u32[]{:S(2)}, u32[]{:S(2)}) collective-permute-start(bf16[224,384]{1,0:T(8,128)(2,1)S(1)} %shard_map.102.mine), channel_id=1, source_target_pairs={{0,16},{16,0},{1,17},{17,1},{2,18},{18,2},{3,19},{19,3},{4,20},{20... | collective-permute-start | bytes 516104 | tf_op jit(solution)/shard_map/ppermute | solution.py:20

commit v4 on v3

--- a/solution.py
+++ b/solution.py
@@ -248,10 +248,7 @@
             [whole, turned] + [block[mask] for mask in group] + ([] if 0 in group else [sums]),
         )
         part.update(zip(group, parts))
-    arrived = {}
-    for mask in straight:
-        part[mask], block[last] = lax.optimization_barrier((part[mask], block[last]))
-        arrived[mask] = exchange(part[mask], "tensor", 1)
+    arrived = {mask: exchange(part[mask], "tensor", 1) for mask in straight}
     state = call(last_kernel, [((hidden_width, own_count), BF16)] * 3, [turned, block[last], sums])
     half_shape = (fsdp // 2, rows, hidden_width)
     sent = call(sent_kernel, [(half_shape, BF16)] * 3, [block[last], *state, sums])

time: 52.2 us -> 53.2 us (1.019)
  starting transfers between devices: 15.8 us -> 17.3 us
    ppermute x14, starting transfers between devices: 12.3 us -> 13.8 us  [exchange(): lax.ppermute(array, axis, [(i, i ^ mask) for i in range(lax.axis_size(axi...]
    ppermute x14, waiting for transfers between devices: 19.9 us -> 19.1 us  [exchange(): lax.ppermute(array, axis, [(i, i ^ mask) for i in range(lax.axis_size(axi...]
  transfers between devices with their start and end apart: 17 -> 17, of which waited for: 10 -> 11; matrix products, arithmetic and copies ran while one was open for 0% -> 0% of each run, Pallas kernels for 16% -> 15%
where the time goes in v4:
time: 53.2 us; the launch traced here: 53 us
  waiting for transfers between devices  24.9 us (47%)
  starting transfers between devices  17.3 us (33%)
  Pallas kernels  10 us (19%)
  between operations  0.75 us (1%)
    ppermute x14, waiting for transfers between devices, exchange(): lax.ppermute(array, axis, [(i, i ^ mask) for i in range(lax.axis_size(axi...  19.1 us
    ppermute x14, starting transfers between devices, exchange(): lax.ppermute(array, axis, [(i, i ^ mask) for i in range(lax.axis_size(axi...  13.8 us
    pallas_call x14, Pallas kernels, call(): pl.pallas_call(body, out_shape=[kind(shape, dtype) for shape, dtype in ou...  10 us
    ppermute x3, waiting for transfers between devices, per_device(): landed.append(lax.ppermute(share, ('dp', 'fsdp'), perm))  5.77 us
    ppermute x3, starting transfers between devices, per_device(): landed.append(lax.ppermute(share, ('dp', 'fsdp'), perm))  3.55 us
  transfers between devices with their start and end apart: 17, of which 11 were waited for; matrix products, arithmetic and copies ran while one was open for 0% of the time, Pallas kernels for 15%

profile of v4, /device:TPU:0, one launch (start us, length us, event | category | flops | bytes accessed | tf_op | source)
XLA Modules:
  0.0 53.0 jit_solution(7302400842464252139)
XLA Ops:
  0.6 1.2 %shard_map.95 = (bf16[2,592,128]{2,1,0:T(8,128)(2,1)S(1)}, bf16[2,576,128]{2,1,0:T(8,128)(2,1)S(1)}) custom-call(bf16[576,128]{1,0:T(8,128)(2,1)} %bitcast.6, bf16[576,128]{1,0:T(8,128)(2,1)} %bitcast.8, bf16[576,128]{1,0:T(8,128)(2,1)} %bitcast.7, bf16[576,128]{1,0:T(8,128)(2,1)} %bitcast.9), custom_call_target="tpu_custom_call" | custom-call | flops 1 | bytes 1 | tf_op jit(solution)/shard_map/pallas_call | solution.py:26
  1.8 3.1 %collective-permute-start.5 = (bf16[2,592,128]{2,1,0:T(8,128)(2,1)S(1)}, bf16[2,592,128]{2,1,0:T(8,128)(2,1)S(1)}, u32[]{:S(2)}, u32[]{:S(2)}) collective-permute-start(bf16[2,592,128]{2,1,0:T(8,128)(2,1)S(1)} %get-tuple-element.50), channel_id=1, source_target_pairs={{0,1},{1,0},{2,3},{3,2},{4,5},{5,4},{6,7},{7,6},{8,9},{9,8},{10,11... | collective-permute-start | bytes 909320 | tf_op jit(solution)/shard_map/ppermute | solution.py:20
  4.9 2.5 %collective-permute-start.4 = (bf16[2,576,128]{2,1,0:T(8,128)(2,1)S(1)}, bf16[2,576,128]{2,1,0:T(8,128)(2,1)S(1)}, u32[]{:S(2)}, u32[]{:S(2)}) collective-permute-start(bf16[2,576,128]{2,1,0:T(8,128)(2,1)S(1)} %get-tuple-element.49.refs_0_), channel_id=1, source_target_pairs={{0,3},{1,2},{2,1},{3,0},{4,7},{5,6},{6,5},{7,4},{8,11},{9,10},{10,... | collective-permute-start | bytes 884744 | tf_op jit(solution)/shard_map/ppermute | solution.py:20
  7.4 1.2 %shard_map.92 = (bf16[3,144,384]{2,1,0:T(8,128)(2,1)S(1)}, bf16[2,144,384]{2,1,0:T(8,128)(2,1)S(1)}, bf16[1,144,384]{2,1,0:T(8,128)(2,1)S(1)}) custom-call(bf16[144,384]{1,0:T(8,128)(2,1)} %refs_3_.1, bf16[144,384]{1,0:T(8,128)(2,1)} %refs_4_.1, bf16[144,384]{1,0:T(8,128)(2,1)} %bitcast.10, bf16[144,384]{1,0:T(8,128)(2,1)} %refs_3_.1, ...), custom_call_target="tpu_custom_call" | custom-call | flops 1 | bytes 1 | tf_op jit(solution)/shard_map/pallas_call | solution.py:26
  8.6 1.6 %collective-permute-start.1 = (bf16[2,144,384]{2,1,0:T(8,128)(2,1)S(1)}, bf16[2,144,384]{2,1,0:T(8,128)(2,1)S(1)}, u32[]{:S(2)}, u32[]{:S(2)}) collective-permute-start(bf16[2,144,384]{2,1,0:T(8,128)(2,1)S(1)} %get-tuple-element.45), channel_id=1, source_target_pairs={{0,8},{4,12},{8,0},{12,4},{1,9},{5,13},{9,1},{13,5},{2,10},{6,14},... | collective-permute-start | bytes 663560 | tf_op jit(solution)/shard_map/ppermute | solution.py:20
  10.2 0.5 collective-permute-start.2
  10.7 6.9 %collective-permute-done.2.refs_1_ = bf16[1,144,384]{2,1,0:T(8,128)(2,1)S(1)} collective-permute-done((bf16[1,144,384]{2,1,0:T(8,128)(2,1)S(1)}, bf16[1,144,384]{2,1,0:T(8,128)(2,1)S(1)}, u32[]{:S(2)}, u32[]{:S(2)}) %collective-permute-start.2) | collective-permute-done | bytes 110624 | tf_op jit(solution)/shard_map/ppermute | solution.py:20
  17.7 2.8 %collective-permute-done.4.refs_0_ = bf16[2,576,128]{2,1,0:T(8,128)(2,1)S(1)} collective-permute-done((bf16[2,576,128]{2,1,0:T(8,128)(2,1)S(1)}, bf16[2,576,128]{2,1,0:T(8,128)(2,1)S(1)}, u32[]{:S(2)}, u32[]{:S(2)}) %collective-permute-start.4) | collective-permute-done | bytes 294944 | tf_op jit(solution)/shard_map/ppermute | solution.py:20
  20.6 0.6 %shard_map.94 = (bf16[3,576,384]{2,1,0:T(8,128)(2,1)S(1)}, bf16[3,384,576]{2,1,0:T(8,128)(2,1)S(1)}) custom-call(bf16[3,144,384]{2,1,0:T(8,128)(2,1)S(1)} %get-tuple-element.44.refs_0_, bf16[3,144,384]{2,1,0:T(8,128)(2,1)S(1)} %collective-permute-done.refs_1_, bf16[3,144,384]{2,1,0:T(8,128)(2,1)S(1)} %shard_map.93.refs_2_, ...), custom_call_target="tpu_custom_call" | custom-call | flops 1 | bytes 1 | tf_op jit(solution)/shard_map/pallas_call | solution.py:26
  21.2 2.0 %shard_map.96 = (f32[3,576,384]{2,1,0:T(8,128)S(1)}, f32[2,576,128]{2,1,0:T(8,128)S(1)}, bf16[2,576,128]{2,1,0:T(8,128)(2,1)S(1)}) custom-call(bf16[3,576,384]{2,1,0:T(8,128)(2,1)S(1)} %get-tuple-element.47.whole, bf16[3,384,576]{2,1,0:T(8,128)(2,1)S(1)} %get-tuple-element.48.turned, bf16[2,576,128]{2,1,0:T(8,128)(2,1)S(1)} %get-tuple-element.49.refs_0_, ...), custom_call_target="tpu_custom_call" | custom-call | flops 1 | bytes 1 | tf_op jit(solution)/shard_map/pallas_call | solution.py:26
  23.2 1.5 %shard_map.97 = (f32[3,576,384]{2,1,0:T(8,128)S(1)}, bf16[2,576,128]{2,1,0:T(8,128)(2,1)S(1)}) custom-call(bf16[3,576,384]{2,1,0:T(8,128)(2,1)S(1)} %get-tuple-element.47.whole, bf16[3,384,576]{2,1,0:T(8,128)(2,1)S(1)} %get-tuple-element.48.turned, bf16[2,576,128]{2,1,0:T(8,128)(2,1)S(1)} %collective-permute-done.4.refs_0_, ...), custom_call_target="tpu_custom_call" | custom-call | flops 1 | bytes 1 | tf_op jit(solution)/shard_map/pallas_call | solution.py:26
  24.7 2.1 %collective-permute-start.14 = (bf16[2,576,128]{2,1,0:T(8,128)(2,1)S(1)}, bf16[2,576,128]{2,1,0:T(8,128)(2,1)S(1)}, u32[]{:S(2)}, u32[]{:S(2)}) collective-permute-start(bf16[2,576,128]{2,1,0:T(8,128)(2,1)S(1)} %get-tuple-element.75), channel_id=1, source_target_pairs={{0,1},{1,0},{2,3},{3,2},{4,5},{5,4},{6,7},{7,6},{8,9},{9,8},{10,11... | collective-permute-start | bytes 884744 | tf_op jit(solution)/shard_map/ppermute | solution.py:20
  26.7 3.8 %collective-permute-done.6.block = bf16[2,576,128]{2,1,0:T(8,128)(2,1)S(1)} collective-permute-done((bf16[2,576,128]{2,1,0:T(8,128)(2,1)S(1)}, bf16[2,576,128]{2,1,0:T(8,128)(2,1)S(1)}, u32[]{:S(2)}, u32[]{:S(2)}) %collective-permute-start.6) | collective-permute-done | bytes 294944 | tf_op jit(solution)/shard_map/ppermute | solution.py:20
  30.5 0.5 shard_map.98
  32.1 0.8 %shard_map.99 = (f32[2,144,384]{2,1,0:T(8,128)S(1)}, f32[2,144,384]{2,1,0:T(8,128)S(1)}, f32[2,144,384]{2,1,0:T(8,128)S(1)}, f32[2,576,128]{2,1,0:T(8,128)S(1)}) custom-call(bf16[3,576,384]{2,1,0:T(8,128)(2,1)S(1)} %get-tuple-element.47.whole, bf16[2,576,128]{2,1,0:T(8,128)(2,1)S(1)} %collective-permute-done.6.block, ...), custom_call_target="tpu_custom_call" | custom-call | flops 1 | bytes 1 | tf_op jit(solution)/shard_map/pallas_call | solution.py:26
  33.9 1.6 %collective-permute-start.10 = (bf16[224,384]{1,0:T(8,128)(2,1)S(1)}, bf16[224,384]{1,0:T(8,128)(2,1)S(1)}, u32[]{:S(2)}, u32[]{:S(2)}) collective-permute-start(bf16[224,384]{1,0:T(8,128)(2,1)S(1)} %get-tuple-element.66), channel_id=1, source_target_pairs={{0,16},{4,20},{8,24},{12,28},{16,0},{20,4},{24,8},{28,12},{1,17},{... | collective-permute-start | bytes 516104 | tf_op jit(solution)/shard_map/ppermute | solution.py:275
  35.4 1.5 %collective-permute-start.11 = (bf16[224,384]{1,0:T(8,128)(2,1)S(1)}, bf16[224,384]{1,0:T(8,128)(2,1)S(1)}, u32[]{:S(2)}, u32[]{:S(2)}) collective-permute-start(bf16[224,384]{1,0:T(8,128)(2,1)S(1)} %get-tuple-element.67), channel_id=1, source_target_pairs={{0,8},{4,12},{8,0},{12,4},{16,24},{20,28},{24,16},{28,20},{1,9},{5... | collective-permute-start | bytes 516104 | tf_op jit(solution)/shard_map/ppermute | solution.py:275
  37.6 2.0 %collective-permute-start.16 = (bf16[2,576,128]{2,1,0:T(8,128)(2,1)S(1)}, bf16[2,576,128]{2,1,0:T(8,128)(2,1)S(1)}, u32[]{:S(2)}, u32[]{:S(2)}) collective-permute-start(bf16[2,576,128]{2,1,0:T(8,128)(2,1)S(1)} %get-tuple-element.77), channel_id=1, source_target_pairs={{0,1},{1,0},{2,3},{3,2},{4,5},{5,4},{6,7},{7,6},{8,9},{9,8},{10,11... | collective-permute-start | bytes 884744 | tf_op jit(solution)/shard_map/ppermute | solution.py:20
  39.5 1.6 %collective-permute-done.10.refs_1_ = bf16[224,384]{1,0:T(8,128)(2,1)S(1)} collective-permute-done((bf16[224,384]{1,0:T(8,128)(2,1)S(1)}, bf16[224,384]{1,0:T(8,128)(2,1)S(1)}, u32[]{:S(2)}, u32[]{:S(2)}) %collective-permute-start.10) | collective-permute-done | bytes 172064 | tf_op jit(solution)/shard_map/ppermute | solution.py:275
  41.1 4.2 %collective-permute-done.11.refs_2_ = bf16[224,384]{1,0:T(8,128)(2,1)S(1)} collective-permute-done((bf16[224,384]{1,0:T(8,128)(2,1)S(1)}, bf16[224,384]{1,0:T(8,128)(2,1)S(1)}, u32[]{:S(2)}, u32[]{:S(2)}) %collective-permute-start.11) | collective-permute-done | bytes 172064 | tf_op jit(solution)/shard_map/ppermute | solution.py:275
  45.4 1.3 %collective-permute-start.13 = (bf16[224,384]{1,0:T(8,128)(2,1)S(1)}, bf16[224,384]{1,0:T(8,128)(2,1)S(1)}, u32[]{:S(2)}, u32[]{:S(2)}) collective-permute-start(bf16[224,384]{1,0:T(8,128)(2,1)S(1)} %shard_map.102.mine), channel_id=1, source_target_pairs={{0,16},{16,0},{1,17},{17,1},{2,18},{18,2},{3,19},{19,3},{4,20},{20... | collective-permute-start | bytes 516104 | tf_op jit(solution)/shard_map/ppermute | solution.py:20
  46.7 4.2 %collective-permute-done.13.other = bf16[224,384]{1,0:T(8,128)(2,1)S(1)} collective-permute-done((bf16[224,384]{1,0:T(8,128)(2,1)S(1)}, bf16[224,384]{1,0:T(8,128)(2,1)S(1)}, u32[]{:S(2)}, u32[]{:S(2)}) %collective-permute-start.13) | collective-permute-done | bytes 172064 | tf_op jit(solution)/shard_map/ppermute | solution.py:20
  50.9 0.8 %shard_map.103 = (bf16[144,384]{1,0:T(8,128)(2,1)}, bf16[144,384]{1,0:T(8,128)(2,1)}, bf16[144,384]{1,0:T(8,128)(2,1)}) custom-call(bf16[224,384]{1,0:T(8,128)(2,1)S(1)} %shard_map.102.mine, bf16[224,384]{1,0:T(8,128)(2,1)S(1)} %collective-permute-done.13.other), custom_call_target="tpu_custom_call" | custom-call | flops 1 | bytes 1 | tf_op jit(solution)/shard_map/pallas_call | solution.py:26
  52.2 0.8 %shard_map.105 = (bf16[576,128]{1,0:T(8,128)(2,1)}, bf16[576,128]{1,0:T(8,128)(2,1)}) custom-call(f32[2,576,128]{2,1,0:T(8,128)S(1)} %get-tuple-element.72.own, bf16[2,576,128]{2,1,0:T(8,128)(2,1)S(1)} %collective-permute-done.15.refs_0_, bf16[2,576,128]{2,1,0:T(8,128)(2,1)S(1)} %collective-permute-done.16.refs_1_), custom_call_target="tpu_custom_call" | custom-call | flops 1 | bytes 1 | tf_op jit(solution)/shard_map/pallas_call | solution.py:26
  (24 shorter events, 3.4 us)
Async XLA Ops:
  1.8 18.8 %collective-permute-start.5 = (bf16[2,592,128]{2,1,0:T(8,128)(2,1)S(1)}, bf16[2,592,128]{2,1,0:T(8,128)(2,1)S(1)}, u32[]{:S(2)}, u32[]{:S(2)}) collective-permute-start(bf16[2,592,128]{2,1,0:T(8,128)(2,1)S(1)} %get-tuple-element.50), channel_id=1, source_target_pairs={{0,1},{1,0},{2,3},{3,2},{4,5},{5,4},{6,7},{7,6},{8,9},{9,8},{10,11... | collective-permute-start | bytes 909320 | tf_op jit(solution)/shard_map/ppermute | solution.py:20
  4.9 15.7 %collective-permute-start.4 = (bf16[2,576,128]{2,1,0:T(8,128)(2,1)S(1)}, bf16[2,576,128]{2,1,0:T(8,128)(2,1)S(1)}, u32[]{:S(2)}, u32[]{:S(2)}) collective-permute-start(bf16[2,576,128]{2,1,0:T(8,128)(2,1)S(1)} %get-tuple-element.49.refs_0_), channel_id=1, source_target_pairs={{0,3},{1,2},{2,1},{3,0},{4,7},{5,6},{6,5},{7,4},{8,11},{9,10},{10,... | collective-permute-start | bytes 884744 | tf_op jit(solution)/shard_map/ppermute | solution.py:20
  8.6 9.0 %collective-permute-start.1 = (bf16[2,144,384]{2,1,0:T(8,128)(2,1)S(1)}, bf16[2,144,384]{2,1,0:T(8,128)(2,1)S(1)}, u32[]{:S(2)}, u32[]{:S(2)}) collective-permute-start(bf16[2,144,384]{2,1,0:T(8,128)(2,1)S(1)} %get-tuple-element.45), channel_id=1, source_target_pairs={{0,8},{4,12},{8,0},{12,4},{1,9},{5,13},{9,1},{13,5},{2,10},{6,14},... | collective-permute-start | bytes 663560 | tf_op jit(solution)/shard_map/ppermute | solution.py:20
  10.2 7.5 %collective-permute-start.2 = (bf16[1,144,384]{2,1,0:T(8,128)(2,1)S(1)}, bf16[1,144,384]{2,1,0:T(8,128)(2,1)S(1)}, u32[]{:S(2)}, u32[]{:S(2)}) collective-permute-start(bf16[1,144,384]{2,1,0:T(8,128)(2,1)S(1)} %get-tuple-element.46), channel_id=1, source_target_pairs={{0,8},{4,12},{8,0},{12,4},{1,9},{5,13},{9,1},{13,5},{2,10},{6,14},... | collective-permute-start | bytes 331784 | tf_op jit(solution)/shard_map/ppermute | solution.py:20
  10.7 9.9 %collective-permute-start = (bf16[3,144,384]{2,1,0:T(8,128)(2,1)S(1)}, bf16[3,144,384]{2,1,0:T(8,128)(2,1)S(1)}, u32[]{:S(2)}, u32[]{:S(2)}) collective-permute-start(bf16[3,144,384]{2,1,0:T(8,128)(2,1)S(1)} %get-tuple-element.44.refs_0_), channel_id=1, source_target_pairs={{0,4},{4,0},{8,12},{12,8},{1,5},{5,1},{9,13},{13,9},{2,6},{6,2},{1... | collective-permute-start | bytes 995336 | tf_op jit(solution)/shard_map/ppermute | solution.py:20
  17.7 2.9 %collective-permute-start.3 = (bf16[3,144,384]{2,1,0:T(8,128)(2,1)S(1)}, bf16[3,144,384]{2,1,0:T(8,128)(2,1)S(1)}, u32[]{:S(2)}, u32[]{:S(2)}) collective-permute-start(bf16[3,144,384]{2,1,0:T(8,128)(2,1)S(1)} %shard_map.93.refs_2_), channel_id=1, source_target_pairs={{0,4},{4,0},{8,12},{12,8},{1,5},{5,1},{9,13},{13,9},{2,6},{6,2},{1... | collective-permute-start | bytes 995336 | tf_op jit(solution)/shard_map/ppermute | solution.py:20
  20.6 9.9 %collective-permute-start.6 = (bf16[2,576,128]{2,1,0:T(8,128)(2,1)S(1)}, bf16[2,576,128]{2,1,0:T(8,128)(2,1)S(1)}, u32[]{:S(2)}, u32[]{:S(2)}) collective-permute-start(bf16[2,576,128]{2,1,0:T(8,128)(2,1)S(1)} %collective-permute-done.4.refs_0_), channel_id=1, source_target_pairs={{0,1},{1,0},{2,3},{3,2},{4,5},{5,4},{6,7},{7,6},{8,9},{9,8},{10,11... | collective-permute-start | bytes 884744 | tf_op jit(solution)/shard_map/ppermute | solution.py:20
  24.7 12.8 %collective-permute-start.14 = (bf16[2,576,128]{2,1,0:T(8,128)(2,1)S(1)}, bf16[2,576,128]{2,1,0:T(8,128)(2,1)S(1)}, u32[]{:S(2)}, u32[]{:S(2)}) collective-permute-start(bf16[2,576,128]{2,1,0:T(8,128)(2,1)S(1)} %get-tuple-element.75), channel_id=1, source_target_pairs={{0,1},{1,0},{2,3},{3,2},{4,5},{5,4},{6,7},{7,6},{8,9},{9,8},{10,11... | collective-permute-start | bytes 884744 | tf_op jit(solution)/shard_map/ppermute | solution.py:20
  31.5 1.5 %collective-permute-start.7 = (bf16[2,144,384]{2,1,0:T(8,128)(2,1)S(1)}, bf16[2,144,384]{2,1,0:T(8,128)(2,1)S(1)}, u32[]{:S(2)}, u32[]{:S(2)}) collective-permute-start(bf16[2,144,384]{2,1,0:T(8,128)(2,1)S(1)} %get-tuple-element.62), channel_id=1, source_target_pairs={{0,4},{4,0},{8,12},{12,8},{1,5},{5,1},{9,13},{13,9},{2,6},{6,2},{1... | collective-permute-start | bytes 663560 | tf_op jit(solution)/shard_map/ppermute | solution.py:20
  31.5 1.8 %collective-permute-start.8 = (bf16[2,144,384]{2,1,0:T(8,128)(2,1)S(1)}, bf16[2,144,384]{2,1,0:T(8,128)(2,1)S(1)}, u32[]{:S(2)}, u32[]{:S(2)}) collective-permute-start(bf16[2,144,384]{2,1,0:T(8,128)(2,1)S(1)} %get-tuple-element.63), channel_id=1, source_target_pairs={{0,4},{4,0},{8,12},{12,8},{1,5},{5,1},{9,13},{13,9},{2,6},{6,2},{1... | collective-permute-start | bytes 663560 | tf_op jit(solution)/shard_map/ppermute | solution.py:20
  32.0 1.6 %collective-permute-start.9 = (bf16[2,144,384]{2,1,0:T(8,128)(2,1)S(1)}, bf16[2,144,384]{2,1,0:T(8,128)(2,1)S(1)}, u32[]{:S(2)}, u32[]{:S(2)}) collective-permute-start(bf16[2,144,384]{2,1,0:T(8,128)(2,1)S(1)} %get-tuple-element.64), channel_id=1, source_target_pairs={{0,4},{4,0},{8,12},{12,8},{1,5},{5,1},{9,13},{13,9},{2,6},{6,2},{1... | collective-permute-start | bytes 663560 | tf_op jit(solution)/shard_map/ppermute | solution.py:20
  33.9 7.3 %collective-permute-start.10 = (bf16[224,384]{1,0:T(8,128)(2,1)S(1)}, bf16[224,384]{1,0:T(8,128)(2,1)S(1)}, u32[]{:S(2)}, u32[]{:S(2)}) collective-permute-start(bf16[224,384]{1,0:T(8,128)(2,1)S(1)} %get-tuple-element.66), channel_id=1, source_target_pairs={{0,16},{4,20},{8,24},{12,28},{16,0},{20,4},{24,8},{28,12},{1,17},{... | collective-permute-start | bytes 516104 | tf_op jit(solution)/shard_map/ppermute | solution.py:275
  35.4 9.9 %collective-permute-start.11 = (bf16[224,384]{1,0:T(8,128)(2,1)S(1)}, bf16[224,384]{1,0:T(8,128)(2,1)S(1)}, u32[]{:S(2)}, u32[]{:S(2)}) collective-permute-start(bf16[224,384]{1,0:T(8,128)(2,1)S(1)} %get-tuple-element.67), channel_id=1, source_target_pairs={{0,8},{4,12},{8,0},{12,4},{16,24},{20,28},{24,16},{28,20},{1,9},{5... | collective-permute-start | bytes 516104 | tf_op jit(solution)/shard_map/ppermute | solution.py:275
  36.9 8.4 %collective-permute-start.12 = (bf16[224,384]{1,0:T(8,128)(2,1)S(1)}, bf16[224,384]{1,0:T(8,128)(2,1)S(1)}, u32[]{:S(2)}, u32[]{:S(2)}) collective-permute-start(bf16[224,384]{1,0:T(8,128)(2,1)S(1)} %get-tuple-element.68), channel_id=1, source_target_pairs={{0,24},{4,28},{8,16},{12,20},{16,8},{20,12},{24,0},{28,4},{1,25},{... | collective-permute-start | bytes 516104 | tf_op jit(solution)/shard_map/ppermute | solution.py:275
  37.5 14.6 %collective-permute-start.15 = (bf16[2,576,128]{2,1,0:T(8,128)(2,1)S(1)}, bf16[2,576,128]{2,1,0:T(8,128)(2,1)S(1)}, u32[]{:S(2)}, u32[]{:S(2)}) collective-permute-start(bf16[2,576,128]{2,1,0:T(8,128)(2,1)S(1)} %shard_map.104), channel_id=1, source_target_pairs={{0,2},{1,3},{2,0},{3,1},{4,6},{5,7},{6,4},{7,5},{8,10},{9,11},{10,... | collective-permute-start | bytes 884744 | tf_op jit(solution)/shard_map/ppermute | solution.py:20
  37.6 14.7 %collective-permute-start.16 = (bf16[2,576,128]{2,1,0:T(8,128)(2,1)S(1)}, bf16[2,576,128]{2,1,0:T(8,128)(2,1)S(1)}, u32[]{:S(2)}, u32[]{:S(2)}) collective-permute-start(bf16[2,576,128]{2,1,0:T(8,128)(2,1)S(1)} %get-tuple-element.77), channel_id=1, source_target_pairs={{0,1},{1,0},{2,3},{3,2},{4,5},{5,4},{6,7},{7,6},{8,9},{9,8},{10,11... | collective-permute-start | bytes 884744 | tf_op jit(solution)/shard_map/ppermute | solution.py:20
  45.4 5.5 %collective-permute-start.13 = (bf16[224,384]{1,0:T(8,128)(2,1)S(1)}, bf16[224,384]{1,0:T(8,128)(2,1)S(1)}, u32[]{:S(2)}, u32[]{:S(2)}) collective-permute-start(bf16[224,384]{1,0:T(8,128)(2,1)S(1)} %shard_map.102.mine), channel_id=1, source_target_pairs={{0,16},{16,0},{1,17},{17,1},{2,18},{18,2},{3,19},{19,3},{4,20},{20... | collective-permute-start | bytes 516104 | tf_op jit(solution)/shard_map/ppermute | solution.py:20

commit v5 on v3

--- a/solution.py
+++ b/solution.py
@@ -34,28 +34,28 @@
     )(*[pltpu.with_memory_space_constraint(operand, inside) for operand in operands])
 
 
-def stack_kernel(counts, *refs):
-    arrays, stacks, sems = refs[: sum(counts)], refs[sum(counts):-1], refs[-1]
-    places = [(stack, i) for stack, count in zip(stacks, counts) for i in range(count)]
-    copies = [
-        pltpu.make_async_copy(array, stack.at[i, pl.ds(0, array.shape[0]), :], sems.at[number])
-        for number, (array, (stack, i)) in enumerate(zip(arrays, places))
-    ]
+def stack_kernel(counts, twin, *refs):
+    arrays, sems = refs[: sum(counts)], refs[-1]
+    stacks = refs[len(arrays):len(arrays) + len(counts)]
+    places = [stack.at[i] for stack, count in zip(stacks, counts) for i in range(count)]
+    copies = [pltpu.make_async_copy(array, place, sems.at[i]) for i, (array, place) in enumerate(zip(arrays, places))]
     for copy in copies:
         copy.start()
     for copy in copies:
         copy.wait()
-
-
-def stack(*groups, spare=()):
+    if twin:
+        refs[-2][:, :stacks[0].shape[1]] = stacks[0][...]
+
+
+def stack(*groups, spare=0):
     arrays = [array for group in groups for array in group]
-    spares = list(spare) + [0] * (len(groups) - len(spare))
+    outs = [((len(group), *group[0].shape), group[0].dtype) for group in groups]
+    if spare:
+        (count, rows, columns), dtype = outs[0]
+        outs.append(((count, rows + spare, columns), dtype))
     return call(
-        functools.partial(stack_kernel, [len(group) for group in groups]),
-        [
-            ((len(group), group[0].shape[0] + rows, *group[0].shape[1:]), group[0].dtype)
-            for group, rows in zip(groups, spares)
-        ],
+        functools.partial(stack_kernel, [len(group) for group in groups], bool(spare)),
+        outs,
         arrays,
         inside=pltpu.HBM,
         scratch=[pltpu.SemaphoreType.DMA((len(arrays),))],
@@ -126,27 +126,25 @@
     token_parts(whole, hidden, grad_gate, grad_up, parts)
 
 
-def last_kernel(turned, block, _, hidden_out, gate_out, up_out):
-    _, _, hidden, grad_gate, grad_up = block_grads(turned, [block])
-    hidden_out[...], gate_out[...], up_out[...] = hidden, grad_gate, grad_up
-
-
 def share_terms(pick, block, hidden, grad_gate, grad_up, before, outs):
     pairs, size = outs[0].shape[:2]
     for i, (side, right) in enumerate(((0, grad_gate), (0, grad_up), (1, hidden))):
         for pair in range(pairs):
             start = pl.multiple_of((2 * pair + pick) * size, 16)
-            term = contract(block[side, pl.ds(start, size), :], right[...], 1, 1)
+            term = contract(block[side, pl.ds(start, size), :], right, 1, 1)
             outs[i][pair] = (before[i, pl.ds(start, size), :] + term).astype(outs[i].dtype)
 
 
-def sent_kernel(block, hidden, grad_gate, grad_up, before, *outs):
+def last_kernel(turned, block, before, hidden_out, gate_out, up_out, *outs):
+    _, _, hidden, grad_gate, grad_up = block_grads(turned, [block])
+    hidden_out[...], gate_out[...], up_out[...] = hidden, grad_gate, grad_up
     share_terms(1 - lax.axis_index("fsdp") % 2, block, hidden, grad_gate, grad_up, before, outs)
 
 
 def kept_kernel(whole, block, hidden, grad_gate, grad_up, before, *outs):
-    share_terms(lax.axis_index("fsdp") % 2, block, hidden, grad_gate, grad_up, before, outs[:-1])
-    token_parts(whole, hidden[...], grad_gate[...], grad_up[...], outs[-1:])
+    values = hidden[...], grad_gate[...], grad_up[...]
+    share_terms(lax.axis_index("fsdp") % 2, block, *values, before, outs[:-1])
+    token_parts(whole, *values, outs[-1:])
 
 
 def pair_sums(count, refs):
@@ -213,8 +211,7 @@
 
     block, weight = {}, {}
     own_weights = [gate_weight, up_weight, down_weight.T]
-    own = [tokens.T, cotangent.T]
-    near, block[0] = stack(own, own, spare=[SPARE])
+    block[0], near = stack([tokens.T, cotangent.T], spare=SPARE)
     weight[0], *runs = stack(own_weights, own_weights[:2], own_weights[2:])
     straight = list(range(3, tensor, 2))
     for mask in straight + [1]:
@@ -252,9 +249,13 @@
     for mask in straight:
         part[mask], block[last] = lax.optimization_barrier((part[mask], block[last]))
         arrived[mask] = exchange(part[mask], "tensor", 1)
-    state = call(last_kernel, [((hidden_width, own_count), BF16)] * 3, [turned, block[last], sums])
     half_shape = (fsdp // 2, rows, hidden_width)
-    sent = call(sent_kernel, [(half_shape, BF16)] * 3, [block[last], *state, sums])
+    results = call(
+        last_kernel,
+        [((hidden_width, own_count), BF16)] * 3 + [(half_shape, BF16)] * 3,
+        [turned, block[last], sums],
+    )
+    state, sent = results[:3], results[3:]
     *kept, part[last] = call(
         kept_kernel, [(half_shape, F32)] * 3 + [(part_shape, F32)], [whole, block[last], *state, sums]
     )

time: 52.2 us -> 52.1 us (level)
    pallas_call x14 -> x13, Pallas kernels: 10 us -> 9.95 us  [call(): pl.pallas_call(body, out_shape=[kind(shape, dtype) for shape, dtype in ou...]
where the time goes in v5:
time: 52.1 us; the launch traced here: 51.9 us
  waiting for transfers between devices  25.4 us (49%)
  starting transfers between devices  15.9 us (31%)
  Pallas kernels  9.95 us (19%)
  between operations  0.74 us (1%)
    ppermute x14, waiting for transfers between devices, exchange(): lax.ppermute(array, axis, [(i, i ^ mask) for i in range(lax.axis_size(axi...  19.9 us
    ppermute x14, starting transfers between devices, exchange(): lax.ppermute(array, axis, [(i, i ^ mask) for i in range(lax.axis_size(axi...  12.3 us
    pallas_call x13, Pallas kernels, call(): pl.pallas_call(body, out_shape=[kind(shape, dtype) for shape, dtype in ou...  9.95 us
    ppermute x3, waiting for transfers between devices, per_device(): landed.append(lax.ppermute(share, ('dp', 'fsdp'), perm))  5.48 us
    ppermute x3, starting transfers between devices, per_device(): landed.append(lax.ppermute(share, ('dp', 'fsdp'), perm))  3.55 us
  transfers between devices with their start and end apart: 17, of which 10 were waited for; matrix products, arithmetic and copies ran while one was open for 0% of the time, Pallas kernels for 16%

profile of v5, /device:TPU:0, one launch (start us, length us, event | category | flops | bytes accessed | tf_op | source)
XLA Modules:
  0.0 51.9 jit_solution(15257045567466154897)
XLA Ops:
  0.6 1.0 %shard_map.95 = (bf16[2,576,128]{2,1,0:T(8,128)(2,1)S(1)}, bf16[2,592,128]{2,1,0:T(8,128)(2,1)S(1)}) custom-call(bf16[576,128]{1,0:T(8,128)(2,1)} %bitcast.8, bf16[576,128]{1,0:T(8,128)(2,1)} %bitcast.9), custom_call_target="tpu_custom_call" | custom-call | flops 1 | bytes 1 | tf_op jit(solution)/shard_map/pallas_call | solution.py:26
  1.7 3.1 %collective-permute-start.5 = (bf16[2,592,128]{2,1,0:T(8,128)(2,1)S(1)}, bf16[2,592,128]{2,1,0:T(8,128)(2,1)S(1)}, u32[]{:S(2)}, u32[]{:S(2)}) collective-permute-start(bf16[2,592,128]{2,1,0:T(8,128)(2,1)S(1)} %get-tuple-element.52), channel_id=1, source_target_pairs={{0,1},{1,0},{2,3},{3,2},{4,5},{5,4},{6,7},{7,6},{8,9},{9,8},{10,11... | collective-permute-start | bytes 909320 | tf_op jit(solution)/shard_map/ppermute | solution.py:20
  4.7 2.5 %collective-permute-start.4 = (bf16[2,576,128]{2,1,0:T(8,128)(2,1)S(1)}, bf16[2,576,128]{2,1,0:T(8,128)(2,1)S(1)}, u32[]{:S(2)}, u32[]{:S(2)}) collective-permute-start(bf16[2,576,128]{2,1,0:T(8,128)(2,1)S(1)} %get-tuple-element.51.refs_0_), channel_id=1, source_target_pairs={{0,3},{1,2},{2,1},{3,0},{4,7},{5,6},{6,5},{7,4},{8,11},{9,10},{10,... | collective-permute-start | bytes 884744 | tf_op jit(solution)/shard_map/ppermute | solution.py:20
  7.2 1.2 %shard_map.92 = (bf16[3,144,384]{2,1,0:T(8,128)(2,1)S(1)}, bf16[2,144,384]{2,1,0:T(8,128)(2,1)S(1)}, bf16[1,144,384]{2,1,0:T(8,128)(2,1)S(1)}) custom-call(bf16[144,384]{1,0:T(8,128)(2,1)} %refs_3_.1, bf16[144,384]{1,0:T(8,128)(2,1)} %refs_4_.1, bf16[144,384]{1,0:T(8,128)(2,1)} %bitcast.6, bf16[144,384]{1,0:T(8,128)(2,1)} %refs_3_.1, ...), custom_call_target="tpu_custom_call" | custom-call | flops 1 | bytes 1 | tf_op jit(solution)/shard_map/pallas_call | solution.py:26
  8.4 1.6 %collective-permute-start.1 = (bf16[2,144,384]{2,1,0:T(8,128)(2,1)S(1)}, bf16[2,144,384]{2,1,0:T(8,128)(2,1)S(1)}, u32[]{:S(2)}, u32[]{:S(2)}) collective-permute-start(bf16[2,144,384]{2,1,0:T(8,128)(2,1)S(1)} %get-tuple-element.47), channel_id=1, source_target_pairs={{0,8},{4,12},{8,0},{12,4},{1,9},{5,13},{9,1},{13,5},{2,10},{6,14},... | collective-permute-start | bytes 663560 | tf_op jit(solution)/shard_map/ppermute | solution.py:20
  10.5 6.9 %collective-permute-done.2.refs_1_ = bf16[1,144,384]{2,1,0:T(8,128)(2,1)S(1)} collective-permute-done((bf16[1,144,384]{2,1,0:T(8,128)(2,1)S(1)}, bf16[1,144,384]{2,1,0:T(8,128)(2,1)S(1)}, u32[]{:S(2)}, u32[]{:S(2)}) %collective-permute-start.2) | collective-permute-done | bytes 110624 | tf_op jit(solution)/shard_map/ppermute | solution.py:20
  17.6 2.8 %collective-permute-done.4.refs_0_ = bf16[2,576,128]{2,1,0:T(8,128)(2,1)S(1)} collective-permute-done((bf16[2,576,128]{2,1,0:T(8,128)(2,1)S(1)}, bf16[2,576,128]{2,1,0:T(8,128)(2,1)S(1)}, u32[]{:S(2)}, u32[]{:S(2)}) %collective-permute-start.4) | collective-permute-done | bytes 294944 | tf_op jit(solution)/shard_map/ppermute | solution.py:20
  20.5 0.6 %shard_map.94 = (bf16[3,576,384]{2,1,0:T(8,128)(2,1)S(1)}, bf16[3,384,576]{2,1,0:T(8,128)(2,1)S(1)}) custom-call(bf16[3,144,384]{2,1,0:T(8,128)(2,1)S(1)} %get-tuple-element.46.refs_0_, bf16[3,144,384]{2,1,0:T(8,128)(2,1)S(1)} %collective-permute-done.refs_1_, bf16[3,144,384]{2,1,0:T(8,128)(2,1)S(1)} %shard_map.93.refs_2_, ...), custom_call_target="tpu_custom_call" | custom-call | flops 1 | bytes 1 | tf_op jit(solution)/shard_map/pallas_call | solution.py:26
  21.0 2.0 %shard_map.96 = (f32[3,576,384]{2,1,0:T(8,128)S(1)}, f32[2,576,128]{2,1,0:T(8,128)S(1)}, bf16[2,576,128]{2,1,0:T(8,128)(2,1)S(1)}) custom-call(bf16[3,576,384]{2,1,0:T(8,128)(2,1)S(1)} %get-tuple-element.49.whole, bf16[3,384,576]{2,1,0:T(8,128)(2,1)S(1)} %get-tuple-element.50.turned, bf16[2,576,128]{2,1,0:T(8,128)(2,1)S(1)} %get-tuple-element.51.refs_0_, ...), custom_call_target="tpu_custom_call" | custom-call | flops 1 | bytes 1 | tf_op jit(solution)/shard_map/pallas_call | solution.py:26
  23.1 1.5 %shard_map.97 = (f32[3,576,384]{2,1,0:T(8,128)S(1)}, bf16[2,576,128]{2,1,0:T(8,128)(2,1)S(1)}) custom-call(bf16[3,576,384]{2,1,0:T(8,128)(2,1)S(1)} %get-tuple-element.49.whole, bf16[3,384,576]{2,1,0:T(8,128)(2,1)S(1)} %get-tuple-element.50.turned, bf16[2,576,128]{2,1,0:T(8,128)(2,1)S(1)} %collective-permute-done.4.refs_0_, ...), custom_call_target="tpu_custom_call" | custom-call | flops 1 | bytes 1 | tf_op jit(solution)/shard_map/pallas_call | solution.py:26
  24.5 3.8 %collective-permute-done.6.block = bf16[2,576,128]{2,1,0:T(8,128)(2,1)S(1)} collective-permute-done((bf16[2,576,128]{2,1,0:T(8,128)(2,1)S(1)}, bf16[2,576,128]{2,1,0:T(8,128)(2,1)S(1)}, u32[]{:S(2)}, u32[]{:S(2)}) %collective-permute-start.6) | collective-permute-done | bytes 294944 | tf_op jit(solution)/shard_map/ppermute | solution.py:20
  28.6 1.0 %shard_map.98 = (bf16[384,128]{1,0:T(8,128)(2,1)S(1)}, bf16[384,128]{1,0:T(8,128)(2,1)S(1)}, bf16[384,128]{1,0:T(8,128)(2,1)S(1)}, bf16[2,144,384]{2,1,0:T(8,128...) custom-call(bf16[3,384,576]{2,1,0:T(8,128)(2,1)S(1)} %get-tuple-element.50.turned, ...), custom_call_target="tpu_custom_call" | custom-call | flops 1 | bytes 1 | tf_op jit(solution)/shard_map/pallas_call | solution.py:26
  30.3 0.7 %shard_map.99 = (f32[2,144,384]{2,1,0:T(8,128)S(1)}, f32[2,144,384]{2,1,0:T(8,128)S(1)}, f32[2,144,384]{2,1,0:T(8,128)S(1)}, f32[2,576,128]{2,1,0:T(8,128)S(1)}) custom-call(bf16[3,576,384]{2,1,0:T(8,128)(2,1)S(1)} %get-tuple-element.49.whole, bf16[2,576,128]{2,1,0:T(8,128)(2,1)S(1)} %collective-permute-done.6.block, ...), custom_call_target="tpu_custom_call" | custom-call | flops 1 | bytes 1 | tf_op jit(solution)/shard_map/pallas_call | solution.py:26
  32.0 1.6 %collective-permute-start.10 = (bf16[224,384]{1,0:T(8,128)(2,1)S(1)}, bf16[224,384]{1,0:T(8,128)(2,1)S(1)}, u32[]{:S(2)}, u32[]{:S(2)}) collective-permute-start(bf16[224,384]{1,0:T(8,128)(2,1)S(1)} %get-tuple-element.70), channel_id=1, source_target_pairs={{0,16},{4,20},{8,24},{12,28},{16,0},{20,4},{24,8},{28,12},{1,17},{... | collective-permute-start | bytes 516104 | tf_op jit(solution)/shard_map/ppermute | solution.py:279
  33.6 1.5 %collective-permute-start.11 = (bf16[224,384]{1,0:T(8,128)(2,1)S(1)}, bf16[224,384]{1,0:T(8,128)(2,1)S(1)}, u32[]{:S(2)}, u32[]{:S(2)}) collective-permute-start(bf16[224,384]{1,0:T(8,128)(2,1)S(1)} %get-tuple-element.71), channel_id=1, source_target_pairs={{0,8},{4,12},{8,0},{12,4},{16,24},{20,28},{24,16},{28,20},{1,9},{5... | collective-permute-start | bytes 516104 | tf_op jit(solution)/shard_map/ppermute | solution.py:279
  35.6 1.7 %collective-permute-start.15 = (bf16[2,576,128]{2,1,0:T(8,128)(2,1)S(1)}, bf16[2,576,128]{2,1,0:T(8,128)(2,1)S(1)}, u32[]{:S(2)}, u32[]{:S(2)}) collective-permute-start(bf16[2,576,128]{2,1,0:T(8,128)(2,1)S(1)} %shard_map.103), channel_id=1, source_target_pairs={{0,2},{1,3},{2,0},{3,1},{4,6},{5,7},{6,4},{7,5},{8,10},{9,11},{10,... | collective-permute-start | bytes 884744 | tf_op jit(solution)/shard_map/ppermute | solution.py:20
  37.4 0.6 %collective-permute-start.16 = (bf16[2,576,128]{2,1,0:T(8,128)(2,1)S(1)}, bf16[2,576,128]{2,1,0:T(8,128)(2,1)S(1)}, u32[]{:S(2)}, u32[]{:S(2)}) collective-permute-start(bf16[2,576,128]{2,1,0:T(8,128)(2,1)S(1)} %get-tuple-element.81), channel_id=1, source_target_pairs={{0,1},{1,0},{2,3},{3,2},{4,5},{5,4},{6,7},{7,6},{8,9},{9,8},{10,11... | collective-permute-start | bytes 884744 | tf_op jit(solution)/shard_map/ppermute | solution.py:20
  38.0 1.3 %collective-permute-done.10.refs_1_ = bf16[224,384]{1,0:T(8,128)(2,1)S(1)} collective-permute-done((bf16[224,384]{1,0:T(8,128)(2,1)S(1)}, bf16[224,384]{1,0:T(8,128)(2,1)S(1)}, u32[]{:S(2)}, u32[]{:S(2)}) %collective-permute-start.10) | collective-permute-done | bytes 172064 | tf_op jit(solution)/shard_map/ppermute | solution.py:279
  39.3 4.2 %collective-permute-done.11.refs_2_ = bf16[224,384]{1,0:T(8,128)(2,1)S(1)} collective-permute-done((bf16[224,384]{1,0:T(8,128)(2,1)S(1)}, bf16[224,384]{1,0:T(8,128)(2,1)S(1)}, u32[]{:S(2)}, u32[]{:S(2)}) %collective-permute-start.11) | collective-permute-done | bytes 172064 | tf_op jit(solution)/shard_map/ppermute | solution.py:279
  43.5 1.3 %collective-permute-start.13 = (bf16[224,384]{1,0:T(8,128)(2,1)S(1)}, bf16[224,384]{1,0:T(8,128)(2,1)S(1)}, u32[]{:S(2)}, u32[]{:S(2)}) collective-permute-start(bf16[224,384]{1,0:T(8,128)(2,1)S(1)} %shard_map.101.mine), channel_id=1, source_target_pairs={{0,16},{16,0},{1,17},{17,1},{2,18},{18,2},{3,19},{19,3},{4,20},{20... | collective-permute-start | bytes 516104 | tf_op jit(solution)/shard_map/ppermute | solution.py:20
  44.8 4.2 %collective-permute-done.13.other = bf16[224,384]{1,0:T(8,128)(2,1)S(1)} collective-permute-done((bf16[224,384]{1,0:T(8,128)(2,1)S(1)}, bf16[224,384]{1,0:T(8,128)(2,1)S(1)}, u32[]{:S(2)}, u32[]{:S(2)}) %collective-permute-start.13) | collective-permute-done | bytes 172064 | tf_op jit(solution)/shard_map/ppermute | solution.py:20
  49.0 0.8 %shard_map.102 = (bf16[144,384]{1,0:T(8,128)(2,1)}, bf16[144,384]{1,0:T(8,128)(2,1)}, bf16[144,384]{1,0:T(8,128)(2,1)}) custom-call(bf16[224,384]{1,0:T(8,128)(2,1)S(1)} %shard_map.101.mine, bf16[224,384]{1,0:T(8,128)(2,1)S(1)} %collective-permute-done.13.other), custom_call_target="tpu_custom_call" | custom-call | flops 1 | bytes 1 | tf_op jit(solution)/shard_map/pallas_call | solution.py:26
  49.8 1.4 %collective-permute-done.15.refs_0_ = bf16[2,576,128]{2,1,0:T(8,128)(2,1)S(1)} collective-permute-done((bf16[2,576,128]{2,1,0:T(8,128)(2,1)S(1)}, bf16[2,576,128]{2,1,0:T(8,128)(2,1)S(1)}, u32[]{:S(2)}, u32[]{:S(2)}) %collective-permute-start.15) | collective-permute-done | bytes 294944 | tf_op jit(solution)/shard_map/ppermute | solution.py:20
  51.2 0.8 %shard_map.104 = (bf16[576,128]{1,0:T(8,128)(2,1)}, bf16[576,128]{1,0:T(8,128)(2,1)}) custom-call(f32[2,576,128]{2,1,0:T(8,128)S(1)} %get-tuple-element.76.own, bf16[2,576,128]{2,1,0:T(8,128)(2,1)S(1)} %collective-permute-done.15.refs_0_, bf16[2,576,128]{2,1,0:T(8,128)(2,1)S(1)} %collective-permute-done.16.refs_1_), custom_call_target="tpu_custom_call" | custom-call | flops 1 | bytes 1 | tf_op jit(solution)/shard_map/pallas_call | solution.py:26
  (23 shorter events, 3.2 us)
Async XLA Ops:
  1.7 18.8 %collective-permute-start.5 = (bf16[2,592,128]{2,1,0:T(8,128)(2,1)S(1)}, bf16[2,592,128]{2,1,0:T(8,128)(2,1)S(1)}, u32[]{:S(2)}, u32[]{:S(2)}) collective-permute-start(bf16[2,592,128]{2,1,0:T(8,128)(2,1)S(1)} %get-tuple-element.52), channel_id=1, source_target_pairs={{0,1},{1,0},{2,3},{3,2},{4,5},{5,4},{6,7},{7,6},{8,9},{9,8},{10,11... | collective-permute-start | bytes 909320 | tf_op jit(solution)/shard_map/ppermute | solution.py:20
  4.7 15.7 %collective-permute-start.4 = (bf16[2,576,128]{2,1,0:T(8,128)(2,1)S(1)}, bf16[2,576,128]{2,1,0:T(8,128)(2,1)S(1)}, u32[]{:S(2)}, u32[]{:S(2)}) collective-permute-start(bf16[2,576,128]{2,1,0:T(8,128)(2,1)S(1)} %get-tuple-element.51.refs_0_), channel_id=1, source_target_pairs={{0,3},{1,2},{2,1},{3,0},{4,7},{5,6},{6,5},{7,4},{8,11},{9,10},{10,... | collective-permute-start | bytes 884744 | tf_op jit(solution)/shard_map/ppermute | solution.py:20
  8.4 9.0 %collective-permute-start.1 = (bf16[2,144,384]{2,1,0:T(8,128)(2,1)S(1)}, bf16[2,144,384]{2,1,0:T(8,128)(2,1)S(1)}, u32[]{:S(2)}, u32[]{:S(2)}) collective-permute-start(bf16[2,144,384]{2,1,0:T(8,128)(2,1)S(1)} %get-tuple-element.47), channel_id=1, source_target_pairs={{0,8},{4,12},{8,0},{12,4},{1,9},{5,13},{9,1},{13,5},{2,10},{6,14},... | collective-permute-start | bytes 663560 | tf_op jit(solution)/shard_map/ppermute | solution.py:20
  10.0 7.5 %collective-permute-start.2 = (bf16[1,144,384]{2,1,0:T(8,128)(2,1)S(1)}, bf16[1,144,384]{2,1,0:T(8,128)(2,1)S(1)}, u32[]{:S(2)}, u32[]{:S(2)}) collective-permute-start(bf16[1,144,384]{2,1,0:T(8,128)(2,1)S(1)} %get-tuple-element.48), channel_id=1, source_target_pairs={{0,8},{4,12},{8,0},{12,4},{1,9},{5,13},{9,1},{13,5},{2,10},{6,14},... | collective-permute-start | bytes 331784 | tf_op jit(solution)/shard_map/ppermute | solution.py:20
  10.5 9.9 %collective-permute-start = (bf16[3,144,384]{2,1,0:T(8,128)(2,1)S(1)}, bf16[3,144,384]{2,1,0:T(8,128)(2,1)S(1)}, u32[]{:S(2)}, u32[]{:S(2)}) collective-permute-start(bf16[3,144,384]{2,1,0:T(8,128)(2,1)S(1)} %get-tuple-element.46.refs_0_), channel_id=1, source_target_pairs={{0,4},{4,0},{8,12},{12,8},{1,5},{5,1},{9,13},{13,9},{2,6},{6,2},{1... | collective-permute-start | bytes 995336 | tf_op jit(solution)/shard_map/ppermute | solution.py:20
  17.5 2.9 %collective-permute-start.3 = (bf16[3,144,384]{2,1,0:T(8,128)(2,1)S(1)}, bf16[3,144,384]{2,1,0:T(8,128)(2,1)S(1)}, u32[]{:S(2)}, u32[]{:S(2)}) collective-permute-start(bf16[3,144,384]{2,1,0:T(8,128)(2,1)S(1)} %shard_map.93.refs_2_), channel_id=1, source_target_pairs={{0,4},{4,0},{8,12},{12,8},{1,5},{5,1},{9,13},{13,9},{2,6},{6,2},{1... | collective-permute-start | bytes 995336 | tf_op jit(solution)/shard_map/ppermute | solution.py:20
  20.4 7.9 %collective-permute-start.6 = (bf16[2,576,128]{2,1,0:T(8,128)(2,1)S(1)}, bf16[2,576,128]{2,1,0:T(8,128)(2,1)S(1)}, u32[]{:S(2)}, u32[]{:S(2)}) collective-permute-start(bf16[2,576,128]{2,1,0:T(8,128)(2,1)S(1)} %collective-permute-done.4.refs_0_), channel_id=1, source_target_pairs={{0,1},{1,0},{2,3},{3,2},{4,5},{5,4},{6,7},{7,6},{8,9},{9,8},{10,11... | collective-permute-start | bytes 884744 | tf_op jit(solution)/shard_map/ppermute | solution.py:20
  28.3 7.2 %collective-permute-start.14 = (bf16[2,576,128]{2,1,0:T(8,128)(2,1)S(1)}, bf16[2,576,128]{2,1,0:T(8,128)(2,1)S(1)}, u32[]{:S(2)}, u32[]{:S(2)}) collective-permute-start(bf16[2,576,128]{2,1,0:T(8,128)(2,1)S(1)} %get-tuple-element.79), channel_id=1, source_target_pairs={{0,1},{1,0},{2,3},{3,2},{4,5},{5,4},{6,7},{7,6},{8,9},{9,8},{10,11... | collective-permute-start | bytes 884744 | tf_op jit(solution)/shard_map/ppermute | solution.py:20
  29.6 1.5 %collective-permute-start.7 = (bf16[2,144,384]{2,1,0:T(8,128)(2,1)S(1)}, bf16[2,144,384]{2,1,0:T(8,128)(2,1)S(1)}, u32[]{:S(2)}, u32[]{:S(2)}) collective-permute-start(bf16[2,144,384]{2,1,0:T(8,128)(2,1)S(1)} %get-tuple-element.66), channel_id=1, source_target_pairs={{0,4},{4,0},{8,12},{12,8},{1,5},{5,1},{9,13},{13,9},{2,6},{6,2},{1... | collective-permute-start | bytes 663560 | tf_op jit(solution)/shard_map/ppermute | solution.py:20
  29.7 1.8 %collective-permute-start.8 = (bf16[2,144,384]{2,1,0:T(8,128)(2,1)S(1)}, bf16[2,144,384]{2,1,0:T(8,128)(2,1)S(1)}, u32[]{:S(2)}, u32[]{:S(2)}) collective-permute-start(bf16[2,144,384]{2,1,0:T(8,128)(2,1)S(1)} %get-tuple-element.67), channel_id=1, source_target_pairs={{0,4},{4,0},{8,12},{12,8},{1,5},{5,1},{9,13},{13,9},{2,6},{6,2},{1... | collective-permute-start | bytes 663560 | tf_op jit(solution)/shard_map/ppermute | solution.py:20
  30.2 1.6 %collective-permute-start.9 = (bf16[2,144,384]{2,1,0:T(8,128)(2,1)S(1)}, bf16[2,144,384]{2,1,0:T(8,128)(2,1)S(1)}, u32[]{:S(2)}, u32[]{:S(2)}) collective-permute-start(bf16[2,144,384]{2,1,0:T(8,128)(2,1)S(1)} %get-tuple-element.68), channel_id=1, source_target_pairs={{0,4},{4,0},{8,12},{12,8},{1,5},{5,1},{9,13},{13,9},{2,6},{6,2},{1... | collective-permute-start | bytes 663560 | tf_op jit(solution)/shard_map/ppermute | solution.py:20
  32.0 7.3 %collective-permute-start.10 = (bf16[224,384]{1,0:T(8,128)(2,1)S(1)}, bf16[224,384]{1,0:T(8,128)(2,1)S(1)}, u32[]{:S(2)}, u32[]{:S(2)}) collective-permute-start(bf16[224,384]{1,0:T(8,128)(2,1)S(1)} %get-tuple-element.70), channel_id=1, source_target_pairs={{0,16},{4,20},{8,24},{12,28},{16,0},{20,4},{24,8},{28,12},{1,17},{... | collective-permute-start | bytes 516104 | tf_op jit(solution)/shard_map/ppermute | solution.py:279
  33.6 9.9 %collective-permute-start.11 = (bf16[224,384]{1,0:T(8,128)(2,1)S(1)}, bf16[224,384]{1,0:T(8,128)(2,1)S(1)}, u32[]{:S(2)}, u32[]{:S(2)}) collective-permute-start(bf16[224,384]{1,0:T(8,128)(2,1)S(1)} %get-tuple-element.71), channel_id=1, source_target_pairs={{0,8},{4,12},{8,0},{12,4},{16,24},{20,28},{24,16},{28,20},{1,9},{5... | collective-permute-start | bytes 516104 | tf_op jit(solution)/shard_map/ppermute | solution.py:279
  35.1 8.4 %collective-permute-start.12 = (bf16[224,384]{1,0:T(8,128)(2,1)S(1)}, bf16[224,384]{1,0:T(8,128)(2,1)S(1)}, u32[]{:S(2)}, u32[]{:S(2)}) collective-permute-start(bf16[224,384]{1,0:T(8,128)(2,1)S(1)} %get-tuple-element.72), channel_id=1, source_target_pairs={{0,24},{4,28},{8,16},{12,20},{16,8},{20,12},{24,0},{28,4},{1,25},{... | collective-permute-start | bytes 516104 | tf_op jit(solution)/shard_map/ppermute | solution.py:279
  35.6 15.6 %collective-permute-start.15 = (bf16[2,576,128]{2,1,0:T(8,128)(2,1)S(1)}, bf16[2,576,128]{2,1,0:T(8,128)(2,1)S(1)}, u32[]{:S(2)}, u32[]{:S(2)}) collective-permute-start(bf16[2,576,128]{2,1,0:T(8,128)(2,1)S(1)} %shard_map.103), channel_id=1, source_target_pairs={{0,2},{1,3},{2,0},{3,1},{4,6},{5,7},{6,4},{7,5},{8,10},{9,11},{10,... | collective-permute-start | bytes 884744 | tf_op jit(solution)/shard_map/ppermute | solution.py:20
  37.4 13.8 %collective-permute-start.16 = (bf16[2,576,128]{2,1,0:T(8,128)(2,1)S(1)}, bf16[2,576,128]{2,1,0:T(8,128)(2,1)S(1)}, u32[]{:S(2)}, u32[]{:S(2)}) collective-permute-start(bf16[2,576,128]{2,1,0:T(8,128)(2,1)S(1)} %get-tuple-element.81), channel_id=1, source_target_pairs={{0,1},{1,0},{2,3},{3,2},{4,5},{5,4},{6,7},{7,6},{8,9},{9,8},{10,11... | collective-permute-start | bytes 884744 | tf_op jit(solution)/shard_map/ppermute | solution.py:20
  43.5 5.5 %collective-permute-start.13 = (bf16[224,384]{1,0:T(8,128)(2,1)S(1)}, bf16[224,384]{1,0:T(8,128)(2,1)S(1)}, u32[]{:S(2)}, u32[]{:S(2)}) collective-permute-start(bf16[224,384]{1,0:T(8,128)(2,1)S(1)} %shard_map.101.mine), channel_id=1, source_target_pairs={{0,16},{16,0},{1,17},{17,1},{2,18},{18,2},{3,19},{19,3},{4,20},{20... | collective-permute-start | bytes 516104 | tf_op jit(solution)/shard_map/ppermute | solution.py:20

commit v6 on v5

--- a/solution.py
+++ b/solution.py
@@ -47,6 +47,18 @@
         refs[-2][:, :stacks[0].shape[1]] = stacks[0][...]
 
 
+def pieces_kernel(*refs):
+    arrays, (stacked, top, bottom, sems) = refs[:-4], refs[-4:]
+    copies = [pltpu.make_async_copy(array, stacked.at[i], sems.at[i]) for i, array in enumerate(arrays)]
+    for copy in copies:
+        copy.start()
+    for copy in copies:
+        copy.wait()
+    length = top.shape[1]
+    top[...] = stacked[:, :length]
+    bottom[...] = stacked[:, stacked.shape[1] - length:]
+
+
 def stack(*groups, spare=0):
     arrays = [array for group in groups for array in group]
     outs = [((len(group), *group[0].shape), group[0].dtype) for group in groups]
@@ -62,12 +74,10 @@
     )
 
 
-def join_kernel(*refs):
-    runs, joined = refs[:-1], refs[-1]
-    first = 0
-    for run in runs:
-        joined[first:first + run.shape[0]] = run[...]
-        first += run.shape[0]
+def join_kernel(top, bottom, joined):
+    length = top.shape[1]
+    joined[:, :length] = top[...]
+    joined[:, joined.shape[1] - length:] = bottom[...]
 
 
 def assemble_kernel(masks, *refs):
@@ -90,14 +100,10 @@
     return (swished * up_sum).astype(BF16), swished, slopes
 
 
-def block_grads(turned, blocks):
-    width = turned.shape[2]
-    rows, columns = (jnp.concatenate([block[side, :width] for block in blocks], axis=1) for side in range(2))
+def block_grads(turned, rows, columns):
     hidden, swished, slopes = forward(turned, rows)
     grad_hidden = contract(turned[2], columns, 1, 0)
-    grad_gate = (grad_hidden * slopes).astype(BF16)
-    grad_up = (grad_hidden * swished).astype(BF16)
-    return rows, columns, hidden, grad_gate, grad_up
+    return hidden, (grad_hidden * slopes).astype(BF16), (grad_hidden * swished).astype(BF16)
 
 
 def token_parts(whole, hidden, grad_gate, grad_up, parts):
@@ -119,31 +125,33 @@
 def group_kernel(count, first, whole, turned, *refs):
     blocks, refs = refs[:count], refs[count:]
     before, (after, *parts) = (None, refs) if first else (refs[0], refs[1:])
-    rows, columns, hidden, grad_gate, grad_up = block_grads(turned, blocks)
+    width = turned.shape[2]
+    rows, columns = (jnp.concatenate([block[side, :width] for block in blocks], axis=1) for side in range(2))
+    hidden, grad_gate, grad_up = block_grads(turned, rows, columns)
     for i, (left, right) in enumerate(weight_terms(rows, columns, hidden, grad_gate, grad_up)):
         term = contract(left, right, 1, 1)
         after[i] = term if first else before[i] + term
     token_parts(whole, hidden, grad_gate, grad_up, parts)
 
 
-def share_terms(pick, block, hidden, grad_gate, grad_up, before, outs):
+def share_terms(pick, tokens, cotangent, hidden, grad_gate, grad_up, before, outs):
     pairs, size = outs[0].shape[:2]
-    for i, (side, right) in enumerate(((0, grad_gate), (0, grad_up), (1, hidden))):
+    for i, (left, right) in enumerate(((tokens, grad_gate), (tokens, grad_up), (cotangent, hidden))):
         for pair in range(pairs):
             start = pl.multiple_of((2 * pair + pick) * size, 16)
-            term = contract(block[side, pl.ds(start, size), :], right, 1, 1)
+            term = contract(left[pl.ds(start, size), :], right, 1, 1)
             outs[i][pair] = (before[i, pl.ds(start, size), :] + term).astype(outs[i].dtype)
 
 
-def last_kernel(turned, block, before, hidden_out, gate_out, up_out, *outs):
-    _, _, hidden, grad_gate, grad_up = block_grads(turned, [block])
+def last_kernel(turned, tokens, cotangent, before, hidden_out, gate_out, up_out, *outs):
+    hidden, grad_gate, grad_up = block_grads(turned, tokens[...], cotangent[...])
     hidden_out[...], gate_out[...], up_out[...] = hidden, grad_gate, grad_up
-    share_terms(1 - lax.axis_index("fsdp") % 2, block, hidden, grad_gate, grad_up, before, outs)
-
-
-def kept_kernel(whole, block, hidden, grad_gate, grad_up, before, *outs):
+    share_terms(1 - lax.axis_index("fsdp") % 2, tokens, cotangent, hidden, grad_gate, grad_up, before, outs)
+
+
+def kept_kernel(whole, tokens, cotangent, hidden, grad_gate, grad_up, before, *outs):
     values = hidden[...], grad_gate[...], grad_up[...]
-    share_terms(lax.axis_index("fsdp") % 2, block, *values, before, outs[:-1])
+    share_terms(lax.axis_index("fsdp") % 2, tokens, cotangent, *values, before, outs[:-1])
     token_parts(whole, *values, outs[-1:])
 
 
@@ -212,20 +220,30 @@
     block, weight = {}, {}
     own_weights = [gate_weight, up_weight, down_weight.T]
     block[0], near = stack([tokens.T, cotangent.T], spare=SPARE)
-    weight[0], *runs = stack(own_weights, own_weights[:2], own_weights[2:])
+    piece = (rows // 2 + 15) // 16 * 16
+    weight[0], *runs = call(
+        pieces_kernel,
+        [((3, length, hidden_width), BF16) for length in (rows, piece, piece)],
+        own_weights,
+        inside=pltpu.HBM,
+        scratch=[pltpu.SemaphoreType.DMA((3,))],
+    )
     straight = list(range(3, tensor, 2))
     for mask in straight + [1]:
         block[mask] = exchange(near if mask == 1 else block[0], "tensor", mask)
     for mask in straight:
         block[mask], block[1] = lax.optimization_barrier((block[mask], block[1]))
-        block[mask ^ 1] = exchange(block[mask], "tensor", 1)
+        if mask != straight[-1]:
+            block[mask ^ 1] = exchange(block[mask], "tensor", 1)
+    final = [exchange(block[straight[-1]][side], "tensor", 1) for side in range(2)]
     masks = list(range(fsdp))
     weight[1] = exchange(weight[0], "fsdp", 1)
     for mask in masks[2::2]:
-        weight[mask], = call(
-            join_kernel, [(weight[0].shape, BF16)], [exchange(run, "fsdp", mask) for run in runs]
-        )
-        weight[mask + 1] = exchange(weight[mask], "fsdp", 1)
+        landed = [exchange(run, "fsdp", mask) for run in runs]
+        weight[mask], = call(join_kernel, [(weight[0].shape, BF16)], landed)
+        weight[mask + 1], = call(
+            join_kernel, [(weight[0].shape, BF16)], [exchange(run, "fsdp", 1) for run in landed]
+        )
     whole, turned = call(
         functools.partial(assemble_kernel, masks),
         [((3, width, hidden_width), BF16), ((3, hidden_width, width), BF16)],
@@ -247,17 +265,17 @@
         part.update(zip(group, parts))
     arrived = {}
     for mask in straight:
-        part[mask], block[last] = lax.optimization_barrier((part[mask], block[last]))
+        part[mask], final = lax.optimization_barrier((part[mask], final))
         arrived[mask] = exchange(part[mask], "tensor", 1)
     half_shape = (fsdp // 2, rows, hidden_width)
     results = call(
         last_kernel,
         [((hidden_width, own_count), BF16)] * 3 + [(half_shape, BF16)] * 3,
-        [turned, block[last], sums],
+        [turned, *final, sums],
     )
     state, sent = results[:3], results[3:]
     *kept, part[last] = call(
-        kept_kernel, [(half_shape, F32)] * 3 + [(part_shape, F32)], [whole, block[last], *state, sums]
+        kept_kernel, [(half_shape, F32)] * 3 + [(part_shape, F32)], [whole, *final, *state, sums]
     )
 
     received = [exchange(array, "fsdp", 1) for array in sent]

time: 52.1 us -> 52.2 us (level)
  starting transfers between devices: 15.9 us -> 17.9 us
  waiting for transfers between devices: 25.4 us -> 23.6 us
    ppermute x14 -> x16, starting transfers between devices: 12.3 us -> 14.3 us  [exchange(): lax.ppermute(array, axis, [(i, i ^ mask) for i in range(lax.axis_size(axi...]
    ppermute x14 -> x16, waiting for transfers between devices: 19.9 us -> 18.1 us  [exchange(): lax.ppermute(array, axis, [(i, i ^ mask) for i in range(lax.axis_size(axi...]
    pallas_call x13 -> x14, Pallas kernels: 9.95 us -> 9.85 us  [call(): pl.pallas_call(body, out_shape=[kind(shape, dtype) for shape, dtype in ou...]
  transfers between devices with their start and end apart: 17 -> 19, of which waited for: 10 -> 12; matrix products, arithmetic and copies ran while one was open for 0% -> 0% of each run, Pallas kernels for 16% -> 15%
where the time goes in v6:
time: 52.2 us; the launch traced here: 52.1 us
  waiting for transfers between devices  23.6 us (45%)
  starting transfers between devices  17.9 us (34%)
  Pallas kernels  9.85 us (19%)
  between operations  0.76 us (1%)
    ppermute x16, waiting for transfers between devices, exchange(): lax.ppermute(array, axis, [(i, i ^ mask) for i in range(lax.axis_size(axi...  18.1 us
    ppermute x16, starting transfers between devices, exchange(): lax.ppermute(array, axis, [(i, i ^ mask) for i in range(lax.axis_size(axi...  14.3 us
    pallas_call x14, Pallas kernels, call(): pl.pallas_call(body, out_shape=[kind(shape, dtype) for shape, dtype in ou...  9.85 us
    ppermute x3, waiting for transfers between devices, per_device(): landed.append(lax.ppermute(share, ('dp', 'fsdp'), perm))  5.48 us
    ppermute x3, starting transfers between devices, per_device(): landed.append(lax.ppermute(share, ('dp', 'fsdp'), perm))  3.55 us
  transfers between devices with their start and end apart: 19, of which 12 were waited for; matrix products, arithmetic and copies ran while one was open for 0% of the time, Pallas kernels for 15%

profile of v6, /device:TPU:0, one launch (start us, length us, event | category | flops | bytes accessed | tf_op | source)
XLA Modules:
  0.0 52.1 jit_solution(15843944516685945312)
XLA Ops:
  0.6 1.0 %shard_map.96 = (bf16[2,576,128]{2,1,0:T(8,128)(2,1)S(1)}, bf16[2,592,128]{2,1,0:T(8,128)(2,1)S(1)}) custom-call(bf16[576,128]{1,0:T(8,128)(2,1)} %bitcast.10, bf16[576,128]{1,0:T(8,128)(2,1)} %bitcast.11), custom_call_target="tpu_custom_call" | custom-call | flops 1 | bytes 1 | tf_op jit(solution)/shard_map/pallas_call | solution.py:26
  1.7 3.1 %collective-permute-start.6 = (bf16[2,592,128]{2,1,0:T(8,128)(2,1)S(1)}, bf16[2,592,128]{2,1,0:T(8,128)(2,1)S(1)}, u32[]{:S(2)}, u32[]{:S(2)}) collective-permute-start(bf16[2,592,128]{2,1,0:T(8,128)(2,1)S(1)} %get-tuple-element.53), channel_id=1, source_target_pairs={{0,1},{1,0},{2,3},{3,2},{4,5},{5,4},{6,7},{7,6},{8,9},{9,8},{10,11... | collective-permute-start | bytes 909320 | tf_op jit(solution)/shard_map/ppermute | solution.py:20
  4.7 2.5 %collective-permute-start.5 = (bf16[2,576,128]{2,1,0:T(8,128)(2,1)S(1)}, bf16[2,576,128]{2,1,0:T(8,128)(2,1)S(1)}, u32[]{:S(2)}, u32[]{:S(2)}) collective-permute-start(bf16[2,576,128]{2,1,0:T(8,128)(2,1)S(1)} %get-tuple-element.52.refs_0_), channel_id=1, source_target_pairs={{0,3},{1,2},{2,1},{3,0},{4,7},{5,6},{6,5},{7,4},{8,11},{9,10},{10,... | collective-permute-start | bytes 884744 | tf_op jit(solution)/shard_map/ppermute | solution.py:20
  7.2 1.1 %shard_map.92 = (bf16[3,144,384]{2,1,0:T(8,128)(2,1)S(1)}, bf16[3,80,384]{2,1,0:T(8,128)(2,1)S(1)}, bf16[3,80,384]{2,1,0:T(8,128)(2,1)S(1)}) custom-call(bf16[144,384]{1,0:T(8,128)(2,1)} %refs_0_.1, bf16[144,384]{1,0:T(8,128)(2,1)} %refs_1_.1, bf16[144,384]{1,0:T(8,128)(2,1)} %bitcast.12), custom_call_target="tpu_custom_call" | custom-call | flops 1 | bytes 1 | tf_op jit(solution)/shard_map/pallas_call | solution.py:26
  8.3 1.6 %collective-permute-start.1 = (bf16[3,80,384]{2,1,0:T(8,128)(2,1)S(1)}, bf16[3,80,384]{2,1,0:T(8,128)(2,1)S(1)}, u32[]{:S(2)}, u32[]{:S(2)}) collective-permute-start(bf16[3,80,384]{2,1,0:T(8,128)(2,1)S(1)} %get-tuple-element.48), channel_id=1, source_target_pairs={{0,8},{4,12},{8,0},{12,4},{1,9},{5,13},{9,1},{13,5},{2,10},{6,14},... | collective-permute-start | bytes 552968 | tf_op jit(solution)/shard_map/ppermute | solution.py:20
  10.4 5.5 %collective-permute-done.1.top = bf16[3,80,384]{2,1,0:T(8,128)(2,1)S(1)} collective-permute-done((bf16[3,80,384]{2,1,0:T(8,128)(2,1)S(1)}, bf16[3,80,384]{2,1,0:T(8,128)(2,1)S(1)}, u32[]{:S(2)}, u32[]{:S(2)}) %collective-permute-start.1) | collective-permute-done | bytes 184352 | tf_op jit(solution)/shard_map/ppermute | solution.py:20
  15.9 2.2 %collective-permute-done.2.bottom = bf16[3,80,384]{2,1,0:T(8,128)(2,1)S(1)} collective-permute-done((bf16[3,80,384]{2,1,0:T(8,128)(2,1)S(1)}, bf16[3,80,384]{2,1,0:T(8,128)(2,1)S(1)}, u32[]{:S(2)}, u32[]{:S(2)}) %collective-permute-start.2) | collective-permute-done | bytes 184352 | tf_op jit(solution)/shard_map/ppermute | solution.py:20
  18.1 2.3 %collective-permute-done.5.refs_0_ = bf16[2,576,128]{2,1,0:T(8,128)(2,1)S(1)} collective-permute-done((bf16[2,576,128]{2,1,0:T(8,128)(2,1)S(1)}, bf16[2,576,128]{2,1,0:T(8,128)(2,1)S(1)}, u32[]{:S(2)}, u32[]{:S(2)}) %collective-permute-start.5) | collective-permute-done | bytes 294944 | tf_op jit(solution)/shard_map/ppermute | solution.py:20
  20.5 2.0 %collective-permute-start.8 = (bf16[576,128]{1,0:T(8,128)(2,1)S(1)}, bf16[576,128]{1,0:T(8,128)(2,1)S(1)}, u32[]{:S(2)}, u32[]{:S(2)}) collective-permute-start(bf16[576,128]{1,0:T(8,128)(2,1)S(1)} %get-tuple-element.89), channel_id=1, source_target_pairs={{0,1},{1,0},{2,3},{3,2},{4,5},{5,4},{6,7},{7,6},{8,9},{9,8},{10,11... | collective-permute-start | bytes 442376 | tf_op jit(solution)/shard_map/ppermute | solution.py:20
  23.2 2.0 %shard_map.97 = (f32[3,576,384]{2,1,0:T(8,128)S(1)}, f32[2,576,128]{2,1,0:T(8,128)S(1)}, bf16[2,576,128]{2,1,0:T(8,128)(2,1)S(1)}) custom-call(bf16[3,576,384]{2,1,0:T(8,128)(2,1)S(1)} %get-tuple-element.50.whole, bf16[3,384,576]{2,1,0:T(8,128)(2,1)S(1)} %get-tuple-element.51.turned, bf16[2,576,128]{2,1,0:T(8,128)(2,1)S(1)} %get-tuple-element.52.refs_0_, ...), custom_call_target="tpu_custom_call" | custom-call | flops 1 | bytes 1 | tf_op jit(solution)/shard_map/pallas_call | solution.py:26
  25.3 1.5 %shard_map.98 = (f32[3,576,384]{2,1,0:T(8,128)S(1)}, bf16[2,576,128]{2,1,0:T(8,128)(2,1)S(1)}) custom-call(bf16[3,576,384]{2,1,0:T(8,128)(2,1)S(1)} %get-tuple-element.50.whole, bf16[3,384,576]{2,1,0:T(8,128)(2,1)S(1)} %get-tuple-element.51.turned, bf16[2,576,128]{2,1,0:T(8,128)(2,1)S(1)} %collective-permute-done.5.refs_0_, ...), custom_call_target="tpu_custom_call" | custom-call | flops 1 | bytes 1 | tf_op jit(solution)/shard_map/pallas_call | solution.py:26
  26.8 1.6 %collective-permute-done.8.cotangent = bf16[576,128]{1,0:T(8,128)(2,1)S(1)} collective-permute-done((bf16[576,128]{1,0:T(8,128)(2,1)S(1)}, bf16[576,128]{1,0:T(8,128)(2,1)S(1)}, u32[]{:S(2)}, u32[]{:S(2)}) %collective-permute-start.8) | collective-permute-done | bytes 147488 | tf_op jit(solution)/shard_map/ppermute | solution.py:20
  28.7 1.0 %shard_map.99 = (bf16[384,128]{1,0:T(8,128)(2,1)S(1)}, bf16[384,128]{1,0:T(8,128)(2,1)S(1)}, bf16[384,128]{1,0:T(8,128)(2,1)S(1)}, bf16[2,144,384]{2,1,0:T(8,128...) custom-call(bf16[3,384,576]{2,1,0:T(8,128)(2,1)S(1)} %get-tuple-element.51.turned, ...), custom_call_target="tpu_custom_call" | custom-call | flops 1 | bytes 1 | tf_op jit(solution)/shard_map/pallas_call | solution.py:26
  30.3 0.7 %shard_map.100 = (f32[2,144,384]{2,1,0:T(8,128)S(1)}, f32[2,144,384]{2,1,0:T(8,128)S(1)}, f32[2,144,384]{2,1,0:T(8,128)S(1)}, f32[2,576,128]{2,1,0:T(8,128)S(1)}) custom-call(bf16[3,576,384]{2,1,0:T(8,128)(2,1)S(1)} %get-tuple-element.50.whole, bf16[576,128]{1,0:T(8,128)(2,1)S(1)} %collective-permute-done.7.tokens, ...), custom_call_target="tpu_custom_call" | custom-call | flops 1 | bytes 1 | tf_op jit(solution)/shard_map/pallas_call | solution.py:26
  32.1 1.6 %collective-permute-start.12 = (bf16[224,384]{1,0:T(8,128)(2,1)S(1)}, bf16[224,384]{1,0:T(8,128)(2,1)S(1)}, u32[]{:S(2)}, u32[]{:S(2)}) collective-permute-start(bf16[224,384]{1,0:T(8,128)(2,1)S(1)} %get-tuple-element.72), channel_id=1, source_target_pairs={{0,16},{4,20},{8,24},{12,28},{16,0},{20,4},{24,8},{28,12},{1,17},{... | collective-permute-start | bytes 516104 | tf_op jit(solution)/shard_map/ppermute | solution.py:297
  33.7 1.5 %collective-permute-start.13 = (bf16[224,384]{1,0:T(8,128)(2,1)S(1)}, bf16[224,384]{1,0:T(8,128)(2,1)S(1)}, u32[]{:S(2)}, u32[]{:S(2)}) collective-permute-start(bf16[224,384]{1,0:T(8,128)(2,1)S(1)} %get-tuple-element.73), channel_id=1, source_target_pairs={{0,8},{4,12},{8,0},{12,4},{16,24},{20,28},{24,16},{28,20},{1,9},{5... | collective-permute-start | bytes 516104 | tf_op jit(solution)/shard_map/ppermute | solution.py:297
  35.7 1.7 %collective-permute-start.17 = (bf16[2,576,128]{2,1,0:T(8,128)(2,1)S(1)}, bf16[2,576,128]{2,1,0:T(8,128)(2,1)S(1)}, u32[]{:S(2)}, u32[]{:S(2)}) collective-permute-start(bf16[2,576,128]{2,1,0:T(8,128)(2,1)S(1)} %shard_map.104), channel_id=1, source_target_pairs={{0,2},{1,3},{2,0},{3,1},{4,6},{5,7},{6,4},{7,5},{8,10},{9,11},{10,... | collective-permute-start | bytes 884744 | tf_op jit(solution)/shard_map/ppermute | solution.py:20
  38.1 1.3 %collective-permute-done.12.refs_1_ = bf16[224,384]{1,0:T(8,128)(2,1)S(1)} collective-permute-done((bf16[224,384]{1,0:T(8,128)(2,1)S(1)}, bf16[224,384]{1,0:T(8,128)(2,1)S(1)}, u32[]{:S(2)}, u32[]{:S(2)}) %collective-permute-start.12) | collective-permute-done | bytes 172064 | tf_op jit(solution)/shard_map/ppermute | solution.py:297
  39.4 4.2 %collective-permute-done.13.refs_2_ = bf16[224,384]{1,0:T(8,128)(2,1)S(1)} collective-permute-done((bf16[224,384]{1,0:T(8,128)(2,1)S(1)}, bf16[224,384]{1,0:T(8,128)(2,1)S(1)}, u32[]{:S(2)}, u32[]{:S(2)}) %collective-permute-start.13) | collective-permute-done | bytes 172064 | tf_op jit(solution)/shard_map/ppermute | solution.py:297
  43.6 1.3 %collective-permute-start.15 = (bf16[224,384]{1,0:T(8,128)(2,1)S(1)}, bf16[224,384]{1,0:T(8,128)(2,1)S(1)}, u32[]{:S(2)}, u32[]{:S(2)}) collective-permute-start(bf16[224,384]{1,0:T(8,128)(2,1)S(1)} %shard_map.102.mine), channel_id=1, source_target_pairs={{0,16},{16,0},{1,17},{17,1},{2,18},{18,2},{3,19},{19,3},{4,20},{20... | collective-permute-start | bytes 516104 | tf_op jit(solution)/shard_map/ppermute | solution.py:20
  44.9 4.2 %collective-permute-done.15.other = bf16[224,384]{1,0:T(8,128)(2,1)S(1)} collective-permute-done((bf16[224,384]{1,0:T(8,128)(2,1)S(1)}, bf16[224,384]{1,0:T(8,128)(2,1)S(1)}, u32[]{:S(2)}, u32[]{:S(2)}) %collective-permute-start.15) | collective-permute-done | bytes 172064 | tf_op jit(solution)/shard_map/ppermute | solution.py:20
  49.1 0.8 %shard_map.103 = (bf16[144,384]{1,0:T(8,128)(2,1)}, bf16[144,384]{1,0:T(8,128)(2,1)}, bf16[144,384]{1,0:T(8,128)(2,1)}) custom-call(bf16[224,384]{1,0:T(8,128)(2,1)S(1)} %shard_map.102.mine, bf16[224,384]{1,0:T(8,128)(2,1)S(1)} %collective-permute-done.15.other), custom_call_target="tpu_custom_call" | custom-call | flops 1 | bytes 1 | tf_op jit(solution)/shard_map/pallas_call | solution.py:26
  49.9 1.4 %collective-permute-done.17.refs_0_ = bf16[2,576,128]{2,1,0:T(8,128)(2,1)S(1)} collective-permute-done((bf16[2,576,128]{2,1,0:T(8,128)(2,1)S(1)}, bf16[2,576,128]{2,1,0:T(8,128)(2,1)S(1)}, u32[]{:S(2)}, u32[]{:S(2)}) %collective-permute-start.17) | collective-permute-done | bytes 294944 | tf_op jit(solution)/shard_map/ppermute | solution.py:20
  51.3 0.8 %shard_map.105 = (bf16[576,128]{1,0:T(8,128)(2,1)}, bf16[576,128]{1,0:T(8,128)(2,1)}) custom-call(f32[2,576,128]{2,1,0:T(8,128)S(1)} %get-tuple-element.78.own, bf16[2,576,128]{2,1,0:T(8,128)(2,1)S(1)} %collective-permute-done.17.refs_0_, bf16[2,576,128]{2,1,0:T(8,128)(2,1)S(1)} %collective-permute-done.18.refs_1_), custom_call_target="tpu_custom_call" | custom-call | flops 1 | bytes 1 | tf_op jit(solution)/shard_map/pallas_call | solution.py:26
  (29 shorter events, 4.5 us)
Async XLA Ops:
  1.7 18.8 %collective-permute-start.6 = (bf16[2,592,128]{2,1,0:T(8,128)(2,1)S(1)}, bf16[2,592,128]{2,1,0:T(8,128)(2,1)S(1)}, u32[]{:S(2)}, u32[]{:S(2)}) collective-permute-start(bf16[2,592,128]{2,1,0:T(8,128)(2,1)S(1)} %get-tuple-element.53), channel_id=1, source_target_pairs={{0,1},{1,0},{2,3},{3,2},{4,5},{5,4},{6,7},{7,6},{8,9},{9,8},{10,11... | collective-permute-start | bytes 909320 | tf_op jit(solution)/shard_map/ppermute | solution.py:20
  4.7 15.7 %collective-permute-start.5 = (bf16[2,576,128]{2,1,0:T(8,128)(2,1)S(1)}, bf16[2,576,128]{2,1,0:T(8,128)(2,1)S(1)}, u32[]{:S(2)}, u32[]{:S(2)}) collective-permute-start(bf16[2,576,128]{2,1,0:T(8,128)(2,1)S(1)} %get-tuple-element.52.refs_0_), channel_id=1, source_target_pairs={{0,3},{1,2},{2,1},{3,0},{4,7},{5,6},{6,5},{7,4},{8,11},{9,10},{10,... | collective-permute-start | bytes 884744 | tf_op jit(solution)/shard_map/ppermute | solution.py:20
  8.3 7.6 %collective-permute-start.1 = (bf16[3,80,384]{2,1,0:T(8,128)(2,1)S(1)}, bf16[3,80,384]{2,1,0:T(8,128)(2,1)S(1)}, u32[]{:S(2)}, u32[]{:S(2)}) collective-permute-start(bf16[3,80,384]{2,1,0:T(8,128)(2,1)S(1)} %get-tuple-element.48), channel_id=1, source_target_pairs={{0,8},{4,12},{8,0},{12,4},{1,9},{5,13},{9,1},{13,5},{2,10},{6,14},... | collective-permute-start | bytes 552968 | tf_op jit(solution)/shard_map/ppermute | solution.py:20
  9.9 8.2 %collective-permute-start.2 = (bf16[3,80,384]{2,1,0:T(8,128)(2,1)S(1)}, bf16[3,80,384]{2,1,0:T(8,128)(2,1)S(1)}, u32[]{:S(2)}, u32[]{:S(2)}) collective-permute-start(bf16[3,80,384]{2,1,0:T(8,128)(2,1)S(1)} %get-tuple-element.49), channel_id=1, source_target_pairs={{0,8},{4,12},{8,0},{12,4},{1,9},{5,13},{9,1},{13,5},{2,10},{6,14},... | collective-permute-start | bytes 552968 | tf_op jit(solution)/shard_map/ppermute | solution.py:20
  10.4 12.3 %collective-permute-start = (bf16[3,144,384]{2,1,0:T(8,128)(2,1)S(1)}, bf16[3,144,384]{2,1,0:T(8,128)(2,1)S(1)}, u32[]{:S(2)}, u32[]{:S(2)}) collective-permute-start(bf16[3,144,384]{2,1,0:T(8,128)(2,1)S(1)} %get-tuple-element.47.refs_0_), channel_id=1, source_target_pairs={{0,4},{4,0},{8,12},{12,8},{1,5},{5,1},{9,13},{13,9},{2,6},{6,2},{1... | collective-permute-start | bytes 995336 | tf_op jit(solution)/shard_map/ppermute | solution.py:20
  15.9 6.7 %collective-permute-start.3 = (bf16[3,80,384]{2,1,0:T(8,128)(2,1)S(1)}, bf16[3,80,384]{2,1,0:T(8,128)(2,1)S(1)}, u32[]{:S(2)}, u32[]{:S(2)}) collective-permute-start(bf16[3,80,384]{2,1,0:T(8,128)(2,1)S(1)} %collective-permute-done.1.top), channel_id=1, source_target_pairs={{0,4},{4,0},{8,12},{12,8},{1,5},{5,1},{9,13},{13,9},{2,6},{6,2},{1... | collective-permute-start | bytes 552968 | tf_op jit(solution)/shard_map/ppermute | solution.py:20
  18.1 4.5 %collective-permute-start.4 = (bf16[3,80,384]{2,1,0:T(8,128)(2,1)S(1)}, bf16[3,80,384]{2,1,0:T(8,128)(2,1)S(1)}, u32[]{:S(2)}, u32[]{:S(2)}) collective-permute-start(bf16[3,80,384]{2,1,0:T(8,128)(2,1)S(1)} %collective-permute-done.2.bottom), channel_id=1, source_target_pairs={{0,4},{4,0},{8,12},{12,8},{1,5},{5,1},{9,13},{13,9},{2,6},{6,2},{1... | collective-permute-start | bytes 552968 | tf_op jit(solution)/shard_map/ppermute | solution.py:20
  20.5 6.4 %collective-permute-start.7 = (bf16[576,128]{1,0:T(8,128)(2,1)S(1)}, bf16[576,128]{1,0:T(8,128)(2,1)S(1)}, u32[]{:S(2)}, u32[]{:S(2)}) collective-permute-start(bf16[576,128]{1,0:T(8,128)(2,1)S(1)} %get-tuple-element.90), channel_id=1, source_target_pairs={{0,1},{1,0},{2,3},{3,2},{4,5},{5,4},{6,7},{7,6},{8,9},{9,8},{10,11... | collective-permute-start | bytes 442376 | tf_op jit(solution)/shard_map/ppermute | solution.py:20
  20.5 7.9 %collective-permute-start.8 = (bf16[576,128]{1,0:T(8,128)(2,1)S(1)}, bf16[576,128]{1,0:T(8,128)(2,1)S(1)}, u32[]{:S(2)}, u32[]{:S(2)}) collective-permute-start(bf16[576,128]{1,0:T(8,128)(2,1)S(1)} %get-tuple-element.89), channel_id=1, source_target_pairs={{0,1},{1,0},{2,3},{3,2},{4,5},{5,4},{6,7},{7,6},{8,9},{9,8},{10,11... | collective-permute-start | bytes 442376 | tf_op jit(solution)/shard_map/ppermute | solution.py:20
  28.4 7.2 %collective-permute-start.16 = (bf16[2,576,128]{2,1,0:T(8,128)(2,1)S(1)}, bf16[2,576,128]{2,1,0:T(8,128)(2,1)S(1)}, u32[]{:S(2)}, u32[]{:S(2)}) collective-permute-start(bf16[2,576,128]{2,1,0:T(8,128)(2,1)S(1)} %get-tuple-element.81), channel_id=1, source_target_pairs={{0,1},{1,0},{2,3},{3,2},{4,5},{5,4},{6,7},{7,6},{8,9},{9,8},{10,11... | collective-permute-start | bytes 884744 | tf_op jit(solution)/shard_map/ppermute | solution.py:20
  29.7 1.5 %collective-permute-start.10 = (bf16[2,144,384]{2,1,0:T(8,128)(2,1)S(1)}, bf16[2,144,384]{2,1,0:T(8,128)(2,1)S(1)}, u32[]{:S(2)}, u32[]{:S(2)}) collective-permute-start(bf16[2,144,384]{2,1,0:T(8,128)(2,1)S(1)} %get-tuple-element.69), channel_id=1, source_target_pairs={{0,4},{4,0},{8,12},{12,8},{1,5},{5,1},{9,13},{13,9},{2,6},{6,2},{1... | collective-permute-start | bytes 663560 | tf_op jit(solution)/shard_map/ppermute | solution.py:20
  29.8 1.8 %collective-permute-start.11 = (bf16[2,144,384]{2,1,0:T(8,128)(2,1)S(1)}, bf16[2,144,384]{2,1,0:T(8,128)(2,1)S(1)}, u32[]{:S(2)}, u32[]{:S(2)}) collective-permute-start(bf16[2,144,384]{2,1,0:T(8,128)(2,1)S(1)} %get-tuple-element.70), channel_id=1, source_target_pairs={{0,4},{4,0},{8,12},{12,8},{1,5},{5,1},{9,13},{13,9},{2,6},{6,2},{1... | collective-permute-start | bytes 663560 | tf_op jit(solution)/shard_map/ppermute | solution.py:20
  30.3 1.6 %collective-permute-start.9 = (bf16[2,144,384]{2,1,0:T(8,128)(2,1)S(1)}, bf16[2,144,384]{2,1,0:T(8,128)(2,1)S(1)}, u32[]{:S(2)}, u32[]{:S(2)}) collective-permute-start(bf16[2,144,384]{2,1,0:T(8,128)(2,1)S(1)} %get-tuple-element.68), channel_id=1, source_target_pairs={{0,4},{4,0},{8,12},{12,8},{1,5},{5,1},{9,13},{13,9},{2,6},{6,2},{1... | collective-permute-start | bytes 663560 | tf_op jit(solution)/shard_map/ppermute | solution.py:20
  32.1 7.3 %collective-permute-start.12 = (bf16[224,384]{1,0:T(8,128)(2,1)S(1)}, bf16[224,384]{1,0:T(8,128)(2,1)S(1)}, u32[]{:S(2)}, u32[]{:S(2)}) collective-permute-start(bf16[224,384]{1,0:T(8,128)(2,1)S(1)} %get-tuple-element.72), channel_id=1, source_target_pairs={{0,16},{4,20},{8,24},{12,28},{16,0},{20,4},{24,8},{28,12},{1,17},{... | collective-permute-start | bytes 516104 | tf_op jit(solution)/shard_map/ppermute | solution.py:297
  33.7 9.9 %collective-permute-start.13 = (bf16[224,384]{1,0:T(8,128)(2,1)S(1)}, bf16[224,384]{1,0:T(8,128)(2,1)S(1)}, u32[]{:S(2)}, u32[]{:S(2)}) collective-permute-start(bf16[224,384]{1,0:T(8,128)(2,1)S(1)} %get-tuple-element.73), channel_id=1, source_target_pairs={{0,8},{4,12},{8,0},{12,4},{16,24},{20,28},{24,16},{28,20},{1,9},{5... | collective-permute-start | bytes 516104 | tf_op jit(solution)/shard_map/ppermute | solution.py:297
  35.2 8.4 %collective-permute-start.14 = (bf16[224,384]{1,0:T(8,128)(2,1)S(1)}, bf16[224,384]{1,0:T(8,128)(2,1)S(1)}, u32[]{:S(2)}, u32[]{:S(2)}) collective-permute-start(bf16[224,384]{1,0:T(8,128)(2,1)S(1)} %get-tuple-element.74), channel_id=1, source_target_pairs={{0,24},{4,28},{8,16},{12,20},{16,8},{20,12},{24,0},{28,4},{1,25},{... | collective-permute-start | bytes 516104 | tf_op jit(solution)/shard_map/ppermute | solution.py:297
  35.7 15.6 %collective-permute-start.17 = (bf16[2,576,128]{2,1,0:T(8,128)(2,1)S(1)}, bf16[2,576,128]{2,1,0:T(8,128)(2,1)S(1)}, u32[]{:S(2)}, u32[]{:S(2)}) collective-permute-start(bf16[2,576,128]{2,1,0:T(8,128)(2,1)S(1)} %shard_map.104), channel_id=1, source_target_pairs={{0,2},{1,3},{2,0},{3,1},{4,6},{5,7},{6,4},{7,5},{8,10},{9,11},{10,... | collective-permute-start | bytes 884744 | tf_op jit(solution)/shard_map/ppermute | solution.py:20
  37.5 13.8 %collective-permute-start.18 = (bf16[2,576,128]{2,1,0:T(8,128)(2,1)S(1)}, bf16[2,576,128]{2,1,0:T(8,128)(2,1)S(1)}, u32[]{:S(2)}, u32[]{:S(2)}) collective-permute-start(bf16[2,576,128]{2,1,0:T(8,128)(2,1)S(1)} %get-tuple-element.83), channel_id=1, source_target_pairs={{0,1},{1,0},{2,3},{3,2},{4,5},{5,4},{6,7},{7,6},{8,9},{9,8},{10,11... | collective-permute-start | bytes 884744 | tf_op jit(solution)/shard_map/ppermute | solution.py:20
  43.6 5.5 %collective-permute-start.15 = (bf16[224,384]{1,0:T(8,128)(2,1)S(1)}, bf16[224,384]{1,0:T(8,128)(2,1)S(1)}, u32[]{:S(2)}, u32[]{:S(2)}) collective-permute-start(bf16[224,384]{1,0:T(8,128)(2,1)S(1)} %shard_map.102.mine), channel_id=1, source_target_pairs={{0,16},{16,0},{1,17},{17,1},{2,18},{18,2},{3,19},{19,3},{4,20},{20... | collective-permute-start | bytes 516104 | tf_op jit(solution)/shard_map/ppermute | solution.py:20

commit v7 on v5

--- a/solution.py
+++ b/solution.py
@@ -141,10 +141,13 @@
     share_terms(1 - lax.axis_index("fsdp") % 2, block, hidden, grad_gate, grad_up, before, outs)
 
 
-def kept_kernel(whole, block, hidden, grad_gate, grad_up, before, *outs):
-    values = hidden[...], grad_gate[...], grad_up[...]
-    share_terms(lax.axis_index("fsdp") % 2, block, *values, before, outs[:-1])
-    token_parts(whole, *values, outs[-1:])
+def kept_kernel(block, hidden, grad_gate, grad_up, before, *outs):
+    own = lax.axis_index("fsdp") % 2
+    share_terms(own, block, hidden[...], grad_gate[...], grad_up[...], before, outs)
+
+
+def last_parts_kernel(whole, hidden, grad_gate, grad_up, part):
+    token_parts(whole, hidden[...], grad_gate[...], grad_up[...], [part])
 
 
 def pair_sums(count, refs):
@@ -255,10 +258,8 @@
         [((hidden_width, own_count), BF16)] * 3 + [(half_shape, BF16)] * 3,
         [turned, block[last], sums],
     )
-    state, sent = results[:3], results[3:]
-    *kept, part[last] = call(
-        kept_kernel, [(half_shape, F32)] * 3 + [(part_shape, F32)], [whole, block[last], *state, sums]
-    )
+    state, sent = list(results[:3]), results[3:]
+    kept = call(kept_kernel, [(half_shape, F32)] * 3, [block[last], *state, sums])
 
     received = [exchange(array, "fsdp", 1) for array in sent]
     if dp == 2:
@@ -297,6 +298,8 @@
         grads = lax.psum(mine, "dp")
 
     back = []
+    state[0], ready = lax.optimization_barrier((state[0], ready))
+    part[last], = call(last_parts_kernel, [(part_shape, F32)], [whole, *state])
     for mask in straight:
         total, = call(middle_kernel, [(part_shape, BF16)], [part[mask ^ 1], arrived[mask], ready])
         part[1], total = lax.optimization_barrier((part[1], total))

time: 52.1 us -> 52.6 us (level)
    ppermute x14, waiting for transfers between devices: 19.9 us -> 20.8 us  [exchange(): lax.ppermute(array, axis, [(i, i ^ mask) for i in range(lax.axis_size(axi...]
    pallas_call x13 -> x14, Pallas kernels: 9.95 us -> 10.1 us  [call(): pl.pallas_call(body, out_shape=[kind(shape, dtype) for shape, dtype in ou...]
where the time goes in v7:
time: 52.6 us; the launch traced here: 52.5 us
  waiting for transfers between devices  25.8 us (49%)
  starting transfers between devices  15.8 us (30%)
  Pallas kernels  10.1 us (19%)
  between operations  0.75 us (1%)
    ppermute x14, waiting for transfers between devices, exchange(): lax.ppermute(array, axis, [(i, i ^ mask) for i in range(lax.axis_size(axi...  20.8 us
    ppermute x14, starting transfers between devices, exchange(): lax.ppermute(array, axis, [(i, i ^ mask) for i in range(lax.axis_size(axi...  12.3 us
    pallas_call x14, Pallas kernels, call(): pl.pallas_call(body, out_shape=[kind(shape, dtype) for shape, dtype in ou...  10.1 us
    ppermute x3, waiting for transfers between devices, per_device(): landed.append(lax.ppermute(share, ('dp', 'fsdp'), perm))  4.96 us
    ppermute x3, starting transfers between devices, per_device(): landed.append(lax.ppermute(share, ('dp', 'fsdp'), perm))  3.55 us
  transfers between devices with their start and end apart: 17, of which 10 were waited for; matrix products, arithmetic and copies ran while one was open for 0% of the time, Pallas kernels for 16%

profile of v7, /device:TPU:0, one launch (start us, length us, event | category | flops | bytes accessed | tf_op | source)
XLA Modules:
  0.0 52.5 jit_solution(6162097317702966988)
XLA Ops:
  0.6 1.0 %shard_map.95 = (bf16[2,576,128]{2,1,0:T(8,128)(2,1)S(1)}, bf16[2,592,128]{2,1,0:T(8,128)(2,1)S(1)}) custom-call(bf16[576,128]{1,0:T(8,128)(2,1)} %bitcast.8, bf16[576,128]{1,0:T(8,128)(2,1)} %bitcast.9), custom_call_target="tpu_custom_call" | custom-call | flops 1 | bytes 1 | tf_op jit(solution)/shard_map/pallas_call | solution.py:26
  1.7 3.1 %collective-permute-start.5 = (bf16[2,592,128]{2,1,0:T(8,128)(2,1)S(1)}, bf16[2,592,128]{2,1,0:T(8,128)(2,1)S(1)}, u32[]{:S(2)}, u32[]{:S(2)}) collective-permute-start(bf16[2,592,128]{2,1,0:T(8,128)(2,1)S(1)} %get-tuple-element.53), channel_id=1, source_target_pairs={{0,1},{1,0},{2,3},{3,2},{4,5},{5,4},{6,7},{7,6},{8,9},{9,8},{10,11... | collective-permute-start | bytes 909320 | tf_op jit(solution)/shard_map/ppermute | solution.py:20
  4.7 2.5 %collective-permute-start.4 = (bf16[2,576,128]{2,1,0:T(8,128)(2,1)S(1)}, bf16[2,576,128]{2,1,0:T(8,128)(2,1)S(1)}, u32[]{:S(2)}, u32[]{:S(2)}) collective-permute-start(bf16[2,576,128]{2,1,0:T(8,128)(2,1)S(1)} %get-tuple-element.52.refs_0_), channel_id=1, source_target_pairs={{0,3},{1,2},{2,1},{3,0},{4,7},{5,6},{6,5},{7,4},{8,11},{9,10},{10,... | collective-permute-start | bytes 884744 | tf_op jit(solution)/shard_map/ppermute | solution.py:20
  7.2 1.2 %shard_map.92 = (bf16[3,144,384]{2,1,0:T(8,128)(2,1)S(1)}, bf16[2,144,384]{2,1,0:T(8,128)(2,1)S(1)}, bf16[1,144,384]{2,1,0:T(8,128)(2,1)S(1)}) custom-call(bf16[144,384]{1,0:T(8,128)(2,1)} %refs_3_.1, bf16[144,384]{1,0:T(8,128)(2,1)} %refs_4_.1, bf16[144,384]{1,0:T(8,128)(2,1)} %bitcast.6, bf16[144,384]{1,0:T(8,128)(2,1)} %refs_3_.1, ...), custom_call_target="tpu_custom_call" | custom-call | flops 1 | bytes 1 | tf_op jit(solution)/shard_map/pallas_call | solution.py:26
  8.4 1.6 %collective-permute-start.1 = (bf16[2,144,384]{2,1,0:T(8,128)(2,1)S(1)}, bf16[2,144,384]{2,1,0:T(8,128)(2,1)S(1)}, u32[]{:S(2)}, u32[]{:S(2)}) collective-permute-start(bf16[2,144,384]{2,1,0:T(8,128)(2,1)S(1)} %get-tuple-element.48), channel_id=1, source_target_pairs={{0,8},{4,12},{8,0},{12,4},{1,9},{5,13},{9,1},{13,5},{2,10},{6,14},... | collective-permute-start | bytes 663560 | tf_op jit(solution)/shard_map/ppermute | solution.py:20
  10.0 0.5 collective-permute-start.2
  10.5 6.9 %collective-permute-done.2.refs_1_ = bf16[1,144,384]{2,1,0:T(8,128)(2,1)S(1)} collective-permute-done((bf16[1,144,384]{2,1,0:T(8,128)(2,1)S(1)}, bf16[1,144,384]{2,1,0:T(8,128)(2,1)S(1)}, u32[]{:S(2)}, u32[]{:S(2)}) %collective-permute-start.2) | collective-permute-done | bytes 110624 | tf_op jit(solution)/shard_map/ppermute | solution.py:20
  17.6 2.8 %collective-permute-done.4.refs_0_ = bf16[2,576,128]{2,1,0:T(8,128)(2,1)S(1)} collective-permute-done((bf16[2,576,128]{2,1,0:T(8,128)(2,1)S(1)}, bf16[2,576,128]{2,1,0:T(8,128)(2,1)S(1)}, u32[]{:S(2)}, u32[]{:S(2)}) %collective-permute-start.4) | collective-permute-done | bytes 294944 | tf_op jit(solution)/shard_map/ppermute | solution.py:20
  20.5 0.6 %shard_map.94 = (bf16[3,576,384]{2,1,0:T(8,128)(2,1)S(1)}, bf16[3,384,576]{2,1,0:T(8,128)(2,1)S(1)}) custom-call(bf16[3,144,384]{2,1,0:T(8,128)(2,1)S(1)} %get-tuple-element.47.refs_0_, bf16[3,144,384]{2,1,0:T(8,128)(2,1)S(1)} %collective-permute-done.refs_1_, bf16[3,144,384]{2,1,0:T(8,128)(2,1)S(1)} %shard_map.93.refs_2_, ...), custom_call_target="tpu_custom_call" | custom-call | flops 1 | bytes 1 | tf_op jit(solution)/shard_map/pallas_call | solution.py:26
  21.0 2.0 %shard_map.96 = (f32[3,576,384]{2,1,0:T(8,128)S(1)}, f32[2,576,128]{2,1,0:T(8,128)S(1)}, bf16[2,576,128]{2,1,0:T(8,128)(2,1)S(1)}) custom-call(bf16[3,576,384]{2,1,0:T(8,128)(2,1)S(1)} %get-tuple-element.50.whole, bf16[3,384,576]{2,1,0:T(8,128)(2,1)S(1)} %get-tuple-element.51.turned, bf16[2,576,128]{2,1,0:T(8,128)(2,1)S(1)} %get-tuple-element.52.refs_0_, ...), custom_call_target="tpu_custom_call" | custom-call | flops 1 | bytes 1 | tf_op jit(solution)/shard_map/pallas_call | solution.py:26
  23.1 1.5 %shard_map.97 = (f32[3,576,384]{2,1,0:T(8,128)S(1)}, bf16[2,576,128]{2,1,0:T(8,128)(2,1)S(1)}) custom-call(bf16[3,576,384]{2,1,0:T(8,128)(2,1)S(1)} %get-tuple-element.50.whole, bf16[3,384,576]{2,1,0:T(8,128)(2,1)S(1)} %get-tuple-element.51.turned, bf16[2,576,128]{2,1,0:T(8,128)(2,1)S(1)} %collective-permute-done.4.refs_0_, ...), custom_call_target="tpu_custom_call" | custom-call | flops 1 | bytes 1 | tf_op jit(solution)/shard_map/pallas_call | solution.py:26
  24.5 3.8 %collective-permute-done.6.block = bf16[2,576,128]{2,1,0:T(8,128)(2,1)S(1)} collective-permute-done((bf16[2,576,128]{2,1,0:T(8,128)(2,1)S(1)}, bf16[2,576,128]{2,1,0:T(8,128)(2,1)S(1)}, u32[]{:S(2)}, u32[]{:S(2)}) %collective-permute-start.6) | collective-permute-done | bytes 294944 | tf_op jit(solution)/shard_map/ppermute | solution.py:20
  28.6 1.0 %shard_map.98 = (bf16[384,128]{1,0:T(8,128)(2,1)S(1)}, bf16[384,128]{1,0:T(8,128)(2,1)S(1)}, bf16[384,128]{1,0:T(8,128)(2,1)S(1)}, bf16[2,144,384]{2,1,0:T(8,128...) custom-call(bf16[3,384,576]{2,1,0:T(8,128)(2,1)S(1)} %get-tuple-element.51.turned, ...), custom_call_target="tpu_custom_call" | custom-call | flops 1 | bytes 1 | tf_op jit(solution)/shard_map/pallas_call | solution.py:26
  32.0 1.6 %collective-permute-start.10 = (bf16[224,384]{1,0:T(8,128)(2,1)S(1)}, bf16[224,384]{1,0:T(8,128)(2,1)S(1)}, u32[]{:S(2)}, u32[]{:S(2)}) collective-permute-start(bf16[224,384]{1,0:T(8,128)(2,1)S(1)} %get-tuple-element.71), channel_id=1, source_target_pairs={{0,16},{4,20},{8,24},{12,28},{16,0},{20,4},{24,8},{28,12},{1,17},{... | collective-permute-start | bytes 516104 | tf_op jit(solution)/shard_map/ppermute | solution.py:280
  33.6 1.5 %collective-permute-start.11 = (bf16[224,384]{1,0:T(8,128)(2,1)S(1)}, bf16[224,384]{1,0:T(8,128)(2,1)S(1)}, u32[]{:S(2)}, u32[]{:S(2)}) collective-permute-start(bf16[224,384]{1,0:T(8,128)(2,1)S(1)} %get-tuple-element.72), channel_id=1, source_target_pairs={{0,8},{4,12},{8,0},{12,4},{16,24},{20,28},{24,16},{28,20},{1,9},{5... | collective-permute-start | bytes 516104 | tf_op jit(solution)/shard_map/ppermute | solution.py:280
  36.1 1.7 %collective-permute-start.15 = (bf16[2,576,128]{2,1,0:T(8,128)(2,1)S(1)}, bf16[2,576,128]{2,1,0:T(8,128)(2,1)S(1)}, u32[]{:S(2)}, u32[]{:S(2)}) collective-permute-start(bf16[2,576,128]{2,1,0:T(8,128)(2,1)S(1)} %shard_map.104), channel_id=1, source_target_pairs={{0,2},{1,3},{2,0},{3,1},{4,6},{5,7},{6,4},{7,5},{8,10},{9,11},{10,... | collective-permute-start | bytes 884744 | tf_op jit(solution)/shard_map/ppermute | solution.py:20
  37.9 0.6 %collective-permute-start.16 = (bf16[2,576,128]{2,1,0:T(8,128)(2,1)S(1)}, bf16[2,576,128]{2,1,0:T(8,128)(2,1)S(1)}, u32[]{:S(2)}, u32[]{:S(2)}) collective-permute-start(bf16[2,576,128]{2,1,0:T(8,128)(2,1)S(1)} %get-tuple-element.83), channel_id=1, source_target_pairs={{0,1},{1,0},{2,3},{3,2},{4,5},{5,4},{6,7},{7,6},{8,9},{9,8},{10,11... | collective-permute-start | bytes 884744 | tf_op jit(solution)/shard_map/ppermute | solution.py:20
  38.5 0.8 %collective-permute-done.10.refs_1_ = bf16[224,384]{1,0:T(8,128)(2,1)S(1)} collective-permute-done((bf16[224,384]{1,0:T(8,128)(2,1)S(1)}, bf16[224,384]{1,0:T(8,128)(2,1)S(1)}, u32[]{:S(2)}, u32[]{:S(2)}) %collective-permute-start.10) | collective-permute-done | bytes 172064 | tf_op jit(solution)/shard_map/ppermute | solution.py:280
  39.3 4.2 %collective-permute-done.11.refs_2_ = bf16[224,384]{1,0:T(8,128)(2,1)S(1)} collective-permute-done((bf16[224,384]{1,0:T(8,128)(2,1)S(1)}, bf16[224,384]{1,0:T(8,128)(2,1)S(1)}, u32[]{:S(2)}, u32[]{:S(2)}) %collective-permute-start.11) | collective-permute-done | bytes 172064 | tf_op jit(solution)/shard_map/ppermute | solution.py:280
  43.5 1.3 %collective-permute-start.13 = (bf16[224,384]{1,0:T(8,128)(2,1)S(1)}, bf16[224,384]{1,0:T(8,128)(2,1)S(1)}, u32[]{:S(2)}, u32[]{:S(2)}) collective-permute-start(bf16[224,384]{1,0:T(8,128)(2,1)S(1)} %shard_map.101.mine), channel_id=1, source_target_pairs={{0,16},{16,0},{1,17},{17,1},{2,18},{18,2},{3,19},{19,3},{4,20},{20... | collective-permute-start | bytes 516104 | tf_op jit(solution)/shard_map/ppermute | solution.py:20
  44.8 4.2 %collective-permute-done.13.other = bf16[224,384]{1,0:T(8,128)(2,1)S(1)} collective-permute-done((bf16[224,384]{1,0:T(8,128)(2,1)S(1)}, bf16[224,384]{1,0:T(8,128)(2,1)S(1)}, u32[]{:S(2)}, u32[]{:S(2)}) %collective-permute-start.13) | collective-permute-done | bytes 172064 | tf_op jit(solution)/shard_map/ppermute | solution.py:20
  49.0 0.8 %shard_map.102 = (bf16[144,384]{1,0:T(8,128)(2,1)}, bf16[144,384]{1,0:T(8,128)(2,1)}, bf16[144,384]{1,0:T(8,128)(2,1)}) custom-call(bf16[224,384]{1,0:T(8,128)(2,1)S(1)} %shard_map.101.mine, bf16[224,384]{1,0:T(8,128)(2,1)S(1)} %collective-permute-done.13.other), custom_call_target="tpu_custom_call" | custom-call | flops 1 | bytes 1 | tf_op jit(solution)/shard_map/pallas_call | solution.py:26
  49.8 1.9 %collective-permute-done.15.refs_0_ = bf16[2,576,128]{2,1,0:T(8,128)(2,1)S(1)} collective-permute-done((bf16[2,576,128]{2,1,0:T(8,128)(2,1)S(1)}, bf16[2,576,128]{2,1,0:T(8,128)(2,1)S(1)}, u32[]{:S(2)}, u32[]{:S(2)}) %collective-permute-start.15) | collective-permute-done | bytes 294944 | tf_op jit(solution)/shard_map/ppermute | solution.py:20
  51.7 0.8 %shard_map.105 = (bf16[576,128]{1,0:T(8,128)(2,1)}, bf16[576,128]{1,0:T(8,128)(2,1)}) custom-call(f32[2,576,128]{2,1,0:T(8,128)S(1)} %get-tuple-element.77.own, bf16[2,576,128]{2,1,0:T(8,128)(2,1)S(1)} %collective-permute-done.15.refs_0_, bf16[2,576,128]{2,1,0:T(8,128)(2,1)S(1)} %collective-permute-done.16.refs_1_), custom_call_target="tpu_custom_call" | custom-call | flops 1 | bytes 1 | tf_op jit(solution)/shard_map/pallas_call | solution.py:26
  (24 shorter events, 3.9 us)
Async XLA Ops:
  1.7 18.8 %collective-permute-start.5 = (bf16[2,592,128]{2,1,0:T(8,128)(2,1)S(1)}, bf16[2,592,128]{2,1,0:T(8,128)(2,1)S(1)}, u32[]{:S(2)}, u32[]{:S(2)}) collective-permute-start(bf16[2,592,128]{2,1,0:T(8,128)(2,1)S(1)} %get-tuple-element.53), channel_id=1, source_target_pairs={{0,1},{1,0},{2,3},{3,2},{4,5},{5,4},{6,7},{7,6},{8,9},{9,8},{10,11... | collective-permute-start | bytes 909320 | tf_op jit(solution)/shard_map/ppermute | solution.py:20
  4.7 15.7 %collective-permute-start.4 = (bf16[2,576,128]{2,1,0:T(8,128)(2,1)S(1)}, bf16[2,576,128]{2,1,0:T(8,128)(2,1)S(1)}, u32[]{:S(2)}, u32[]{:S(2)}) collective-permute-start(bf16[2,576,128]{2,1,0:T(8,128)(2,1)S(1)} %get-tuple-element.52.refs_0_), channel_id=1, source_target_pairs={{0,3},{1,2},{2,1},{3,0},{4,7},{5,6},{6,5},{7,4},{8,11},{9,10},{10,... | collective-permute-start | bytes 884744 | tf_op jit(solution)/shard_map/ppermute | solution.py:20
  8.4 9.0 %collective-permute-start.1 = (bf16[2,144,384]{2,1,0:T(8,128)(2,1)S(1)}, bf16[2,144,384]{2,1,0:T(8,128)(2,1)S(1)}, u32[]{:S(2)}, u32[]{:S(2)}) collective-permute-start(bf16[2,144,384]{2,1,0:T(8,128)(2,1)S(1)} %get-tuple-element.48), channel_id=1, source_target_pairs={{0,8},{4,12},{8,0},{12,4},{1,9},{5,13},{9,1},{13,5},{2,10},{6,14},... | collective-permute-start | bytes 663560 | tf_op jit(solution)/shard_map/ppermute | solution.py:20
  10.0 7.5 %collective-permute-start.2 = (bf16[1,144,384]{2,1,0:T(8,128)(2,1)S(1)}, bf16[1,144,384]{2,1,0:T(8,128)(2,1)S(1)}, u32[]{:S(2)}, u32[]{:S(2)}) collective-permute-start(bf16[1,144,384]{2,1,0:T(8,128)(2,1)S(1)} %get-tuple-element.49), channel_id=1, source_target_pairs={{0,8},{4,12},{8,0},{12,4},{1,9},{5,13},{9,1},{13,5},{2,10},{6,14},... | collective-permute-start | bytes 331784 | tf_op jit(solution)/shard_map/ppermute | solution.py:20
  10.5 9.9 %collective-permute-start = (bf16[3,144,384]{2,1,0:T(8,128)(2,1)S(1)}, bf16[3,144,384]{2,1,0:T(8,128)(2,1)S(1)}, u32[]{:S(2)}, u32[]{:S(2)}) collective-permute-start(bf16[3,144,384]{2,1,0:T(8,128)(2,1)S(1)} %get-tuple-element.47.refs_0_), channel_id=1, source_target_pairs={{0,4},{4,0},{8,12},{12,8},{1,5},{5,1},{9,13},{13,9},{2,6},{6,2},{1... | collective-permute-start | bytes 995336 | tf_op jit(solution)/shard_map/ppermute | solution.py:20
  17.5 2.9 %collective-permute-start.3 = (bf16[3,144,384]{2,1,0:T(8,128)(2,1)S(1)}, bf16[3,144,384]{2,1,0:T(8,128)(2,1)S(1)}, u32[]{:S(2)}, u32[]{:S(2)}) collective-permute-start(bf16[3,144,384]{2,1,0:T(8,128)(2,1)S(1)} %shard_map.93.refs_2_), channel_id=1, source_target_pairs={{0,4},{4,0},{8,12},{12,8},{1,5},{5,1},{9,13},{13,9},{2,6},{6,2},{1... | collective-permute-start | bytes 995336 | tf_op jit(solution)/shard_map/ppermute | solution.py:20
  20.4 7.9 %collective-permute-start.6 = (bf16[2,576,128]{2,1,0:T(8,128)(2,1)S(1)}, bf16[2,576,128]{2,1,0:T(8,128)(2,1)S(1)}, u32[]{:S(2)}, u32[]{:S(2)}) collective-permute-start(bf16[2,576,128]{2,1,0:T(8,128)(2,1)S(1)} %collective-permute-done.4.refs_0_), channel_id=1, source_target_pairs={{0,1},{1,0},{2,3},{3,2},{4,5},{5,4},{6,7},{7,6},{8,9},{9,8},{10,11... | collective-permute-start | bytes 884744 | tf_op jit(solution)/shard_map/ppermute | solution.py:20
  28.3 7.7 %collective-permute-start.14 = (bf16[2,576,128]{2,1,0:T(8,128)(2,1)S(1)}, bf16[2,576,128]{2,1,0:T(8,128)(2,1)S(1)}, u32[]{:S(2)}, u32[]{:S(2)}) collective-permute-start(bf16[2,576,128]{2,1,0:T(8,128)(2,1)S(1)} %get-tuple-element.80), channel_id=1, source_target_pairs={{0,1},{1,0},{2,3},{3,2},{4,5},{5,4},{6,7},{7,6},{8,9},{9,8},{10,11... | collective-permute-start | bytes 884744 | tf_op jit(solution)/shard_map/ppermute | solution.py:20
  29.6 1.5 %collective-permute-start.7 = (bf16[2,144,384]{2,1,0:T(8,128)(2,1)S(1)}, bf16[2,144,384]{2,1,0:T(8,128)(2,1)S(1)}, u32[]{:S(2)}, u32[]{:S(2)}) collective-permute-start(bf16[2,144,384]{2,1,0:T(8,128)(2,1)S(1)} %get-tuple-element.67), channel_id=1, source_target_pairs={{0,4},{4,0},{8,12},{12,8},{1,5},{5,1},{9,13},{13,9},{2,6},{6,2},{1... | collective-permute-start | bytes 663560 | tf_op jit(solution)/shard_map/ppermute | solution.py:20
  29.7 1.8 %collective-permute-start.8 = (bf16[2,144,384]{2,1,0:T(8,128)(2,1)S(1)}, bf16[2,144,384]{2,1,0:T(8,128)(2,1)S(1)}, u32[]{:S(2)}, u32[]{:S(2)}) collective-permute-start(bf16[2,144,384]{2,1,0:T(8,128)(2,1)S(1)} %get-tuple-element.68), channel_id=1, source_target_pairs={{0,4},{4,0},{8,12},{12,8},{1,5},{5,1},{9,13},{13,9},{2,6},{6,2},{1... | collective-permute-start | bytes 663560 | tf_op jit(solution)/shard_map/ppermute | solution.py:20
  30.2 1.6 %collective-permute-start.9 = (bf16[2,144,384]{2,1,0:T(8,128)(2,1)S(1)}, bf16[2,144,384]{2,1,0:T(8,128)(2,1)S(1)}, u32[]{:S(2)}, u32[]{:S(2)}) collective-permute-start(bf16[2,144,384]{2,1,0:T(8,128)(2,1)S(1)} %get-tuple-element.69), channel_id=1, source_target_pairs={{0,4},{4,0},{8,12},{12,8},{1,5},{5,1},{9,13},{13,9},{2,6},{6,2},{1... | collective-permute-start | bytes 663560 | tf_op jit(solution)/shard_map/ppermute | solution.py:20
  32.0 7.3 %collective-permute-start.10 = (bf16[224,384]{1,0:T(8,128)(2,1)S(1)}, bf16[224,384]{1,0:T(8,128)(2,1)S(1)}, u32[]{:S(2)}, u32[]{:S(2)}) collective-permute-start(bf16[224,384]{1,0:T(8,128)(2,1)S(1)} %get-tuple-element.71), channel_id=1, source_target_pairs={{0,16},{4,20},{8,24},{12,28},{16,0},{20,4},{24,8},{28,12},{1,17},{... | collective-permute-start | bytes 516104 | tf_op jit(solution)/shard_map/ppermute | solution.py:280
  33.6 9.9 %collective-permute-start.11 = (bf16[224,384]{1,0:T(8,128)(2,1)S(1)}, bf16[224,384]{1,0:T(8,128)(2,1)S(1)}, u32[]{:S(2)}, u32[]{:S(2)}) collective-permute-start(bf16[224,384]{1,0:T(8,128)(2,1)S(1)} %get-tuple-element.72), channel_id=1, source_target_pairs={{0,8},{4,12},{8,0},{12,4},{16,24},{20,28},{24,16},{28,20},{1,9},{5... | collective-permute-start | bytes 516104 | tf_op jit(solution)/shard_map/ppermute | solution.py:280
  35.1 8.4 %collective-permute-start.12 = (bf16[224,384]{1,0:T(8,128)(2,1)S(1)}, bf16[224,384]{1,0:T(8,128)(2,1)S(1)}, u32[]{:S(2)}, u32[]{:S(2)}) collective-permute-start(bf16[224,384]{1,0:T(8,128)(2,1)S(1)} %get-tuple-element.73), channel_id=1, source_target_pairs={{0,24},{4,28},{8,16},{12,20},{16,8},{20,12},{24,0},{28,4},{1,25},{... | collective-permute-start | bytes 516104 | tf_op jit(solution)/shard_map/ppermute | solution.py:280
  36.1 15.6 %collective-permute-start.15 = (bf16[2,576,128]{2,1,0:T(8,128)(2,1)S(1)}, bf16[2,576,128]{2,1,0:T(8,128)(2,1)S(1)}, u32[]{:S(2)}, u32[]{:S(2)}) collective-permute-start(bf16[2,576,128]{2,1,0:T(8,128)(2,1)S(1)} %shard_map.104), channel_id=1, source_target_pairs={{0,2},{1,3},{2,0},{3,1},{4,6},{5,7},{6,4},{7,5},{8,10},{9,11},{10,... | collective-permute-start | bytes 884744 | tf_op jit(solution)/shard_map/ppermute | solution.py:20
  37.9 13.8 %collective-permute-start.16 = (bf16[2,576,128]{2,1,0:T(8,128)(2,1)S(1)}, bf16[2,576,128]{2,1,0:T(8,128)(2,1)S(1)}, u32[]{:S(2)}, u32[]{:S(2)}) collective-permute-start(bf16[2,576,128]{2,1,0:T(8,128)(2,1)S(1)} %get-tuple-element.83), channel_id=1, source_target_pairs={{0,1},{1,0},{2,3},{3,2},{4,5},{5,4},{6,7},{7,6},{8,9},{9,8},{10,11... | collective-permute-start | bytes 884744 | tf_op jit(solution)/shard_map/ppermute | solution.py:20
  43.5 5.5 %collective-permute-start.13 = (bf16[224,384]{1,0:T(8,128)(2,1)S(1)}, bf16[224,384]{1,0:T(8,128)(2,1)S(1)}, u32[]{:S(2)}, u32[]{:S(2)}) collective-permute-start(bf16[224,384]{1,0:T(8,128)(2,1)S(1)} %shard_map.101.mine), channel_id=1, source_target_pairs={{0,16},{16,0},{1,17},{17,1},{2,18},{18,2},{3,19},{19,3},{4,20},{20... | collective-permute-start | bytes 516104 | tf_op jit(solution)/shard_map/ppermute | solution.py:20

commit v8 on v5

--- a/solution.py
+++ b/solution.py
@@ -220,12 +220,13 @@
         block[mask], block[1] = lax.optimization_barrier((block[mask], block[1]))
         block[mask ^ 1] = exchange(block[mask], "tensor", 1)
     masks = list(range(fsdp))
-    weight[1] = exchange(weight[0], "fsdp", 1)
     for mask in masks[2::2]:
         weight[mask], = call(
             join_kernel, [(weight[0].shape, BF16)], [exchange(run, "fsdp", mask) for run in runs]
         )
+        weight[0], weight[mask] = lax.optimization_barrier((weight[0], weight[mask]))
         weight[mask + 1] = exchange(weight[mask], "fsdp", 1)
+    weight[1] = exchange(weight[0], "fsdp", 1)
     whole, turned = call(
         functools.partial(assemble_kernel, masks),
         [((3, width, hidden_width), BF16), ((3, hidden_width, width), BF16)],

time: 52.1 us -> 52.1 us (level)
  no operation moved by 1% of the time
where the time goes in v8:
time: 52.1 us; the launch traced here: 51.9 us
  waiting for transfers between devices  24.9 us (48%)
  starting transfers between devices  16.3 us (31%)
  Pallas kernels  9.95 us (19%)
  between operations  0.74 us (1%)
    ppermute x14, waiting for transfers between devices, exchange(): lax.ppermute(array, axis, [(i, i ^ mask) for i in range(lax.axis_size(axi...  19.4 us
    ppermute x14, starting transfers between devices, exchange(): lax.ppermute(array, axis, [(i, i ^ mask) for i in range(lax.axis_size(axi...  12.8 us
    pallas_call x13, Pallas kernels, call(): pl.pallas_call(body, out_shape=[kind(shape, dtype) for shape, dtype in ou...  9.95 us
    ppermute x3, waiting for transfers between devices, per_device(): landed.append(lax.ppermute(share, ('dp', 'fsdp'), perm))  5.48 us
    ppermute x3, starting transfers between devices, per_device(): landed.append(lax.ppermute(share, ('dp', 'fsdp'), perm))  3.55 us
  transfers between devices with their start and end apart: 17, of which 10 were waited for; matrix products, arithmetic and copies ran while one was open for 0% of the time, Pallas kernels for 16%

profile of v8, /device:TPU:0, one launch (start us, length us, event | category | flops | bytes accessed | tf_op | source)
XLA Modules:
  0.0 51.9 jit_solution(15418987353275607197)
XLA Ops:
  0.6 1.0 %shard_map.95 = (bf16[2,576,128]{2,1,0:T(8,128)(2,1)S(1)}, bf16[2,592,128]{2,1,0:T(8,128)(2,1)S(1)}) custom-call(bf16[576,128]{1,0:T(8,128)(2,1)} %bitcast.8, bf16[576,128]{1,0:T(8,128)(2,1)} %bitcast.9), custom_call_target="tpu_custom_call" | custom-call | flops 1 | bytes 1 | tf_op jit(solution)/shard_map/pallas_call | solution.py:26
  1.7 3.1 %collective-permute-start.5 = (bf16[2,592,128]{2,1,0:T(8,128)(2,1)S(1)}, bf16[2,592,128]{2,1,0:T(8,128)(2,1)S(1)}, u32[]{:S(2)}, u32[]{:S(2)}) collective-permute-start(bf16[2,592,128]{2,1,0:T(8,128)(2,1)S(1)} %get-tuple-element.56), channel_id=1, source_target_pairs={{0,1},{1,0},{2,3},{3,2},{4,5},{5,4},{6,7},{7,6},{8,9},{9,8},{10,11... | collective-permute-start | bytes 909320 | tf_op jit(solution)/shard_map/ppermute | solution.py:20
  4.7 2.5 %collective-permute-start.4 = (bf16[2,576,128]{2,1,0:T(8,128)(2,1)S(1)}, bf16[2,576,128]{2,1,0:T(8,128)(2,1)S(1)}, u32[]{:S(2)}, u32[]{:S(2)}) collective-permute-start(bf16[2,576,128]{2,1,0:T(8,128)(2,1)S(1)} %get-tuple-element.55.refs_0_), channel_id=1, source_target_pairs={{0,3},{1,2},{2,1},{3,0},{4,7},{5,6},{6,5},{7,4},{8,11},{9,10},{10,... | collective-permute-start | bytes 884744 | tf_op jit(solution)/shard_map/ppermute | solution.py:20
  7.2 1.2 %shard_map.92 = (bf16[3,144,384]{2,1,0:T(8,128)(2,1)S(1)}, bf16[2,144,384]{2,1,0:T(8,128)(2,1)S(1)}, bf16[1,144,384]{2,1,0:T(8,128)(2,1)S(1)}) custom-call(bf16[144,384]{1,0:T(8,128)(2,1)} %refs_3_.1, bf16[144,384]{1,0:T(8,128)(2,1)} %refs_4_.1, bf16[144,384]{1,0:T(8,128)(2,1)} %bitcast.6, bf16[144,384]{1,0:T(8,128)(2,1)} %refs_3_.1, ...), custom_call_target="tpu_custom_call" | custom-call | flops 1 | bytes 1 | tf_op jit(solution)/shard_map/pallas_call | solution.py:26
  8.4 1.6 %collective-permute-start = (bf16[2,144,384]{2,1,0:T(8,128)(2,1)S(1)}, bf16[2,144,384]{2,1,0:T(8,128)(2,1)S(1)}, u32[]{:S(2)}, u32[]{:S(2)}) collective-permute-start(bf16[2,144,384]{2,1,0:T(8,128)(2,1)S(1)} %get-tuple-element.49), channel_id=1, source_target_pairs={{0,8},{4,12},{8,0},{12,4},{1,9},{5,13},{9,1},{13,5},{2,10},{6,14},... | collective-permute-start | bytes 663560 | tf_op jit(solution)/shard_map/ppermute | solution.py:20
  10.5 7.0 %collective-permute-done.1.refs_1_ = bf16[1,144,384]{2,1,0:T(8,128)(2,1)S(1)} collective-permute-done((bf16[1,144,384]{2,1,0:T(8,128)(2,1)S(1)}, bf16[1,144,384]{2,1,0:T(8,128)(2,1)S(1)}, u32[]{:S(2)}, u32[]{:S(2)}) %collective-permute-start.1) | collective-permute-done | bytes 110624 | tf_op jit(solution)/shard_map/ppermute | solution.py:20
  18.1 2.3 %collective-permute-done.4.refs_0_ = bf16[2,576,128]{2,1,0:T(8,128)(2,1)S(1)} collective-permute-done((bf16[2,576,128]{2,1,0:T(8,128)(2,1)S(1)}, bf16[2,576,128]{2,1,0:T(8,128)(2,1)S(1)}, u32[]{:S(2)}, u32[]{:S(2)}) %collective-permute-start.4) | collective-permute-done | bytes 294944 | tf_op jit(solution)/shard_map/ppermute | solution.py:20
  20.5 0.6 %shard_map.94 = (bf16[3,576,384]{2,1,0:T(8,128)(2,1)S(1)}, bf16[3,384,576]{2,1,0:T(8,128)(2,1)S(1)}) custom-call(bf16[3,144,384]{2,1,0:T(8,128)(2,1)S(1)} %get-tuple-element.51.refs_0_, bf16[3,144,384]{2,1,0:T(8,128)(2,1)S(1)} %collective-permute-done.2.refs_1_, bf16[3,144,384]{2,1,0:T(8,128)(2,1)S(1)} %shard_map.93.refs_2_, ...), custom_call_target="tpu_custom_call" | custom-call | flops 1 | bytes 1 | tf_op jit(solution)/shard_map/pallas_call | solution.py:26
  21.0 2.0 %shard_map.96 = (f32[3,576,384]{2,1,0:T(8,128)S(1)}, f32[2,576,128]{2,1,0:T(8,128)S(1)}, bf16[2,576,128]{2,1,0:T(8,128)(2,1)S(1)}) custom-call(bf16[3,576,384]{2,1,0:T(8,128)(2,1)S(1)} %get-tuple-element.53.whole, bf16[3,384,576]{2,1,0:T(8,128)(2,1)S(1)} %get-tuple-element.54.turned, bf16[2,576,128]{2,1,0:T(8,128)(2,1)S(1)} %get-tuple-element.55.refs_0_, ...), custom_call_target="tpu_custom_call" | custom-call | flops 1 | bytes 1 | tf_op jit(solution)/shard_map/pallas_call | solution.py:26
  23.1 1.5 %shard_map.97 = (f32[3,576,384]{2,1,0:T(8,128)S(1)}, bf16[2,576,128]{2,1,0:T(8,128)(2,1)S(1)}) custom-call(bf16[3,576,384]{2,1,0:T(8,128)(2,1)S(1)} %get-tuple-element.53.whole, bf16[3,384,576]{2,1,0:T(8,128)(2,1)S(1)} %get-tuple-element.54.turned, bf16[2,576,128]{2,1,0:T(8,128)(2,1)S(1)} %collective-permute-done.4.refs_0_, ...), custom_call_target="tpu_custom_call" | custom-call | flops 1 | bytes 1 | tf_op jit(solution)/shard_map/pallas_call | solution.py:26
  24.5 3.8 %collective-permute-done.6.block = bf16[2,576,128]{2,1,0:T(8,128)(2,1)S(1)} collective-permute-done((bf16[2,576,128]{2,1,0:T(8,128)(2,1)S(1)}, bf16[2,576,128]{2,1,0:T(8,128)(2,1)S(1)}, u32[]{:S(2)}, u32[]{:S(2)}) %collective-permute-start.6) | collective-permute-done | bytes 294944 | tf_op jit(solution)/shard_map/ppermute | solution.py:20
  28.6 1.0 %shard_map.98 = (bf16[384,128]{1,0:T(8,128)(2,1)S(1)}, bf16[384,128]{1,0:T(8,128)(2,1)S(1)}, bf16[384,128]{1,0:T(8,128)(2,1)S(1)}, bf16[2,144,384]{2,1,0:T(8,128...) custom-call(bf16[3,384,576]{2,1,0:T(8,128)(2,1)S(1)} %get-tuple-element.54.turned, ...), custom_call_target="tpu_custom_call" | custom-call | flops 1 | bytes 1 | tf_op jit(solution)/shard_map/pallas_call | solution.py:26
  30.3 0.7 %shard_map.99 = (f32[2,144,384]{2,1,0:T(8,128)S(1)}, f32[2,144,384]{2,1,0:T(8,128)S(1)}, f32[2,144,384]{2,1,0:T(8,128)S(1)}, f32[2,576,128]{2,1,0:T(8,128)S(1)}) custom-call(bf16[3,576,384]{2,1,0:T(8,128)(2,1)S(1)} %get-tuple-element.53.whole, bf16[2,576,128]{2,1,0:T(8,128)(2,1)S(1)} %collective-permute-done.6.block, ...), custom_call_target="tpu_custom_call" | custom-call | flops 1 | bytes 1 | tf_op jit(solution)/shard_map/pallas_call | solution.py:26
  32.0 1.6 %collective-permute-start.10 = (bf16[224,384]{1,0:T(8,128)(2,1)S(1)}, bf16[224,384]{1,0:T(8,128)(2,1)S(1)}, u32[]{:S(2)}, u32[]{:S(2)}) collective-permute-start(bf16[224,384]{1,0:T(8,128)(2,1)S(1)} %get-tuple-element.74), channel_id=1, source_target_pairs={{0,16},{4,20},{8,24},{12,28},{16,0},{20,4},{24,8},{28,12},{1,17},{... | collective-permute-start | bytes 516104 | tf_op jit(solution)/shard_map/ppermute | solution.py:280
  33.6 1.5 %collective-permute-start.11 = (bf16[224,384]{1,0:T(8,128)(2,1)S(1)}, bf16[224,384]{1,0:T(8,128)(2,1)S(1)}, u32[]{:S(2)}, u32[]{:S(2)}) collective-permute-start(bf16[224,384]{1,0:T(8,128)(2,1)S(1)} %get-tuple-element.75), channel_id=1, source_target_pairs={{0,8},{4,12},{8,0},{12,4},{16,24},{20,28},{24,16},{28,20},{1,9},{5... | collective-permute-start | bytes 516104 | tf_op jit(solution)/shard_map/ppermute | solution.py:280
  35.6 1.7 %collective-permute-start.15 = (bf16[2,576,128]{2,1,0:T(8,128)(2,1)S(1)}, bf16[2,576,128]{2,1,0:T(8,128)(2,1)S(1)}, u32[]{:S(2)}, u32[]{:S(2)}) collective-permute-start(bf16[2,576,128]{2,1,0:T(8,128)(2,1)S(1)} %shard_map.103), channel_id=1, source_target_pairs={{0,2},{1,3},{2,0},{3,1},{4,6},{5,7},{6,4},{7,5},{8,10},{9,11},{10,... | collective-permute-start | bytes 884744 | tf_op jit(solution)/shard_map/ppermute | solution.py:20
  37.4 0.6 %collective-permute-start.16 = (bf16[2,576,128]{2,1,0:T(8,128)(2,1)S(1)}, bf16[2,576,128]{2,1,0:T(8,128)(2,1)S(1)}, u32[]{:S(2)}, u32[]{:S(2)}) collective-permute-start(bf16[2,576,128]{2,1,0:T(8,128)(2,1)S(1)} %get-tuple-element.85), channel_id=1, source_target_pairs={{0,1},{1,0},{2,3},{3,2},{4,5},{5,4},{6,7},{7,6},{8,9},{9,8},{10,11... | collective-permute-start | bytes 884744 | tf_op jit(solution)/shard_map/ppermute | solution.py:20
  38.0 1.3 %collective-permute-done.10.refs_1_ = bf16[224,384]{1,0:T(8,128)(2,1)S(1)} collective-permute-done((bf16[224,384]{1,0:T(8,128)(2,1)S(1)}, bf16[224,384]{1,0:T(8,128)(2,1)S(1)}, u32[]{:S(2)}, u32[]{:S(2)}) %collective-permute-start.10) | collective-permute-done | bytes 172064 | tf_op jit(solution)/shard_map/ppermute | solution.py:280
  39.3 4.2 %collective-permute-done.11.refs_2_ = bf16[224,384]{1,0:T(8,128)(2,1)S(1)} collective-permute-done((bf16[224,384]{1,0:T(8,128)(2,1)S(1)}, bf16[224,384]{1,0:T(8,128)(2,1)S(1)}, u32[]{:S(2)}, u32[]{:S(2)}) %collective-permute-start.11) | collective-permute-done | bytes 172064 | tf_op jit(solution)/shard_map/ppermute | solution.py:280
  43.5 1.3 %collective-permute-start.13 = (bf16[224,384]{1,0:T(8,128)(2,1)S(1)}, bf16[224,384]{1,0:T(8,128)(2,1)S(1)}, u32[]{:S(2)}, u32[]{:S(2)}) collective-permute-start(bf16[224,384]{1,0:T(8,128)(2,1)S(1)} %shard_map.101.mine), channel_id=1, source_target_pairs={{0,16},{16,0},{1,17},{17,1},{2,18},{18,2},{3,19},{19,3},{4,20},{20... | collective-permute-start | bytes 516104 | tf_op jit(solution)/shard_map/ppermute | solution.py:20
  44.8 4.2 %collective-permute-done.13.other = bf16[224,384]{1,0:T(8,128)(2,1)S(1)} collective-permute-done((bf16[224,384]{1,0:T(8,128)(2,1)S(1)}, bf16[224,384]{1,0:T(8,128)(2,1)S(1)}, u32[]{:S(2)}, u32[]{:S(2)}) %collective-permute-start.13) | collective-permute-done | bytes 172064 | tf_op jit(solution)/shard_map/ppermute | solution.py:20
  49.0 0.8 %shard_map.102 = (bf16[144,384]{1,0:T(8,128)(2,1)}, bf16[144,384]{1,0:T(8,128)(2,1)}, bf16[144,384]{1,0:T(8,128)(2,1)}) custom-call(bf16[224,384]{1,0:T(8,128)(2,1)S(1)} %shard_map.101.mine, bf16[224,384]{1,0:T(8,128)(2,1)S(1)} %collective-permute-done.13.other), custom_call_target="tpu_custom_call" | custom-call | flops 1 | bytes 1 | tf_op jit(solution)/shard_map/pallas_call | solution.py:26
  49.8 1.4 %collective-permute-done.15.refs_0_ = bf16[2,576,128]{2,1,0:T(8,128)(2,1)S(1)} collective-permute-done((bf16[2,576,128]{2,1,0:T(8,128)(2,1)S(1)}, bf16[2,576,128]{2,1,0:T(8,128)(2,1)S(1)}, u32[]{:S(2)}, u32[]{:S(2)}) %collective-permute-start.15) | collective-permute-done | bytes 294944 | tf_op jit(solution)/shard_map/ppermute | solution.py:20
  51.2 0.8 %shard_map.104 = (bf16[576,128]{1,0:T(8,128)(2,1)}, bf16[576,128]{1,0:T(8,128)(2,1)}) custom-call(f32[2,576,128]{2,1,0:T(8,128)S(1)} %get-tuple-element.80.own, bf16[2,576,128]{2,1,0:T(8,128)(2,1)S(1)} %collective-permute-done.15.refs_0_, bf16[2,576,128]{2,1,0:T(8,128)(2,1)S(1)} %collective-permute-done.16.refs_1_), custom_call_target="tpu_custom_call" | custom-call | flops 1 | bytes 1 | tf_op jit(solution)/shard_map/pallas_call | solution.py:26
  (23 shorter events, 3.7 us)
Async XLA Ops:
  1.7 18.8 %collective-permute-start.5 = (bf16[2,592,128]{2,1,0:T(8,128)(2,1)S(1)}, bf16[2,592,128]{2,1,0:T(8,128)(2,1)S(1)}, u32[]{:S(2)}, u32[]{:S(2)}) collective-permute-start(bf16[2,592,128]{2,1,0:T(8,128)(2,1)S(1)} %get-tuple-element.56), channel_id=1, source_target_pairs={{0,1},{1,0},{2,3},{3,2},{4,5},{5,4},{6,7},{7,6},{8,9},{9,8},{10,11... | collective-permute-start | bytes 909320 | tf_op jit(solution)/shard_map/ppermute | solution.py:20
  4.7 15.7 %collective-permute-start.4 = (bf16[2,576,128]{2,1,0:T(8,128)(2,1)S(1)}, bf16[2,576,128]{2,1,0:T(8,128)(2,1)S(1)}, u32[]{:S(2)}, u32[]{:S(2)}) collective-permute-start(bf16[2,576,128]{2,1,0:T(8,128)(2,1)S(1)} %get-tuple-element.55.refs_0_), channel_id=1, source_target_pairs={{0,3},{1,2},{2,1},{3,0},{4,7},{5,6},{6,5},{7,4},{8,11},{9,10},{10,... | collective-permute-start | bytes 884744 | tf_op jit(solution)/shard_map/ppermute | solution.py:20
  8.4 9.0 %collective-permute-start = (bf16[2,144,384]{2,1,0:T(8,128)(2,1)S(1)}, bf16[2,144,384]{2,1,0:T(8,128)(2,1)S(1)}, u32[]{:S(2)}, u32[]{:S(2)}) collective-permute-start(bf16[2,144,384]{2,1,0:T(8,128)(2,1)S(1)} %get-tuple-element.49), channel_id=1, source_target_pairs={{0,8},{4,12},{8,0},{12,4},{1,9},{5,13},{9,1},{13,5},{2,10},{6,14},... | collective-permute-start | bytes 663560 | tf_op jit(solution)/shard_map/ppermute | solution.py:20
  10.0 7.5 %collective-permute-start.1 = (bf16[1,144,384]{2,1,0:T(8,128)(2,1)S(1)}, bf16[1,144,384]{2,1,0:T(8,128)(2,1)S(1)}, u32[]{:S(2)}, u32[]{:S(2)}) collective-permute-start(bf16[1,144,384]{2,1,0:T(8,128)(2,1)S(1)} %get-tuple-element.50), channel_id=1, source_target_pairs={{0,8},{4,12},{8,0},{12,4},{1,9},{5,13},{9,1},{13,5},{2,10},{6,14},... | collective-permute-start | bytes 331784 | tf_op jit(solution)/shard_map/ppermute | solution.py:20
  17.5 2.9 %collective-permute-start.2 = (bf16[3,144,384]{2,1,0:T(8,128)(2,1)S(1)}, bf16[3,144,384]{2,1,0:T(8,128)(2,1)S(1)}, u32[]{:S(2)}, u32[]{:S(2)}) collective-permute-start(bf16[3,144,384]{2,1,0:T(8,128)(2,1)S(1)} %get-tuple-element.51.refs_0_), channel_id=1, source_target_pairs={{0,4},{4,0},{8,12},{12,8},{1,5},{5,1},{9,13},{13,9},{2,6},{6,2},{1... | collective-permute-start | bytes 995336 | tf_op jit(solution)/shard_map/ppermute | solution.py:20
  17.6 2.8 %collective-permute-start.3 = (bf16[3,144,384]{2,1,0:T(8,128)(2,1)S(1)}, bf16[3,144,384]{2,1,0:T(8,128)(2,1)S(1)}, u32[]{:S(2)}, u32[]{:S(2)}) collective-permute-start(bf16[3,144,384]{2,1,0:T(8,128)(2,1)S(1)} %shard_map.93.refs_2_), channel_id=1, source_target_pairs={{0,4},{4,0},{8,12},{12,8},{1,5},{5,1},{9,13},{13,9},{2,6},{6,2},{1... | collective-permute-start | bytes 995336 | tf_op jit(solution)/shard_map/ppermute | solution.py:20
  20.4 7.9 %collective-permute-start.6 = (bf16[2,576,128]{2,1,0:T(8,128)(2,1)S(1)}, bf16[2,576,128]{2,1,0:T(8,128)(2,1)S(1)}, u32[]{:S(2)}, u32[]{:S(2)}) collective-permute-start(bf16[2,576,128]{2,1,0:T(8,128)(2,1)S(1)} %collective-permute-done.4.refs_0_), channel_id=1, source_target_pairs={{0,1},{1,0},{2,3},{3,2},{4,5},{5,4},{6,7},{7,6},{8,9},{9,8},{10,11... | collective-permute-start | bytes 884744 | tf_op jit(solution)/shard_map/ppermute | solution.py:20
  28.3 7.2 %collective-permute-start.14 = (bf16[2,576,128]{2,1,0:T(8,128)(2,1)S(1)}, bf16[2,576,128]{2,1,0:T(8,128)(2,1)S(1)}, u32[]{:S(2)}, u32[]{:S(2)}) collective-permute-start(bf16[2,576,128]{2,1,0:T(8,128)(2,1)S(1)} %get-tuple-element.83), channel_id=1, source_target_pairs={{0,1},{1,0},{2,3},{3,2},{4,5},{5,4},{6,7},{7,6},{8,9},{9,8},{10,11... | collective-permute-start | bytes 884744 | tf_op jit(solution)/shard_map/ppermute | solution.py:20
  29.6 1.5 %collective-permute-start.7 = (bf16[2,144,384]{2,1,0:T(8,128)(2,1)S(1)}, bf16[2,144,384]{2,1,0:T(8,128)(2,1)S(1)}, u32[]{:S(2)}, u32[]{:S(2)}) collective-permute-start(bf16[2,144,384]{2,1,0:T(8,128)(2,1)S(1)} %get-tuple-element.70), channel_id=1, source_target_pairs={{0,4},{4,0},{8,12},{12,8},{1,5},{5,1},{9,13},{13,9},{2,6},{6,2},{1... | collective-permute-start | bytes 663560 | tf_op jit(solution)/shard_map/ppermute | solution.py:20
  29.7 1.8 %collective-permute-start.8 = (bf16[2,144,384]{2,1,0:T(8,128)(2,1)S(1)}, bf16[2,144,384]{2,1,0:T(8,128)(2,1)S(1)}, u32[]{:S(2)}, u32[]{:S(2)}) collective-permute-start(bf16[2,144,384]{2,1,0:T(8,128)(2,1)S(1)} %get-tuple-element.71), channel_id=1, source_target_pairs={{0,4},{4,0},{8,12},{12,8},{1,5},{5,1},{9,13},{13,9},{2,6},{6,2},{1... | collective-permute-start | bytes 663560 | tf_op jit(solution)/shard_map/ppermute | solution.py:20
  30.2 1.6 %collective-permute-start.9 = (bf16[2,144,384]{2,1,0:T(8,128)(2,1)S(1)}, bf16[2,144,384]{2,1,0:T(8,128)(2,1)S(1)}, u32[]{:S(2)}, u32[]{:S(2)}) collective-permute-start(bf16[2,144,384]{2,1,0:T(8,128)(2,1)S(1)} %get-tuple-element.72), channel_id=1, source_target_pairs={{0,4},{4,0},{8,12},{12,8},{1,5},{5,1},{9,13},{13,9},{2,6},{6,2},{1... | collective-permute-start | bytes 663560 | tf_op jit(solution)/shard_map/ppermute | solution.py:20
  32.0 7.3 %collective-permute-start.10 = (bf16[224,384]{1,0:T(8,128)(2,1)S(1)}, bf16[224,384]{1,0:T(8,128)(2,1)S(1)}, u32[]{:S(2)}, u32[]{:S(2)}) collective-permute-start(bf16[224,384]{1,0:T(8,128)(2,1)S(1)} %get-tuple-element.74), channel_id=1, source_target_pairs={{0,16},{4,20},{8,24},{12,28},{16,0},{20,4},{24,8},{28,12},{1,17},{... | collective-permute-start | bytes 516104 | tf_op jit(solution)/shard_map/ppermute | solution.py:280
  33.6 9.9 %collective-permute-start.11 = (bf16[224,384]{1,0:T(8,128)(2,1)S(1)}, bf16[224,384]{1,0:T(8,128)(2,1)S(1)}, u32[]{:S(2)}, u32[]{:S(2)}) collective-permute-start(bf16[224,384]{1,0:T(8,128)(2,1)S(1)} %get-tuple-element.75), channel_id=1, source_target_pairs={{0,8},{4,12},{8,0},{12,4},{16,24},{20,28},{24,16},{28,20},{1,9},{5... | collective-permute-start | bytes 516104 | tf_op jit(solution)/shard_map/ppermute | solution.py:280
  35.1 8.4 %collective-permute-start.12 = (bf16[224,384]{1,0:T(8,128)(2,1)S(1)}, bf16[224,384]{1,0:T(8,128)(2,1)S(1)}, u32[]{:S(2)}, u32[]{:S(2)}) collective-permute-start(bf16[224,384]{1,0:T(8,128)(2,1)S(1)} %get-tuple-element.76), channel_id=1, source_target_pairs={{0,24},{4,28},{8,16},{12,20},{16,8},{20,12},{24,0},{28,4},{1,25},{... | collective-permute-start | bytes 516104 | tf_op jit(solution)/shard_map/ppermute | solution.py:280
  35.6 15.6 %collective-permute-start.15 = (bf16[2,576,128]{2,1,0:T(8,128)(2,1)S(1)}, bf16[2,576,128]{2,1,0:T(8,128)(2,1)S(1)}, u32[]{:S(2)}, u32[]{:S(2)}) collective-permute-start(bf16[2,576,128]{2,1,0:T(8,128)(2,1)S(1)} %shard_map.103), channel_id=1, source_target_pairs={{0,2},{1,3},{2,0},{3,1},{4,6},{5,7},{6,4},{7,5},{8,10},{9,11},{10,... | collective-permute-start | bytes 884744 | tf_op jit(solution)/shard_map/ppermute | solution.py:20
  37.4 13.8 %collective-permute-start.16 = (bf16[2,576,128]{2,1,0:T(8,128)(2,1)S(1)}, bf16[2,576,128]{2,1,0:T(8,128)(2,1)S(1)}, u32[]{:S(2)}, u32[]{:S(2)}) collective-permute-start(bf16[2,576,128]{2,1,0:T(8,128)(2,1)S(1)} %get-tuple-element.85), channel_id=1, source_target_pairs={{0,1},{1,0},{2,3},{3,2},{4,5},{5,4},{6,7},{7,6},{8,9},{9,8},{10,11... | collective-permute-start | bytes 884744 | tf_op jit(solution)/shard_map/ppermute | solution.py:20
  43.5 5.5 %collective-permute-start.13 = (bf16[224,384]{1,0:T(8,128)(2,1)S(1)}, bf16[224,384]{1,0:T(8,128)(2,1)S(1)}, u32[]{:S(2)}, u32[]{:S(2)}) collective-permute-start(bf16[224,384]{1,0:T(8,128)(2,1)S(1)} %shard_map.101.mine), channel_id=1, source_target_pairs={{0,16},{16,0},{1,17},{17,1},{2,18},{18,2},{3,19},{19,3},{4,20},{20... | collective-permute-start | bytes 516104 | tf_op jit(solution)/shard_map/ppermute | solution.py:20

commit v9 on v8

--- a/solution.py
+++ b/solution.py
@@ -274,7 +274,7 @@
         )
         ready = shares[0]
         landed = [ready]
-        for i, share in list(enumerate(shares))[1:]:
+        for i, share in reversed(list(enumerate(shares))[1:]):
             mask, flip = 2 * (i // 2), i % 2
             perm = [(d * fsdp + f, (d ^ flip) * fsdp + (f ^ mask)) for d in range(dp) for f in range(fsdp)]
             landed.append(lax.ppermute(share, ("dp", "fsdp"), perm))

time: 52.1 us -> 52.1 us (level)
  transfers between devices with their start and end apart: 17 -> 17, of which waited for: 10 -> 11; matrix products, arithmetic and copies ran while one was open for 0% -> 0% of each run, Pallas kernels for 16% -> 16%
where the time goes in v9:
time: 52.1 us; the launch traced here: 51.9 us
  waiting for transfers between devices  24.7 us (47%)
  starting transfers between devices  16.6 us (32%)
  Pallas kernels  9.95 us (19%)
  between operations  0.74 us (1%)
    ppermute x14, waiting for transfers between devices, exchange(): lax.ppermute(array, axis, [(i, i ^ mask) for i in range(lax.axis_size(axi...  19.4 us
    ppermute x14, starting transfers between devices, exchange(): lax.ppermute(array, axis, [(i, i ^ mask) for i in range(lax.axis_size(axi...  13.1 us
    pallas_call x13, Pallas kernels, call(): pl.pallas_call(body, out_shape=[kind(shape, dtype) for shape, dtype in ou...  9.95 us
    ppermute x3, waiting for transfers between devices, per_device(): landed.append(lax.ppermute(share, ('dp', 'fsdp'), perm))  5.27 us
    ppermute x3, starting transfers between devices, per_device(): landed.append(lax.ppermute(share, ('dp', 'fsdp'), perm))  3.55 us
  transfers between devices with their start and end apart: 17, of which 11 were waited for; matrix products, arithmetic and copies ran while one was open for 0% of the time, Pallas kernels for 16%

profile of v9, /device:TPU:0, one launch (start us, length us, event | category | flops | bytes accessed | tf_op | source)
XLA Modules:
  0.0 51.9 jit_solution(2292895744214474738)
XLA Ops:
  0.6 1.0 %shard_map.95 = (bf16[2,576,128]{2,1,0:T(8,128)(2,1)S(1)}, bf16[2,592,128]{2,1,0:T(8,128)(2,1)S(1)}) custom-call(bf16[576,128]{1,0:T(8,128)(2,1)} %bitcast.8, bf16[576,128]{1,0:T(8,128)(2,1)} %bitcast.9), custom_call_target="tpu_custom_call" | custom-call | flops 1 | bytes 1 | tf_op jit(solution)/shard_map/pallas_call | solution.py:26
  1.7 3.1 %collective-permute-start.5 = (bf16[2,592,128]{2,1,0:T(8,128)(2,1)S(1)}, bf16[2,592,128]{2,1,0:T(8,128)(2,1)S(1)}, u32[]{:S(2)}, u32[]{:S(2)}) collective-permute-start(bf16[2,592,128]{2,1,0:T(8,128)(2,1)S(1)} %get-tuple-element.56), channel_id=1, source_target_pairs={{0,1},{1,0},{2,3},{3,2},{4,5},{5,4},{6,7},{7,6},{8,9},{9,8},{10,11... | collective-permute-start | bytes 909320 | tf_op jit(solution)/shard_map/ppermute | solution.py:20
  4.7 2.5 %collective-permute-start.4 = (bf16[2,576,128]{2,1,0:T(8,128)(2,1)S(1)}, bf16[2,576,128]{2,1,0:T(8,128)(2,1)S(1)}, u32[]{:S(2)}, u32[]{:S(2)}) collective-permute-start(bf16[2,576,128]{2,1,0:T(8,128)(2,1)S(1)} %get-tuple-element.55.refs_0_), channel_id=1, source_target_pairs={{0,3},{1,2},{2,1},{3,0},{4,7},{5,6},{6,5},{7,4},{8,11},{9,10},{10,... | collective-permute-start | bytes 884744 | tf_op jit(solution)/shard_map/ppermute | solution.py:20
  7.2 1.2 %shard_map.92 = (bf16[3,144,384]{2,1,0:T(8,128)(2,1)S(1)}, bf16[2,144,384]{2,1,0:T(8,128)(2,1)S(1)}, bf16[1,144,384]{2,1,0:T(8,128)(2,1)S(1)}) custom-call(bf16[144,384]{1,0:T(8,128)(2,1)} %refs_3_.1, bf16[144,384]{1,0:T(8,128)(2,1)} %refs_4_.1, bf16[144,384]{1,0:T(8,128)(2,1)} %bitcast.6, bf16[144,384]{1,0:T(8,128)(2,1)} %refs_3_.1, ...), custom_call_target="tpu_custom_call" | custom-call | flops 1 | bytes 1 | tf_op jit(solution)/shard_map/pallas_call | solution.py:26
  8.4 1.6 %collective-permute-start = (bf16[2,144,384]{2,1,0:T(8,128)(2,1)S(1)}, bf16[2,144,384]{2,1,0:T(8,128)(2,1)S(1)}, u32[]{:S(2)}, u32[]{:S(2)}) collective-permute-start(bf16[2,144,384]{2,1,0:T(8,128)(2,1)S(1)} %get-tuple-element.49), channel_id=1, source_target_pairs={{0,8},{4,12},{8,0},{12,4},{1,9},{5,13},{9,1},{13,5},{2,10},{6,14},... | collective-permute-start | bytes 663560 | tf_op jit(solution)/shard_map/ppermute | solution.py:20
  10.5 7.0 %collective-permute-done.1.refs_1_ = bf16[1,144,384]{2,1,0:T(8,128)(2,1)S(1)} collective-permute-done((bf16[1,144,384]{2,1,0:T(8,128)(2,1)S(1)}, bf16[1,144,384]{2,1,0:T(8,128)(2,1)S(1)}, u32[]{:S(2)}, u32[]{:S(2)}) %collective-permute-start.1) | collective-permute-done | bytes 110624 | tf_op jit(solution)/shard_map/ppermute | solution.py:20
  18.1 2.3 %collective-permute-done.4.refs_0_ = bf16[2,576,128]{2,1,0:T(8,128)(2,1)S(1)} collective-permute-done((bf16[2,576,128]{2,1,0:T(8,128)(2,1)S(1)}, bf16[2,576,128]{2,1,0:T(8,128)(2,1)S(1)}, u32[]{:S(2)}, u32[]{:S(2)}) %collective-permute-start.4) | collective-permute-done | bytes 294944 | tf_op jit(solution)/shard_map/ppermute | solution.py:20
  20.5 0.6 %shard_map.94 = (bf16[3,576,384]{2,1,0:T(8,128)(2,1)S(1)}, bf16[3,384,576]{2,1,0:T(8,128)(2,1)S(1)}) custom-call(bf16[3,144,384]{2,1,0:T(8,128)(2,1)S(1)} %get-tuple-element.51.refs_0_, bf16[3,144,384]{2,1,0:T(8,128)(2,1)S(1)} %collective-permute-done.2.refs_1_, bf16[3,144,384]{2,1,0:T(8,128)(2,1)S(1)} %shard_map.93.refs_2_, ...), custom_call_target="tpu_custom_call" | custom-call | flops 1 | bytes 1 | tf_op jit(solution)/shard_map/pallas_call | solution.py:26
  21.0 2.0 %shard_map.96 = (f32[3,576,384]{2,1,0:T(8,128)S(1)}, f32[2,576,128]{2,1,0:T(8,128)S(1)}, bf16[2,576,128]{2,1,0:T(8,128)(2,1)S(1)}) custom-call(bf16[3,576,384]{2,1,0:T(8,128)(2,1)S(1)} %get-tuple-element.53.whole, bf16[3,384,576]{2,1,0:T(8,128)(2,1)S(1)} %get-tuple-element.54.turned, bf16[2,576,128]{2,1,0:T(8,128)(2,1)S(1)} %get-tuple-element.55.refs_0_, ...), custom_call_target="tpu_custom_call" | custom-call | flops 1 | bytes 1 | tf_op jit(solution)/shard_map/pallas_call | solution.py:26
  23.1 1.5 %shard_map.97 = (f32[3,576,384]{2,1,0:T(8,128)S(1)}, bf16[2,576,128]{2,1,0:T(8,128)(2,1)S(1)}) custom-call(bf16[3,576,384]{2,1,0:T(8,128)(2,1)S(1)} %get-tuple-element.53.whole, bf16[3,384,576]{2,1,0:T(8,128)(2,1)S(1)} %get-tuple-element.54.turned, bf16[2,576,128]{2,1,0:T(8,128)(2,1)S(1)} %collective-permute-done.4.refs_0_, ...), custom_call_target="tpu_custom_call" | custom-call | flops 1 | bytes 1 | tf_op jit(solution)/shard_map/pallas_call | solution.py:26
  24.5 3.8 %collective-permute-done.6.block = bf16[2,576,128]{2,1,0:T(8,128)(2,1)S(1)} collective-permute-done((bf16[2,576,128]{2,1,0:T(8,128)(2,1)S(1)}, bf16[2,576,128]{2,1,0:T(8,128)(2,1)S(1)}, u32[]{:S(2)}, u32[]{:S(2)}) %collective-permute-start.6) | collective-permute-done | bytes 294944 | tf_op jit(solution)/shard_map/ppermute | solution.py:20
  28.6 1.0 %shard_map.98 = (bf16[384,128]{1,0:T(8,128)(2,1)S(1)}, bf16[384,128]{1,0:T(8,128)(2,1)S(1)}, bf16[384,128]{1,0:T(8,128)(2,1)S(1)}, bf16[2,144,384]{2,1,0:T(8,128...) custom-call(bf16[3,384,576]{2,1,0:T(8,128)(2,1)S(1)} %get-tuple-element.54.turned, ...), custom_call_target="tpu_custom_call" | custom-call | flops 1 | bytes 1 | tf_op jit(solution)/shard_map/pallas_call | solution.py:26
  30.3 0.7 %shard_map.99 = (f32[2,144,384]{2,1,0:T(8,128)S(1)}, f32[2,144,384]{2,1,0:T(8,128)S(1)}, f32[2,144,384]{2,1,0:T(8,128)S(1)}, f32[2,576,128]{2,1,0:T(8,128)S(1)}) custom-call(bf16[3,576,384]{2,1,0:T(8,128)(2,1)S(1)} %get-tuple-element.53.whole, bf16[2,576,128]{2,1,0:T(8,128)(2,1)S(1)} %collective-permute-done.6.block, ...), custom_call_target="tpu_custom_call" | custom-call | flops 1 | bytes 1 | tf_op jit(solution)/shard_map/pallas_call | solution.py:26
  32.0 2.5 %collective-permute-start.10 = (bf16[224,384]{1,0:T(8,128)(2,1)S(1)}, bf16[224,384]{1,0:T(8,128)(2,1)S(1)}, u32[]{:S(2)}, u32[]{:S(2)}) collective-permute-start(bf16[224,384]{1,0:T(8,128)(2,1)S(1)} %get-tuple-element.74), channel_id=1, source_target_pairs={{0,24},{4,28},{8,16},{12,20},{16,8},{20,12},{24,0},{28,4},{1,25},{... | collective-permute-start | bytes 516104 | tf_op jit(solution)/shard_map/ppermute | solution.py:280
  35.0 0.5 %collective-permute-start.12 = (bf16[224,384]{1,0:T(8,128)(2,1)S(1)}, bf16[224,384]{1,0:T(8,128)(2,1)S(1)}, u32[]{:S(2)}, u32[]{:S(2)}) collective-permute-start(bf16[224,384]{1,0:T(8,128)(2,1)S(1)} %get-tuple-element.76), channel_id=1, source_target_pairs={{0,16},{4,20},{8,24},{12,28},{16,0},{20,4},{24,8},{28,12},{1,17},{... | collective-permute-start | bytes 516104 | tf_op jit(solution)/shard_map/ppermute | solution.py:280
  35.6 1.7 %collective-permute-start.15 = (bf16[2,576,128]{2,1,0:T(8,128)(2,1)S(1)}, bf16[2,576,128]{2,1,0:T(8,128)(2,1)S(1)}, u32[]{:S(2)}, u32[]{:S(2)}) collective-permute-start(bf16[2,576,128]{2,1,0:T(8,128)(2,1)S(1)} %shard_map.103), channel_id=1, source_target_pairs={{0,2},{1,3},{2,0},{3,1},{4,6},{5,7},{6,4},{7,5},{8,10},{9,11},{10,... | collective-permute-start | bytes 884744 | tf_op jit(solution)/shard_map/ppermute | solution.py:20
  37.4 0.6 %collective-permute-start.16 = (bf16[2,576,128]{2,1,0:T(8,128)(2,1)S(1)}, bf16[2,576,128]{2,1,0:T(8,128)(2,1)S(1)}, u32[]{:S(2)}, u32[]{:S(2)}) collective-permute-start(bf16[2,576,128]{2,1,0:T(8,128)(2,1)S(1)} %get-tuple-element.85), channel_id=1, source_target_pairs={{0,1},{1,0},{2,3},{3,2},{4,5},{5,4},{6,7},{7,6},{8,9},{9,8},{10,11... | collective-permute-start | bytes 884744 | tf_op jit(solution)/shard_map/ppermute | solution.py:20
  38.0 2.2 %collective-permute-done.10.refs_1_ = bf16[224,384]{1,0:T(8,128)(2,1)S(1)} collective-permute-done((bf16[224,384]{1,0:T(8,128)(2,1)S(1)}, bf16[224,384]{1,0:T(8,128)(2,1)S(1)}, u32[]{:S(2)}, u32[]{:S(2)}) %collective-permute-start.10) | collective-permute-done | bytes 172064 | tf_op jit(solution)/shard_map/ppermute | solution.py:280
  40.2 2.9 %collective-permute-done.11.refs_2_ = bf16[224,384]{1,0:T(8,128)(2,1)S(1)} collective-permute-done((bf16[224,384]{1,0:T(8,128)(2,1)S(1)}, bf16[224,384]{1,0:T(8,128)(2,1)S(1)}, u32[]{:S(2)}, u32[]{:S(2)}) %collective-permute-start.11) | collective-permute-done | bytes 172064 | tf_op jit(solution)/shard_map/ppermute | solution.py:280
  43.3 1.6 %collective-permute-start.13 = (bf16[224,384]{1,0:T(8,128)(2,1)S(1)}, bf16[224,384]{1,0:T(8,128)(2,1)S(1)}, u32[]{:S(2)}, u32[]{:S(2)}) collective-permute-start(bf16[224,384]{1,0:T(8,128)(2,1)S(1)} %shard_map.101.mine), channel_id=1, source_target_pairs={{0,16},{16,0},{1,17},{17,1},{2,18},{18,2},{3,19},{19,3},{4,20},{20... | collective-permute-start | bytes 516104 | tf_op jit(solution)/shard_map/ppermute | solution.py:20
  44.9 4.7 %collective-permute-done.13.other = bf16[224,384]{1,0:T(8,128)(2,1)S(1)} collective-permute-done((bf16[224,384]{1,0:T(8,128)(2,1)S(1)}, bf16[224,384]{1,0:T(8,128)(2,1)S(1)}, u32[]{:S(2)}, u32[]{:S(2)}) %collective-permute-start.13) | collective-permute-done | bytes 172064 | tf_op jit(solution)/shard_map/ppermute | solution.py:20
  49.6 0.8 %shard_map.102 = (bf16[144,384]{1,0:T(8,128)(2,1)}, bf16[144,384]{1,0:T(8,128)(2,1)}, bf16[144,384]{1,0:T(8,128)(2,1)}) custom-call(bf16[224,384]{1,0:T(8,128)(2,1)S(1)} %shard_map.101.mine, bf16[224,384]{1,0:T(8,128)(2,1)S(1)} %collective-permute-done.13.other), custom_call_target="tpu_custom_call" | custom-call | flops 1 | bytes 1 | tf_op jit(solution)/shard_map/pallas_call | solution.py:26
  50.3 0.8 %collective-permute-done.15.refs_0_ = bf16[2,576,128]{2,1,0:T(8,128)(2,1)S(1)} collective-permute-done((bf16[2,576,128]{2,1,0:T(8,128)(2,1)S(1)}, bf16[2,576,128]{2,1,0:T(8,128)(2,1)S(1)}, u32[]{:S(2)}, u32[]{:S(2)}) %collective-permute-start.15) | collective-permute-done | bytes 294944 | tf_op jit(solution)/shard_map/ppermute | solution.py:20
  51.2 0.8 %shard_map.104 = (bf16[576,128]{1,0:T(8,128)(2,1)}, bf16[576,128]{1,0:T(8,128)(2,1)}) custom-call(f32[2,576,128]{2,1,0:T(8,128)S(1)} %get-tuple-element.80.own, bf16[2,576,128]{2,1,0:T(8,128)(2,1)S(1)} %collective-permute-done.15.refs_0_, bf16[2,576,128]{2,1,0:T(8,128)(2,1)S(1)} %collective-permute-done.16.refs_1_), custom_call_target="tpu_custom_call" | custom-call | flops 1 | bytes 1 | tf_op jit(solution)/shard_map/pallas_call | solution.py:26
  (23 shorter events, 3.8 us)
Async XLA Ops:
  1.7 18.8 %collective-permute-start.5 = (bf16[2,592,128]{2,1,0:T(8,128)(2,1)S(1)}, bf16[2,592,128]{2,1,0:T(8,128)(2,1)S(1)}, u32[]{:S(2)}, u32[]{:S(2)}) collective-permute-start(bf16[2,592,128]{2,1,0:T(8,128)(2,1)S(1)} %get-tuple-element.56), channel_id=1, source_target_pairs={{0,1},{1,0},{2,3},{3,2},{4,5},{5,4},{6,7},{7,6},{8,9},{9,8},{10,11... | collective-permute-start | bytes 909320 | tf_op jit(solution)/shard_map/ppermute | solution.py:20
  4.7 15.7 %collective-permute-start.4 = (bf16[2,576,128]{2,1,0:T(8,128)(2,1)S(1)}, bf16[2,576,128]{2,1,0:T(8,128)(2,1)S(1)}, u32[]{:S(2)}, u32[]{:S(2)}) collective-permute-start(bf16[2,576,128]{2,1,0:T(8,128)(2,1)S(1)} %get-tuple-element.55.refs_0_), channel_id=1, source_target_pairs={{0,3},{1,2},{2,1},{3,0},{4,7},{5,6},{6,5},{7,4},{8,11},{9,10},{10,... | collective-permute-start | bytes 884744 | tf_op jit(solution)/shard_map/ppermute | solution.py:20
  8.4 9.0 %collective-permute-start = (bf16[2,144,384]{2,1,0:T(8,128)(2,1)S(1)}, bf16[2,144,384]{2,1,0:T(8,128)(2,1)S(1)}, u32[]{:S(2)}, u32[]{:S(2)}) collective-permute-start(bf16[2,144,384]{2,1,0:T(8,128)(2,1)S(1)} %get-tuple-element.49), channel_id=1, source_target_pairs={{0,8},{4,12},{8,0},{12,4},{1,9},{5,13},{9,1},{13,5},{2,10},{6,14},... | collective-permute-start | bytes 663560 | tf_op jit(solution)/shard_map/ppermute | solution.py:20
  10.0 7.5 %collective-permute-start.1 = (bf16[1,144,384]{2,1,0:T(8,128)(2,1)S(1)}, bf16[1,144,384]{2,1,0:T(8,128)(2,1)S(1)}, u32[]{:S(2)}, u32[]{:S(2)}) collective-permute-start(bf16[1,144,384]{2,1,0:T(8,128)(2,1)S(1)} %get-tuple-element.50), channel_id=1, source_target_pairs={{0,8},{4,12},{8,0},{12,4},{1,9},{5,13},{9,1},{13,5},{2,10},{6,14},... | collective-permute-start | bytes 331784 | tf_op jit(solution)/shard_map/ppermute | solution.py:20
  17.5 2.9 %collective-permute-start.2 = (bf16[3,144,384]{2,1,0:T(8,128)(2,1)S(1)}, bf16[3,144,384]{2,1,0:T(8,128)(2,1)S(1)}, u32[]{:S(2)}, u32[]{:S(2)}) collective-permute-start(bf16[3,144,384]{2,1,0:T(8,128)(2,1)S(1)} %get-tuple-element.51.refs_0_), channel_id=1, source_target_pairs={{0,4},{4,0},{8,12},{12,8},{1,5},{5,1},{9,13},{13,9},{2,6},{6,2},{1... | collective-permute-start | bytes 995336 | tf_op jit(solution)/shard_map/ppermute | solution.py:20
  17.6 2.8 %collective-permute-start.3 = (bf16[3,144,384]{2,1,0:T(8,128)(2,1)S(1)}, bf16[3,144,384]{2,1,0:T(8,128)(2,1)S(1)}, u32[]{:S(2)}, u32[]{:S(2)}) collective-permute-start(bf16[3,144,384]{2,1,0:T(8,128)(2,1)S(1)} %shard_map.93.refs_2_), channel_id=1, source_target_pairs={{0,4},{4,0},{8,12},{12,8},{1,5},{5,1},{9,13},{13,9},{2,6},{6,2},{1... | collective-permute-start | bytes 995336 | tf_op jit(solution)/shard_map/ppermute | solution.py:20
  20.4 7.9 %collective-permute-start.6 = (bf16[2,576,128]{2,1,0:T(8,128)(2,1)S(1)}, bf16[2,576,128]{2,1,0:T(8,128)(2,1)S(1)}, u32[]{:S(2)}, u32[]{:S(2)}) collective-permute-start(bf16[2,576,128]{2,1,0:T(8,128)(2,1)S(1)} %collective-permute-done.4.refs_0_), channel_id=1, source_target_pairs={{0,1},{1,0},{2,3},{3,2},{4,5},{5,4},{6,7},{7,6},{8,9},{9,8},{10,11... | collective-permute-start | bytes 884744 | tf_op jit(solution)/shard_map/ppermute | solution.py:20
  28.3 7.2 %collective-permute-start.14 = (bf16[2,576,128]{2,1,0:T(8,128)(2,1)S(1)}, bf16[2,576,128]{2,1,0:T(8,128)(2,1)S(1)}, u32[]{:S(2)}, u32[]{:S(2)}) collective-permute-start(bf16[2,576,128]{2,1,0:T(8,128)(2,1)S(1)} %get-tuple-element.83), channel_id=1, source_target_pairs={{0,1},{1,0},{2,3},{3,2},{4,5},{5,4},{6,7},{7,6},{8,9},{9,8},{10,11... | collective-permute-start | bytes 884744 | tf_op jit(solution)/shard_map/ppermute | solution.py:20
  29.6 1.5 %collective-permute-start.7 = (bf16[2,144,384]{2,1,0:T(8,128)(2,1)S(1)}, bf16[2,144,384]{2,1,0:T(8,128)(2,1)S(1)}, u32[]{:S(2)}, u32[]{:S(2)}) collective-permute-start(bf16[2,144,384]{2,1,0:T(8,128)(2,1)S(1)} %get-tuple-element.70), channel_id=1, source_target_pairs={{0,4},{4,0},{8,12},{12,8},{1,5},{5,1},{9,13},{13,9},{2,6},{6,2},{1... | collective-permute-start | bytes 663560 | tf_op jit(solution)/shard_map/ppermute | solution.py:20
  29.7 1.8 %collective-permute-start.8 = (bf16[2,144,384]{2,1,0:T(8,128)(2,1)S(1)}, bf16[2,144,384]{2,1,0:T(8,128)(2,1)S(1)}, u32[]{:S(2)}, u32[]{:S(2)}) collective-permute-start(bf16[2,144,384]{2,1,0:T(8,128)(2,1)S(1)} %get-tuple-element.71), channel_id=1, source_target_pairs={{0,4},{4,0},{8,12},{12,8},{1,5},{5,1},{9,13},{13,9},{2,6},{6,2},{1... | collective-permute-start | bytes 663560 | tf_op jit(solution)/shard_map/ppermute | solution.py:20
  30.2 1.6 %collective-permute-start.9 = (bf16[2,144,384]{2,1,0:T(8,128)(2,1)S(1)}, bf16[2,144,384]{2,1,0:T(8,128)(2,1)S(1)}, u32[]{:S(2)}, u32[]{:S(2)}) collective-permute-start(bf16[2,144,384]{2,1,0:T(8,128)(2,1)S(1)} %get-tuple-element.72), channel_id=1, source_target_pairs={{0,4},{4,0},{8,12},{12,8},{1,5},{5,1},{9,13},{13,9},{2,6},{6,2},{1... | collective-permute-start | bytes 663560 | tf_op jit(solution)/shard_map/ppermute | solution.py:20
  32.0 8.2 %collective-permute-start.10 = (bf16[224,384]{1,0:T(8,128)(2,1)S(1)}, bf16[224,384]{1,0:T(8,128)(2,1)S(1)}, u32[]{:S(2)}, u32[]{:S(2)}) collective-permute-start(bf16[224,384]{1,0:T(8,128)(2,1)S(1)} %get-tuple-element.74), channel_id=1, source_target_pairs={{0,24},{4,28},{8,16},{12,20},{16,8},{20,12},{24,0},{28,4},{1,25},{... | collective-permute-start | bytes 516104 | tf_op jit(solution)/shard_map/ppermute | solution.py:280
  34.5 8.6 %collective-permute-start.11 = (bf16[224,384]{1,0:T(8,128)(2,1)S(1)}, bf16[224,384]{1,0:T(8,128)(2,1)S(1)}, u32[]{:S(2)}, u32[]{:S(2)}) collective-permute-start(bf16[224,384]{1,0:T(8,128)(2,1)S(1)} %get-tuple-element.75), channel_id=1, source_target_pairs={{0,8},{4,12},{8,0},{12,4},{16,24},{20,28},{24,16},{28,20},{1,9},{5... | collective-permute-start | bytes 516104 | tf_op jit(solution)/shard_map/ppermute | solution.py:280
  35.0 8.2 %collective-permute-start.12 = (bf16[224,384]{1,0:T(8,128)(2,1)S(1)}, bf16[224,384]{1,0:T(8,128)(2,1)S(1)}, u32[]{:S(2)}, u32[]{:S(2)}) collective-permute-start(bf16[224,384]{1,0:T(8,128)(2,1)S(1)} %get-tuple-element.76), channel_id=1, source_target_pairs={{0,16},{4,20},{8,24},{12,28},{16,0},{20,4},{24,8},{28,12},{1,17},{... | collective-permute-start | bytes 516104 | tf_op jit(solution)/shard_map/ppermute | solution.py:280
  35.6 15.6 %collective-permute-start.15 = (bf16[2,576,128]{2,1,0:T(8,128)(2,1)S(1)}, bf16[2,576,128]{2,1,0:T(8,128)(2,1)S(1)}, u32[]{:S(2)}, u32[]{:S(2)}) collective-permute-start(bf16[2,576,128]{2,1,0:T(8,128)(2,1)S(1)} %shard_map.103), channel_id=1, source_target_pairs={{0,2},{1,3},{2,0},{3,1},{4,6},{5,7},{6,4},{7,5},{8,10},{9,11},{10,... | collective-permute-start | bytes 884744 | tf_op jit(solution)/shard_map/ppermute | solution.py:20
  37.4 13.8 %collective-permute-start.16 = (bf16[2,576,128]{2,1,0:T(8,128)(2,1)S(1)}, bf16[2,576,128]{2,1,0:T(8,128)(2,1)S(1)}, u32[]{:S(2)}, u32[]{:S(2)}) collective-permute-start(bf16[2,576,128]{2,1,0:T(8,128)(2,1)S(1)} %get-tuple-element.85), channel_id=1, source_target_pairs={{0,1},{1,0},{2,3},{3,2},{4,5},{5,4},{6,7},{7,6},{8,9},{9,8},{10,11... | collective-permute-start | bytes 884744 | tf_op jit(solution)/shard_map/ppermute | solution.py:20
  43.3 6.3 %collective-permute-start.13 = (bf16[224,384]{1,0:T(8,128)(2,1)S(1)}, bf16[224,384]{1,0:T(8,128)(2,1)S(1)}, u32[]{:S(2)}, u32[]{:S(2)}) collective-permute-start(bf16[224,384]{1,0:T(8,128)(2,1)S(1)} %shard_map.101.mine), channel_id=1, source_target_pairs={{0,16},{16,0},{1,17},{17,1},{2,18},{18,2},{3,19},{19,3},{4,20},{20... | collective-permute-start | bytes 516104 | tf_op jit(solution)/shard_map/ppermute | solution.py:20
